TPU v7x, 512 devices: a whole 4x8x8 slice. The times are simulated.
512 devices in a mesh: dp: 8 (over z), expert: 64 (over x, y, core).
Axes of the slice: x: 4, y: 8, z: 8, core: 2. Of those that a mesh axis runs over, the one named last changes fastest.
Arguments:
- cotangent: bfloat16 [65536, 4096], P(('dp', 'expert')), may hold values from -6 to 6
- route_weight: float32 [65536, 8], P(('dp', 'expert')), may hold values from 0.05 to 1
- expert_ids: int32 [65536, 8], P(('dp', 'expert')), may hold values from 0 to 63, as said below
- slot_ids: int32 [65536, 8], P(('dp', 'expert')), may hold values from 0 to 19, as said below
- hidden_saved: bfloat16 [8, 64, 1024, 768], P('dp', 'expert'), may hold values from -6 to 6
- down_weight: bfloat16 [64, 768, 4096], P('expert', None, 'dp'), may hold values from -0.09375 to 0.09375
- adapter_a: bfloat16 [64, 16, 768], P('expert'), may hold values from -0.21875 to 0.21875
- adapter_out_maps: bfloat16 [64, 16, 4096], P('expert'), may hold values from -1.5 to 1.5
- rollout_owner: int32 [64], replicated, may hold values from 0 to 63, each once
Outputs:
- grad_hidden: bfloat16 [8, 64, 1024, 768], P('dp', 'expert')
- grad_a_rollout: bfloat16 [64, 16, 768], P('expert', None, 'dp')
- grad_b_rollout: bfloat16 [64, 16, 4096], P('expert', None, 'dp')
Inputs may be any that keep to these rules, and one draw needn't show every extreme that they name: `expert_ids`: the 8 experts of a row are distinct. In each aligned block of 128 rows every expert is named by at most 20 rows, and some expert by exactly that many. `slot_ids`: within an aligned block of 128 rows, the rows that name one expert carry distinct slots, each below the number of such rows; a slot of 16 or more marks a pair beyond capacity.
All inputs are finite; a program needn't handle non-finite values.
Results may differ from a plain program's by a relative error of at most 0.0057.
Values may be sent and summed in bfloat16 or wider, within the bound.
No kernel may reach another device: no remote copies, remote signals or barrier semaphores. Data moves between devices by JAX's collectives and lax.ppermute only.
A program may use at most 128 MiB of HBM per device.

v0:
```python
import jax
import jax.numpy as jnp
from jax import lax
from jax.sharding import PartitionSpec as P

ADAPTER_SCALE = 2.0


def per_device(
    cotangent,
    route_weight,
    expert_ids,
    slot_ids,
    hidden_saved,
    down_weight,
    adapter_a,
    adapter_out_maps,
    rollout_owner,
):
    ranks = lax.axis_size("expert")
    groups = lax.axis_size("dp")
    tok_rows, width = cotangent.shape
    top = expert_ids.shape[1]
    local = adapter_a.shape[0]
    rank_dim = adapter_a.shape[1]
    hidden_width = adapter_a.shape[2]
    capacity = hidden_saved.shape[2] // ranks
    slots_per = ranks * capacity
    keep = slot_ids < capacity
    flat_pos = jnp.where(
        keep,
        expert_ids % local * slots_per + expert_ids // local * capacity + slot_ids,
        local * slots_per,
    ).reshape(-1)
    anchor = (
        jnp.zeros((local * slots_per,), jnp.int32)
        .at[flat_pos]
        .set(jnp.arange(tok_rows * top, dtype=jnp.int32), mode="drop")
    )
    filled = jnp.zeros((local * slots_per,), jnp.float32).at[flat_pos].set(1.0, mode="drop")
    weights = route_weight.reshape(-1)
    routed_tokens = (
        weights[anchor][:, None] * cotangent[anchor // top].astype(jnp.float32) * filled[:, None]
    ).astype(jnp.bfloat16)
    routed_tokens = routed_tokens.reshape(local, ranks, capacity, width)
    arrived = lax.all_to_all(routed_tokens, "expert", split_axis=1, concat_axis=1, tiled=True)
    slot_rows = arrived.reshape(local, slots_per, width)
    hidden = hidden_saved[0]
    rank_feature_block = (
        ADAPTER_SCALE
        * jnp.einsum(
            "esd,erd->esr", slot_rows, adapter_out_maps, preferred_element_type=jnp.float32
        )
    ).astype(jnp.bfloat16)
    hidden_projection = jnp.einsum(
        "esf,erf->esr", hidden, adapter_a, preferred_element_type=jnp.float32
    ).astype(jnp.bfloat16)
    back = jnp.einsum(
        "esd,efd->esf",
        slot_rows,
        lax.all_gather(down_weight, "dp", axis=2, tiled=True),
        preferred_element_type=jnp.float32,
    )
    back = back + jnp.einsum(
        "esr,erf->esf", rank_feature_block, adapter_a, preferred_element_type=jnp.float32
    )
    grad_hidden = back.astype(jnp.bfloat16)[None]
    out_map_gradient = ADAPTER_SCALE * jnp.einsum(
        "esr,esd->erd", hidden_projection, slot_rows, preferred_element_type=jnp.float32
    )
    grad_a = jnp.einsum(
        "esr,esf->erf", rank_feature_block, hidden, preferred_element_type=jnp.float32
    )
    piece_a = hidden_width // groups
    piece_b = width // groups
    total_a, total_b = lax.psum((grad_a, out_map_gradient), "dp")
    member = lax.axis_index("dp")
    share_a = lax.dynamic_slice_in_dim(total_a, member * piece_a, piece_a, 2)
    share_b = lax.dynamic_slice_in_dim(total_b, member * piece_b, piece_b, 2)
    share_a = share_a.astype(jnp.bfloat16)
    share_b = share_b.astype(jnp.bfloat16)
    mine = lax.axis_index("expert") * local + jnp.arange(local, dtype=jnp.int32)
    place = rollout_owner[mine]
    target_dev = place // local
    seat = place % local
    bucket_a = (
        jnp.zeros((ranks, local, rank_dim, piece_a), jnp.bfloat16).at[target_dev, seat].set(share_a)
    )
    bucket_b = (
        jnp.zeros((ranks, local, rank_dim, piece_b), jnp.bfloat16).at[target_dev, seat].set(share_b)
    )
    got_a, got_b = (
        lax.all_to_all(bucket_a, "expert", split_axis=0, concat_axis=0, tiled=True),
        lax.all_to_all(bucket_b, "expert", split_axis=0, concat_axis=0, tiled=True),
    )
    relay_a = jnp.sum(got_a.astype(jnp.float32), axis=0).astype(jnp.bfloat16)
    relay_b = jnp.sum(got_b.astype(jnp.float32), axis=0).astype(jnp.bfloat16)
    return (grad_hidden, relay_a, relay_b)


def solution(mesh):
    return jax.shard_map(
        per_device,
        mesh=mesh,
        in_specs=(
            P(("dp", "expert"), None),
            P(("dp", "expert"), None),
            P(("dp", "expert"), None),
            P(("dp", "expert"), None),
            P("dp", "expert", None, None),
            P("expert", None, "dp"),
            P("expert", None, None),
            P("expert", None, None),
            P(),
        ),
        out_specs=(P("dp", "expert", None, None), P("expert", None, "dp"), P("expert", None, "dp")),
        check_vma=False,
    )
```

profile of v0, /device:TPU:1, one launch (start us, length us, event | category | flops | bytes accessed | tf_op | source)
XLA Modules:
  0.0 352.1 jit_solution(691759661732857302)
XLA Ops:
  7.2 0.9 add_select_fusion.2
  8.0 0.1 copy.15
  8.2 0.1 reshape.237
  8.3 4.3 %scatter_custom_fusion = s32[1024]{0:T(1024)S(1)} fusion(s32[1024]{0:T(1024)S(1)} %bitcast.57, s32[1024]{0:T(1024)S(1)} %iota.3, s32[]{:T(128)} %constant.125.clone.1), kind=kCustom, calls=%fused_computation.47 | custom fusion | bytes 4100 | tf_op jit(solution)/shard_map/scatter | solution.py:38
  12.6 4.3 %scatter_custom_fusion.1 = f32[1024]{0:T(1024)S(1)} fusion(s32[1024]{0:T(1024)S(1)} %bitcast.58, f32[1024]{0:T(1024)S(1)} %broadcast.176, f32[]{:T(128)} %constant.133.clone.1), kind=kCustom, calls=%fused_computation.45 | custom fusion | bytes 4100 | tf_op jit(solution)/shard_map/scatter | solution.py:40
  17.0 0.8 copy.14
  17.9 4.5 %gather_fusion = f32[1024]{0:T(1024)S(1)} fusion(f32[1024]{0:T(1024)S(1)} %reshape.236, s32[1024]{0:T(1024)S(1)} %get-tuple-element.40), kind=kCustom, calls=%fused_computation | custom fusion | bytes 12288 | tf_op jit(solution)/shard_map/gather | solution.py:43
  22.5 7.7 %gather_fusion.1 = bf16[1024,4096]{1,0:T(8,128)(2,1)} fusion(bf16[128,4096]{1,0:T(8,128)(2,1)S(1)} %copy-done.1, s32[1024]{0:T(1024)S(1)} %get-tuple-element.41), kind=kCustom, calls=%fused_computation.1 | custom fusion | bytes 16781312 | tf_op jit(solution)/shard_map/gather | solution.py:43
  30.2 11.1 %fusion.1 = bf16[1,64,16,4096]{3,2,0,1:T(8,128)(2,1)} fusion(bf16[1,64,16,4096]{3,2,0,1:T(8,128)(2,1)} %bitcast.54, f32[64,16]{1,0:T(8,128)S(1)} %mul.69, f32[64,16]{1,0:T(8,128)S(1)} %mul.66), kind=kLoop, calls=%fused_computation.6 | loop fusion | flops 16777216 | bytes 16785408 | tf_op jit(solution)/shard_map/convert_element_type | solution.py:44
  41.3 12.1 %all-to-all-start = ((bf16[1,64,16,4096]{3,2,0,1:T(8,128)(2,1)}), bf16[1,64,16,4096]{3,2,0,1:T(8,128)(2,1)}, u32[]{:S(2)}, u32[]{:S(2)}) async-start(bf16[1,64,16,4096]{3,2,0,1:T(8,128)(2,1)} %fusion.1), calls=%async_computation | async-start | bytes 16777216 | tf_op jit(solution)/shard_map/all_to_all | solution.py:46
  53.5 0.2 all-gather.2.cloned.1.call-start
  53.7 0.5 all-gather.2.cloned.1.call-update
  54.2 0.6 dynamic-slice.14
  56.8 0.7 and_reduce_fusion
  57.5 181.8 %all-to-all-done = bf16[1,64,16,4096]{3,2,0,1:T(8,128)(2,1)} async-done(((bf16[1,64,16,4096]{3,2,0,1:T(8,128)(2,1)}), bf16[1,64,16,4096]{3,2,0,1:T(8,128)(2,1)}, u32[]{:S(2)}, u32[]{:S(2)}) %all-to-all-start) | async-done | bytes 8388640 | tf_op jit(solution)/shard_map/all_to_all | solution.py:46
  239.3 5.6 %fusion.16 = bf16[1024,16]{0,1:T(8,128)(2,1)S(1)} fusion(bf16[1024,4096]{1,0:T(8,128)(2,1)} %bitcast.3, bf16[1,16,4096]{2,1,0:T(8,128)(2,1)S(1)} %copy-done.3), kind=kOutput, calls=%fused_computation.20 | convolution fusion | flops 134250496 | bytes 8552448 | tf_op jit(solution)/shard_map/esd,erd->esr/dot_general | solution.py:51
  244.9 0.3 fusion.10
  245.3 5.0 %fusion.4 = f32[1,16,4096]{2,1,0:T(8,128)S(1)} fusion(bf16[1024,4096]{1,0:T(8,128)(2,1)} %bitcast.3, bf16[1,1,1024,768]{3,2,1,0:T(8,128)(2,1)S(1)} %copy-done, bf16[1,16,768]{2,1,0:T(8,128)(2,1)S(1)} %copy-done.4), kind=kOutput, calls=%fused_computation.10 | convolution fusion | flops 159465472 | bytes 10248192 | tf_op jit(solution)/shard_map/esr,esd->erd/dot_general | solution.py:68
  250.3 32.6 %all-reduce.2 = (bf16[1,16,768]{2,1,0:T(8,128)(2,1)S(1)}, bf16[1,16,4096]{2,1,0:T(8,128)(2,1)S(1)}) all-reduce(f32[1,16,768]{2,1,0:T(8,128)S(1)} %fusion.10, f32[1,16,4096]{2,1,0:T(8,128)S(1)} %fusion.4), channel_id=1, replica_groups=mesh['dp'=8,'expert'=64] {'dp'}, use_global_device_ids=true, to_apply=%region_3.4 | all-reduce | flops 77824 | bytes 466944 | tf_op jit(solution)/shard_map/psum | solution.py:76
  282.9 0.7 broadcast_in_dim.39
  283.6 1.3 fusion.30
  285.0 12.9 %all-to-all-start.1 = ((bf16[64,1,16,96]{3,2,1,0:T(8,128)(2,1)}), bf16[64,1,16,96]{3,2,1,0:T(8,128)(2,1)S(1)}, u32[]{:S(2)}, u32[]{:S(2)}) async-start(bf16[64,1,16,96]{3,2,1,0:T(8,128)(2,1)} %fusion.30), calls=%async_computation.1 | async-start | bytes 524288 | tf_op jit(solution)/shard_map/all_to_all | solution.py:93
  297.9 0.1 broadcast_in_dim.41
  298.0 0.7 fusion.25
  298.7 1.0 copy-done.2
  299.7 10.2 %all-to-all-done.1 = bf16[64,1,16,96]{3,2,1,0:T(8,128)(2,1)S(1)} async-done(((bf16[64,1,16,96]{3,2,1,0:T(8,128)(2,1)}), bf16[64,1,16,96]{3,2,1,0:T(8,128)(2,1)S(1)}, u32[]{:S(2)}, u32[]{:S(2)}) %all-to-all-start.1) | async-done | bytes 196640 | tf_op jit(solution)/shard_map/all_to_all | solution.py:93
  309.9 6.0 %all-to-all-start.2 = ((bf16[64,1,16,512]{3,2,1,0:T(8,128)(2,1)}), bf16[64,1,16,512]{3,2,1,0:T(8,128)(2,1)S(1)}, u32[]{:S(2)}, u32[]{:S(2)}) async-start(bf16[64,1,16,512]{3,2,1,0:T(8,128)(2,1)} %copy-done.2), calls=%async_computation.2 | async-start | bytes 2097152 | tf_op jit(solution)/shard_map/all_to_all | solution.py:94
  315.9 11.0 %fusion.2 = f32[1024,768]{1,0:T(8,128)S(1)} fusion(bf16[1024,4096]{1,0:T(8,128)(2,1)} %bitcast.3, bf16[1,768,4096]{2,1,0:T(8,128)(2,1)} %all-gather.2.cloned.1.call-done), kind=kOutput, calls=%fused_computation.7 | convolution fusion | flops 6442450944 | bytes 17825792 | tf_op jit(solution)/shard_map/esd,efd->esf/dot_general | solution.py:58
  326.9 1.8 fusion.9
  328.7 0.7 reduce_sum.28
  329.4 15.1 %all-to-all-done.2 = bf16[64,1,16,512]{3,2,1,0:T(8,128)(2,1)S(1)} async-done(((bf16[64,1,16,512]{3,2,1,0:T(8,128)(2,1)}), bf16[64,1,16,512]{3,2,1,0:T(8,128)(2,1)S(1)}, u32[]{:S(2)}, u32[]{:S(2)}) %all-to-all-start.2) | async-done | bytes 1048608 | tf_op jit(solution)/shard_map/all_to_all | solution.py:94
  344.5 0.8 reduce_sum.30
  (21 shorter events, 0.3 us)
Async XLA Ops:
  7.2 237.7 %copy-start = (bf16[1,1,1024,768]{3,2,1,0:T(8,128)(2,1)S(1)}, bf16[1,1,1024,768]{3,2,1,0:T(8,128)(2,1)}, u32[]{:S(2)}) copy-start(bf16[1,1,1024,768]{3,2,1,0:T(8,128)(2,1)} %param.17) | copy-start | bytes 4718596
  7.2 15.3 %copy-start.1 = (bf16[128,4096]{1,0:T(8,128)(2,1)S(1)}, bf16[128,4096]{1,0:T(8,128)(2,1)}, u32[]{:S(2)}) copy-start(bf16[128,4096]{1,0:T(8,128)(2,1)} %param.13) | copy-start | bytes 3145732
  41.3 12.9 %copy-start.6 = (s32[64]{0:T(128)S(1)}, s32[64]{0:T(128)}, u32[]{:S(2)}) copy-start(s32[64]{0:T(128)} %param.21) | copy-start | bytes 772
  41.3 15.4 %copy-start.5 = (s32[4]{0:T(128)S(1)}, s32[4]{0:T(128)}, u32[]{:S(2)}) copy-start(s32[4]{0:T(128)} %constant.140.clone.1) | copy-start | bytes 52
  41.3 198.0 %copy-start.3 = (bf16[1,16,4096]{2,1,0:T(8,128)(2,1)S(1)}, bf16[1,16,4096]{2,1,0:T(8,128)(2,1)}, u32[]{:S(2)}) copy-start(bf16[1,16,4096]{2,1,0:T(8,128)(2,1)} %param.20) | copy-start | bytes 393220
  41.3 197.9 %all-to-all-start = ((bf16[1,64,16,4096]{3,2,0,1:T(8,128)(2,1)}), bf16[1,64,16,4096]{3,2,0,1:T(8,128)(2,1)}, u32[]{:S(2)}, u32[]{:S(2)}) async-start(bf16[1,64,16,4096]{3,2,0,1:T(8,128)(2,1)} %fusion.1), calls=%async_computation | async-start | bytes 16777216 | tf_op jit(solution)/shard_map/all_to_all | solution.py:46
  53.5 191.8 %copy-start.4 = (bf16[1,16,768]{2,1,0:T(8,128)(2,1)S(1)}, bf16[1,16,768]{2,1,0:T(8,128)(2,1)}, u32[]{:S(2)}) copy-start(bf16[1,16,768]{2,1,0:T(8,128)(2,1)} %param.19) | copy-start | bytes 73732
  53.5 262.5 %all-gather.2.cloned.1.call-start = ((), (), s32[]{:S(2)}) async-start(), calls=%async_computation.3 | async-start | bytes 7077888 | tf_op jit(solution)/shard_map/all_gather | solution.py:61
  285.0 24.9 %all-to-all-start.1 = ((bf16[64,1,16,96]{3,2,1,0:T(8,128)(2,1)}), bf16[64,1,16,96]{3,2,1,0:T(8,128)(2,1)S(1)}, u32[]{:S(2)}, u32[]{:S(2)}) async-start(bf16[64,1,16,96]{3,2,1,0:T(8,128)(2,1)} %fusion.30), calls=%async_computation.1 | async-start | bytes 524288 | tf_op jit(solution)/shard_map/all_to_all | solution.py:93
  298.7 1.1 copy-start.2
  309.9 34.6 %all-to-all-start.2 = ((bf16[64,1,16,512]{3,2,1,0:T(8,128)(2,1)}), bf16[64,1,16,512]{3,2,1,0:T(8,128)(2,1)S(1)}, u32[]{:S(2)}, u32[]{:S(2)}) async-start(bf16[64,1,16,512]{3,2,1,0:T(8,128)(2,1)} %copy-done.2), calls=%async_computation.2 | async-start | bytes 2097152 | tf_op jit(solution)/shard_map/all_to_all | solution.py:94
Sparse Core Ops, SparseCore 0:
  56.4 81.8 all-gather.1
where the time goes:
time: 353 us; the launch traced here: 352 us
  waiting for transfers between devices  208 us (59%)
  blocking collectives  32.6 us (9%)
  starting transfers between devices  31.3 us (9%)
  local copies, waits for them, and re-layouts  24.6 us (7%)
  matrix products  23.7 us (7%)
  between operations  16.2 us (5%)
  other arithmetic  16.1 us (5%)
    all_to_all x1, waiting for transfers between devices, per_device(): lax.all_to_all(routed_tokens, 'expert', split_axis=1, concat_axis=1, tile...  182 us
    psum x1, blocking collectives, per_device(): total_a, total_b = lax.psum((grad_a, out_map_gradient), 'dp')  32.6 us
    all_to_all x1, waiting for transfers between devices, per_device(): lax.all_to_all(bucket_b, 'expert', split_axis=0, concat_axis=0, tiled=True)  15.1 us
    all_to_all x1, starting transfers between devices, per_device(): lax.all_to_all(bucket_a, 'expert', split_axis=0, concat_axis=0, tiled=True)  12.9 us
    all_to_all x1, starting transfers between devices, per_device(): lax.all_to_all(routed_tokens, 'expert', split_axis=1, concat_axis=1, tile...  12.1 us
    convert_element_type x1, other arithmetic, per_device(): routed_tokens = (weights[anchor][:, None] * cotangent[anchor // top].asty...  11.1 us
    dot_general x1, matrix products, per_device(): jnp.einsum('esd,efd->esf', slot_rows, lax.all_gather(down_weight, 'dp', a...  11 us
    all_to_all x1, waiting for transfers between devices, per_device(): lax.all_to_all(bucket_a, 'expert', split_axis=0, concat_axis=0, tiled=True)  10.2 us
  transfers between devices with their start and end apart: 4, of which 3 were waited for; matrix products, arithmetic and copies ran while one was open for 8% of the time, Pallas kernels for 0%

commit v1 on v0

v1 whole, which is shorter than its diff:
```python
import functools

import jax
import jax.numpy as jnp
from jax import lax
from jax.experimental import pallas as pl
from jax.experimental.pallas import tpu as pltpu
from jax.sharding import Mesh, PartitionSpec as P

ADAPTER_SCALE = 2.0
GROUPS, NX, NY, NC = 8, 4, 8, 2
COLS = NX * NC
CAP = 16
META = 128
MIB = 1024 * 1024
VM = pl.BlockSpec(memory_space=pltpu.VMEM)
SM = pl.BlockSpec(memory_space=pltpu.SMEM)
NT = (((1,), (1,)), ((), ()))
TN = (((0,), (0,)), ((), ()))
NN = (((1,), (0,)), ((), ()))


def dot(a, b, dims):
    return lax.dot_general(a, b, dims, preferred_element_type=jnp.float32)


def params(mib):
    return pltpu.CompilerParams(vmem_limit_bytes=mib * MIB)


def pack_kernel(cot, weight, ids, slots, out):
    width = cot.shape[1]
    out[:, :width] = cot[...]
    w = weight[...]
    hi = w.astype(jnp.bfloat16)
    rest = w - hi.astype(jnp.float32)
    mid = rest.astype(jnp.bfloat16)
    low = (rest - mid.astype(jnp.float32)).astype(jnp.bfloat16)
    zero = jnp.zeros(low.shape, jnp.float32)
    rows = [
        ids[...].astype(jnp.float32),
        slots[...].astype(jnp.float32),
        hi.astype(jnp.float32),
        mid.astype(jnp.float32),
        low.astype(jnp.float32),
        zero,
    ]
    table = jnp.concatenate(rows, axis=0).astype(jnp.bfloat16)
    out[0:48, width:] = table
    out[48:, width:] = jnp.zeros((out.shape[0] - 48, META), jnp.bfloat16)


def pack(cot, weight, ids, slots):
    return pl.pallas_call(
        pack_kernel,
        out_shape=jax.ShapeDtypeStruct((cot.shape[0], cot.shape[1] + META), jnp.bfloat16),
        in_specs=[VM] * 4,
        out_specs=VM,
        compiler_params=params(12),
    )(cot, weight, ids, slots)


def build_kernel(halves, me, *refs):
    out = refs[-1]
    blocks = refs[:-1]
    count = 1 if halves else len(blocks)
    for b in range(count):
        first = blocks[b]
        width = first.shape[1] - META
        table = first[0:48, width:].astype(jnp.float32)
        expert = table[0:8].astype(jnp.int32)
        slot = table[8:16].astype(jnp.int32)
        weight = table[16:24] + table[24:32] + table[32:40]
        dest = (expert // (NY * NC)) * NC + expert % NC
        here = ((expert // NC) % NY == me[0]) & (slot < CAP)
        code = jnp.where(here, dest * CAP + slot, -1)
        tokens = code.shape[1]
        row = lax.broadcasted_iota(jnp.int32, (COLS * CAP, tokens), 0)
        pick = jnp.zeros((COLS * CAP, tokens), jnp.float32)
        scale = jnp.zeros((COLS * CAP, tokens), jnp.float32)
        for k in range(code.shape[0]):
            match = row == code[k : k + 1]
            pick = jnp.where(match, 1.0, pick)
            scale = jnp.where(match, weight[k : k + 1], scale)
        scale = jnp.sum(scale, axis=1, keepdims=True)
        pick = pick.astype(jnp.bfloat16)
        step = 1024
        for at in range(0, width, step):
            if halves:
                value = jnp.concatenate([blocks[0][:, at : at + step], blocks[1][:, at : at + step]], axis=0)
            else:
                value = first[:, at : at + step]
            rows = (scale * dot(pick, value, NN)).astype(jnp.bfloat16)
            out[:, b, :, at : at + step] = rows.reshape(COLS, CAP, step)


def build(me, blocks, halves=False):
    width = blocks[0].shape[1] - META
    count = 1 if halves else len(blocks)
    return pl.pallas_call(
        functools.partial(build_kernel, halves),
        out_shape=jax.ShapeDtypeStruct((COLS, count, CAP, width), jnp.bfloat16),
        in_specs=[SM] + [VM] * len(blocks),
        out_specs=VM,
        compiler_params=params(20),
    )(me, *blocks)


def places(me, offsets):
    found = []
    for x in range(NX):
        for c in range(NC):
            for offset in offsets:
                found.append(x * NY * NC + ((me + offset + NY) % NY) * NC + c)
    return found


def grads_kernel(offsets, first, last, *refs):
    if first:
        me, g, hidden, amap, bmap = refs[:5]
        old_a = old_b = None
        rest = refs[5:]
    else:
        me, g, hidden, amap, bmap, old_a, old_b = refs[:7]
        rest = refs[7:]
    hid = rest[-1]
    outs = rest[:-1]
    for i, src in enumerate(places(me[0], offsets)):
        hid[i * CAP : (i + 1) * CAP] = hidden[src]
    rows = hid.shape[0]
    width = g.shape[-1]
    tokens = g[...].reshape(rows, width)
    rb = (ADAPTER_SCALE * dot(tokens, bmap[...], NT)).astype(jnp.bfloat16)
    outs[0][...] = rb
    z = dot(hid[...], amap[...], NT).astype(jnp.bfloat16)
    grad_b = ADAPTER_SCALE * dot(z, tokens, TN)
    grad_a = dot(rb, hid[...], TN)
    if old_a is not None:
        grad_b = grad_b + old_b[...]
        grad_a = grad_a + old_a[...]
    if not last:
        outs[1][...] = grad_a
        outs[2][...] = grad_b
    else:
        sent = outs[1]
        wide_b = width // GROUPS
        wide_a = hid.shape[1] // GROUPS
        for z_to in range(GROUPS):
            sent[z_to, :, :wide_b] = grad_b[:, z_to * wide_b : (z_to + 1) * wide_b].astype(jnp.bfloat16)
            sent[z_to, :, wide_b : wide_b + wide_a] = grad_a[:, z_to * wide_a : (z_to + 1) * wide_a].astype(
                jnp.bfloat16
            )


def grads(me, g, hidden, amap, bmap, old, offsets, last):
    rows = g.shape[0] * g.shape[1] * g.shape[2]
    rank, width = bmap.shape
    hidden_width = amap.shape[1]
    shapes = [jax.ShapeDtypeStruct((rows, rank), jnp.bfloat16)]
    if last:
        piece = width // GROUPS + hidden_width // GROUPS
        shapes += [jax.ShapeDtypeStruct((GROUPS, rank, piece), jnp.bfloat16)]
    else:
        shapes += [
            jax.ShapeDtypeStruct((rank, hidden_width), jnp.float32),
            jax.ShapeDtypeStruct((rank, width), jnp.float32),
        ]
    args = [me, g, hidden, amap, bmap] + list(old)
    return pl.pallas_call(
        functools.partial(grads_kernel, offsets, not old, last),
        out_shape=shapes,
        in_specs=[SM] + [VM] * (len(args) - 1),
        out_specs=[VM] * len(shapes),
        scratch_shapes=[pltpu.VMEM((rows, hidden_width), jnp.bfloat16)],
        compiler_params=params(20),
    )(*args)


def back_kernel(chunks, me, weight, amap, *refs):
    out = refs[-1]
    for n, offsets in enumerate(chunks):
        g, rb = refs[2 * n], refs[2 * n + 1]
        rows = rb.shape[0]
        width = g.shape[-1]
        wide = weight.shape[-1]
        total = dot(rb[...], amap[...], NN)
        for z in range(GROUPS):
            total = total + dot(g[:, :, :, z * wide : (z + 1) * wide].reshape(rows, wide), weight[z], NT)
        total = total.astype(jnp.bfloat16)
        for i, src in enumerate(places(me[0], offsets)):
            out[src] = total[i * CAP : (i + 1) * CAP]


def back(me, weight, amap, pairs, chunks):
    flat = [ref for pair in pairs for ref in pair]
    return pl.pallas_call(
        functools.partial(back_kernel, chunks),
        out_shape=jax.ShapeDtypeStruct((NX * NY * NC, CAP, amap.shape[1]), jnp.bfloat16),
        in_specs=[SM] + [VM] * (2 + len(flat)),
        out_specs=VM,
        compiler_params=params(32),
    )(me, weight, amap, *flat)


def spread_kernel(got, out):
    total = jnp.sum(got[...].astype(jnp.float32), axis=0).astype(jnp.bfloat16)
    for d in range(COLS):
        out[d] = total


def spread(got):
    return pl.pallas_call(
        spread_kernel,
        out_shape=jax.ShapeDtypeStruct((COLS,) + got.shape[1:], got.dtype),
        in_specs=[VM],
        out_specs=VM,
    )(got)


def turn_kernel(where, owner, got, out):
    x, y, c = where[0], where[1], where[2]
    for y_to in range(NY):
        target = x * NY * NC + y_to * NC + c
        for s in range(COLS):
            expert = (s // NC) * NY * NC + y * NC + s % NC

            @pl.when(owner[expert] == target)
            def _():
                out[y_to] = got[s]


def turn(where, owner, got):
    return pl.pallas_call(
        turn_kernel,
        out_shape=jax.ShapeDtypeStruct((NY,) + got.shape[1:], got.dtype),
        in_specs=[SM, SM, VM],
        out_specs=VM,
    )(where, owner, got)


def take_kernel(wide_b, where, owner, got, out_a, out_b):
    mine = (where[0] * NY + where[1]) * NC + where[2]
    for expert in range(NX * NY * NC):

        @pl.when(owner[expert] == mine)
        def _():
            row = got[(expert // NC) % NY]
            out_b[...] = row[:, :wide_b]
            out_a[...] = row[:, wide_b:]


def take(where, owner, got, wide_a, wide_b):
    rank = got.shape[1]
    return pl.pallas_call(
        functools.partial(take_kernel, wide_b),
        out_shape=[
            jax.ShapeDtypeStruct((rank, wide_a), got.dtype),
            jax.ShapeDtypeStruct((rank, wide_b), got.dtype),
        ],
        in_specs=[SM, SM, VM],
        out_specs=[VM, VM],
    )(where, owner, got)


def per_device(
    cotangent,
    route_weight,
    expert_ids,
    slot_ids,
    hidden_saved,
    down_weight,
    adapter_a,
    adapter_out_maps,
    rollout_owner,
):
    width = cotangent.shape[1]
    hidden_width = adapter_a.shape[2]
    x = lax.axis_index("x").astype(jnp.int32)
    y = lax.axis_index("y").astype(jnp.int32)
    c = lax.axis_index("core").astype(jnp.int32)
    me = y.reshape(1)
    where = jnp.stack([x, y, c])
    up = [(i, (i + 1) % NY) for i in range(NY)]
    down = [(i, (i - 1) % NY) for i in range(NY)]
    row = ("x", "core")

    weight = lax.all_gather(down_weight[0], "dp")
    own = pack(cotangent, route_weight.T, expert_ids.T, slot_ids.T)
    hidden = hidden_saved.reshape(NX * NY * NC, CAP, hidden_width)
    amap = adapter_a[0]
    bmap = adapter_out_maps[0]

    def send(rows):
        return lax.all_to_all(rows, row, 0, 0, tiled=True)

    chunks = [(0,)] + [(-d, d) for d in range(1, NY // 2)] + [(NY // 2,)]
    from_down, from_up = own, own
    arrived = [send(build(me, [own]))]
    for d in range(1, NY // 2):
        from_down = lax.ppermute(from_down, "y", up)
        from_up = lax.ppermute(from_up, "y", down)
        arrived.append(send(build(me, [from_down, from_up])))
    half = own.shape[0] // 2
    far_low = lax.ppermute(from_down[:half], "y", up)
    far_high = lax.ppermute(from_up[half:], "y", down)
    arrived.append(send(build(me, [far_low, far_high], halves=True)))

    old = ()
    pairs = []
    for n, offsets in enumerate(chunks):
        last = n == len(chunks) - 1
        rb, *old = grads(me, arrived[n], hidden, amap, bmap, old, offsets, last)
        pairs.append((arrived[n], rb))
    sent = old[0]
    got = lax.all_to_all(sent, "dp", 0, 0, tiled=True)
    row_items = lax.all_to_all(spread(got), row, 0, 0, tiled=True)
    column_items = lax.all_to_all(turn(where, rollout_owner, row_items), "y", 0, 0, tiled=True)
    out_a, out_b = take(where, rollout_owner, column_items, hidden_width // GROUPS, width // GROUPS)
    grad_hidden = back(me, weight, amap, pairs, chunks)
    return (
        grad_hidden.reshape(1, 1, NX * NY * NC * CAP, hidden_width),
        out_a[None],
        out_b[None],
    )


def solution(mesh):
    parts = Mesh(mesh.devices.reshape(GROUPS, NX, NY, NC), ("dp", "x", "y", "core"))
    every = ("dp", "x", "y", "core")
    expert = ("x", "y", "core")
    return jax.shard_map(
        per_device,
        mesh=parts,
        in_specs=(
            P(every, None),
            P(every, None),
            P(every, None),
            P(every, None),
            P("dp", expert, None, None),
            P(expert, None, "dp"),
            P(expert, None, None),
            P(expert, None, None),
            P(),
        ),
        out_specs=(P("dp", expert, None, None), P(expert, None, "dp"), P(expert, None, "dp")),
        check_vma=False,
    )
```

time: 353 us -> 255 us (0.72)
  waiting for transfers between devices: 208 us -> 91.6 us
  Pallas kernels: 0 us -> 34.3 us
  starting transfers between devices: 31.3 us -> 64.4 us
  matrix products: 23.7 us -> 0 us
  other arithmetic: 16.1 us -> 0.65 us
  local copies, waits for them, and re-layouts: 24.6 us -> 17.8 us
    all_to_all x3 -> x6, waiting for transfers between devices: 207 us -> 20.6 us  [the longest x5 15.6 us: send(): return lax.all_to_all(rows, row, 0, 0, tiled=True)]
    ppermute x0 -> x8, waiting for transfers between devices: none -> 70.4 us  [the longest x3 50 us: per_device(): from_down = lax.ppermute(from_down, 'y', up)]
    pallas_call x0 -> x15, Pallas kernels: none -> 34.3 us  [the longest x1 12.5 us: back(): pl.pallas_call(functools.partial(back_kernel, chunks), out_shape=jax.Shap...]
    psum x1 -> x0, blocking collectives: 32.6 us -> none  [per_device(): total_a, total_b = lax.psum((grad_a, out_map_gradient), 'dp')]
    all_to_all x0 -> x2, blocking collectives: none -> 30.9 us  [the longest x1 18.1 us: per_device(): got = lax.all_to_all(sent, 'dp', 0, 0, tiled=True)]
    ppermute x0 -> x8, starting transfers between devices: none -> 27.8 us  [the longest x3 11.8 us: per_device(): from_down = lax.ppermute(from_down, 'y', up)]
    dot_general x5 -> x0, matrix products: 23.7 us -> none  [the longest x1 11 us: per_device(): jnp.einsum('esd,efd->esf', slot_rows, lax.all_gather(down_weight, 'dp', a...]
    unnamed x15 -> x42, local copies, waits for them, and re-layouts: 1.87 us -> 17.8 us
  transfers between devices with their start and end apart: 4 -> 15, of which waited for: 3 -> 12; matrix products, arithmetic and copies ran while one was open for 8% -> 0% of each run, Pallas kernels for 0% -> 9%
where the time goes in v1:
time: 255 us; the launch traced here: 254 us
  waiting for transfers between devices  91.6 us (36%)
  starting transfers between devices  64.4 us (25%)
  Pallas kernels  34.3 us (13%)
  blocking collectives  30.9 us (12%)
  local copies, waits for them, and re-layouts  17.8 us (7%)
  between operations  14.2 us (6%)
    ppermute x3, waiting for transfers between devices, per_device(): from_down = lax.ppermute(from_down, 'y', up)  50 us
    all_to_all x5, starting transfers between devices, send(): return lax.all_to_all(rows, row, 0, 0, tiled=True)  30.7 us
    all_to_all x1, blocking collectives, per_device(): got = lax.all_to_all(sent, 'dp', 0, 0, tiled=True)  18.1 us
    unnamed x42, local copies, waits for them, and re-layouts  17.8 us
    all_to_all x5, waiting for transfers between devices, send(): return lax.all_to_all(rows, row, 0, 0, tiled=True)  15.6 us
    all_to_all x1, blocking collectives, per_device(): lax.all_to_all(turn(where, rollout_owner, row_items), 'y', 0, 0, tiled=True)  12.8 us
    pallas_call x1, Pallas kernels, back(): pl.pallas_call(functools.partial(back_kernel, chunks), out_shape=jax.Shap...  12.5 us
    ppermute x3, starting transfers between devices, per_device(): from_down = lax.ppermute(from_down, 'y', up)  11.8 us
  transfers between devices with their start and end apart: 15, of which 12 were waited for; matrix products, arithmetic and copies ran while one was open for 0% of the time, Pallas kernels for 9%

profile of v1, /device:TPU:1, one launch (start us, length us, event | category | flops | bytes accessed | tf_op | source)
XLA Modules:
  0.0 254.0 jit_solution(14638479756624259933)
XLA Ops:
  11.3 4.0 %collective-permute-start = (bf16[128,4224]{1,0:T(8,128)(2,1)S(1)}, bf16[128,4224]{1,0:T(8,128)(2,1)S(1)}, u32[]{:S(2)}, u32[]{:S(2)}) collective-permute-start(bf16[128,4224]{1,0:T(8,128)(2,1)S(1)} %shard_map.112.refs_0_), channel_id=1, source_target_pairs={{0,2},{2,4},{4,6},{6,8},{8,10},{10,12},{12,14},{14,0},{1,3},{3,5},... | collective-permute-start | bytes 3244040 | tf_op jit(solution)/shard_map/ppermute | solution.py:300
  15.3 3.8 %collective-permute-start.1 = (bf16[128,4224]{1,0:T(8,128)(2,1)S(1)}, bf16[128,4224]{1,0:T(8,128)(2,1)}, u32[]{:S(2)}, u32[]{:S(2)}) collective-permute-start(bf16[128,4224]{1,0:T(8,128)(2,1)S(1)} %shard_map.112.refs_0_), channel_id=1, source_target_pairs={{0,14},{2,0},{4,2},{6,4},{8,6},{10,8},{12,10},{14,12},{1,15},{3,1}... | collective-permute-start | bytes 3244040 | tf_op jit(solution)/shard_map/ppermute | solution.py:301
  20.6 9.5 %all-to-all-start = ((bf16[8,1,16,4096]{3,2,1,0:T(8,128)(2,1)}), bf16[8,1,16,4096]{3,2,1,0:T(8,128)(2,1)S(1)}, u32[]{:S(2)}, u32[]{:S(2)}) async-start(bf16[8,1,16,4096]{3,2,1,0:T(8,128)(2,1)} %shard_map.113), calls=%async_computation | async-start | bytes 2097152 | tf_op jit(solution)/shard_map/all_to_all | solution.py:294
  30.1 5.5 %collective-permute-done.refs_0_ = bf16[128,4224]{1,0:T(8,128)(2,1)S(1)} collective-permute-done((bf16[128,4224]{1,0:T(8,128)(2,1)S(1)}, bf16[128,4224]{1,0:T(8,128)(2,1)S(1)}, u32[]{:S(2)}, u32[]{:S(2)}) %collective-permute-start) | collective-permute-done | bytes 1081376 | tf_op jit(solution)/shard_map/ppermute | solution.py:300
  35.7 2.2 collective-permute-done.1.refs_1_
  41.4 3.9 %all-to-all-done.refs_1_.refs_0_ = bf16[8,1,16,4096]{3,2,1,0:T(8,128)(2,1)S(1)} async-done(((bf16[8,1,16,4096]{3,2,1,0:T(8,128)(2,1)}), bf16[8,1,16,4096]{3,2,1,0:T(8,128)(2,1)S(1)}, u32[]{:S(2)}, u32[]{:S(2)}) %all-to-all-start) | async-done | bytes 1048608 | tf_op jit(solution)/shard_map/all_to_all | solution.py:294
  46.3 6.1 %all-to-all-start.1 = ((bf16[8,2,16,4096]{3,2,1,0:T(8,128)(2,1)}), bf16[8,2,16,4096]{3,2,1,0:T(8,128)(2,1)S(1)}, u32[]{:S(2)}, u32[]{:S(2)}) async-start(bf16[8,2,16,4096]{3,2,1,0:T(8,128)(2,1)} %copy-done.7), calls=%async_computation.1 | async-start | bytes 4194304 | tf_op jit(solution)/shard_map/all_to_all | solution.py:294
  52.4 3.2 %collective-permute-start.2 = (bf16[128,4224]{1,0:T(8,128)(2,1)S(1)}, bf16[128,4224]{1,0:T(8,128)(2,1)S(1)}, u32[]{:S(2)}, u32[]{:S(2)}) collective-permute-start(bf16[128,4224]{1,0:T(8,128)(2,1)S(1)} %collective-permute-done.refs_0_), channel_id=1, source_target_pairs={{0,2},{2,4},{4,6},{6,8},{8,10},{10,12},{12,14},{14,0},{1,3},{3,5},... | collective-permute-start | bytes 3244040 | tf_op jit(solution)/shard_map/ppermute | solution.py:300
  55.6 3.7 %collective-permute-start.3 = (bf16[128,4224]{1,0:T(8,128)(2,1)}, bf16[128,4224]{1,0:T(8,128)(2,1)S(1)}, u32[]{:S(2)}, u32[]{:S(2)}) collective-permute-start(bf16[128,4224]{1,0:T(8,128)(2,1)} %collective-permute-done.1.refs_1_), channel_id=1, source_target_pairs={{0,14},{2,0},{4,2},{6,4},{8,6},{10,8},{12,10},{14,12},{1,15},{3,1}... | collective-permute-start | bytes 3244040 | tf_op jit(solution)/shard_map/ppermute | solution.py:301
  59.4 22.4 %collective-permute-done.2.refs_0_ = bf16[128,4224]{1,0:T(8,128)(2,1)S(1)} collective-permute-done((bf16[128,4224]{1,0:T(8,128)(2,1)S(1)}, bf16[128,4224]{1,0:T(8,128)(2,1)S(1)}, u32[]{:S(2)}, u32[]{:S(2)}) %collective-permute-start.2) | collective-permute-done | bytes 1081376 | tf_op jit(solution)/shard_map/ppermute | solution.py:300
  81.8 2.4 collective-permute-done.3.refs_1_
  89.7 5.1 %all-to-all-start.2 = ((bf16[8,2,16,4096]{3,2,1,0:T(8,128)(2,1)}), bf16[8,2,16,4096]{3,2,1,0:T(8,128)(2,1)}, u32[]{:S(2)}, u32[]{:S(2)}) async-start(bf16[8,2,16,4096]{3,2,1,0:T(8,128)(2,1)} %copy-done.8), calls=%async_computation.2 | async-start | bytes 4194304 | tf_op jit(solution)/shard_map/all_to_all | solution.py:294
  94.9 4.6 %collective-permute-start.4 = (bf16[128,4224]{1,0:T(8,128)(2,1)S(1)}, bf16[128,4224]{1,0:T(8,128)(2,1)S(1)}, u32[]{:S(2)}, u32[]{:S(2)}) collective-permute-start(bf16[128,4224]{1,0:T(8,128)(2,1)S(1)} %copy-done.13), channel_id=1, source_target_pairs={{0,2},{2,4},{4,6},{6,8},{8,10},{10,12},{12,14},{14,0},{1,3},{3,5},... | collective-permute-start | bytes 3244040 | tf_op jit(solution)/shard_map/ppermute | solution.py:300
  101.4 22.0 %collective-permute-done.4.refs_0_ = bf16[128,4224]{1,0:T(8,128)(2,1)S(1)} collective-permute-done((bf16[128,4224]{1,0:T(8,128)(2,1)S(1)}, bf16[128,4224]{1,0:T(8,128)(2,1)S(1)}, u32[]{:S(2)}, u32[]{:S(2)}) %collective-permute-start.4) | collective-permute-done | bytes 1081376 | tf_op jit(solution)/shard_map/ppermute | solution.py:300
  123.4 3.3 %collective-permute-done.5.refs_1_ = bf16[128,4224]{1,0:T(8,128)(2,1)S(1)} collective-permute-done((bf16[128,4224]{1,0:T(8,128)(2,1)}, bf16[128,4224]{1,0:T(8,128)(2,1)S(1)}, u32[]{:S(2)}, u32[]{:S(2)}) %collective-permute-start.5) | collective-permute-done | bytes 1081376 | tf_op jit(solution)/shard_map/ppermute | solution.py:301
  126.7 2.1 shard_map.119
  128.9 5.6 %all-to-all-start.3 = ((bf16[8,2,16,4096]{3,2,1,0:T(8,128)(2,1)}), bf16[8,2,16,4096]{3,2,1,0:T(8,128)(2,1)}, u32[]{:S(2)}, u32[]{:S(2)}) async-start(bf16[8,2,16,4096]{3,2,1,0:T(8,128)(2,1)} %shard_map.119), calls=%async_computation.3 | async-start | bytes 4194304 | tf_op jit(solution)/shard_map/all_to_all | solution.py:294
  134.5 3.4 %collective-permute-start.6 = (bf16[64,4224]{1,0:T(8,128)(2,1)S(1)}, bf16[64,4224]{1,0:T(8,128)(2,1)S(1)}, u32[]{:S(2)}, u32[]{:S(2)}) collective-permute-start(bf16[64,4224]{1,0:T(8,128)(2,1)S(1)} %slice.8), channel_id=1, source_target_pairs={{0,2},{2,4},{4,6},{6,8},{8,10},{10,12},{12,14},{14,0},{1,3},{3,5},... | collective-permute-start | bytes 1622024 | tf_op jit(solution)/shard_map/ppermute | solution.py:304
  137.9 3.1 %collective-permute-start.7 = (bf16[64,4224]{1,0:T(8,128)(2,1)S(1)}, bf16[64,4224]{1,0:T(8,128)(2,1)S(1)}, u32[]{:S(2)}, u32[]{:S(2)}) collective-permute-start(bf16[64,4224]{1,0:T(8,128)(2,1)S(1)} %slice.9), channel_id=1, source_target_pairs={{0,14},{2,0},{4,2},{6,4},{8,6},{10,8},{12,10},{14,12},{1,15},{3,1}... | collective-permute-start | bytes 1622024 | tf_op jit(solution)/shard_map/ppermute | solution.py:305
  141.0 10.6 %collective-permute-done.6.refs_0_ = bf16[64,4224]{1,0:T(8,128)(2,1)S(1)} collective-permute-done((bf16[64,4224]{1,0:T(8,128)(2,1)S(1)}, bf16[64,4224]{1,0:T(8,128)(2,1)S(1)}, u32[]{:S(2)}, u32[]{:S(2)}) %collective-permute-start.6) | collective-permute-done | bytes 540704 | tf_op jit(solution)/shard_map/ppermute | solution.py:304
  155.0 5.9 %all-to-all-done.3.refs_1_.refs_6_ = bf16[8,2,16,4096]{3,2,1,0:T(8,128)(2,1)} async-done(((bf16[8,2,16,4096]{3,2,1,0:T(8,128)(2,1)}), bf16[8,2,16,4096]{3,2,1,0:T(8,128)(2,1)}, u32[]{:S(2)}, u32[]{:S(2)}) %all-to-all-start.3) | async-done | bytes 2097184 | tf_op jit(solution)/shard_map/all_to_all | solution.py:294
  160.9 4.3 %all-to-all-start.4 = ((bf16[8,1,16,4096]{3,2,1,0:T(8,128)(2,1)}), bf16[8,1,16,4096]{3,2,1,0:T(8,128)(2,1)S(1)}, u32[]{:S(2)}, u32[]{:S(2)}) async-start(bf16[8,1,16,4096]{3,2,1,0:T(8,128)(2,1)} %copy-done.10), calls=%async_computation.4 | async-start | bytes 2097152 | tf_op jit(solution)/shard_map/all_to_all | solution.py:294
  168.7 2.9 %shard_map.118 = (bf16[256,16]{1,0:T(8,128)(2,1)S(1)}, f32[16,768]{1,0:T(8,128)S(1)}, f32[16,4096]{1,0:T(8,128)S(1)}) custom-call(s32[1]{0:T(128)} %bitcast.me.refs_0_, bf16[8,2,16,4096]{3,2,1,0:T(8,128)(2,1)} %all-to-all-done.2.refs_1_.refs_4_, bf16[64,16,768]{2,1,0:T(8,128)(2,1)S(1)} %bitcast.14, bf16[16,768]{1,0:T(8,128)(2,1)S(1)} %bitcast.24, ...), custom_call_target="tpu_custom_call" | custom-call | tf_op jit(solution)/shard_map/pallas_call | solution.py:169
  171.6 2.9 %shard_map.120 = (bf16[256,16]{1,0:T(8,128)(2,1)S(1)}, f32[16,768]{1,0:T(8,128)S(1)}, f32[16,4096]{1,0:T(8,128)S(1)}) custom-call(s32[1]{0:T(128)} %bitcast.me.refs_0_, bf16[8,2,16,4096]{3,2,1,0:T(8,128)(2,1)} %all-to-all-done.3.refs_1_.refs_6_, bf16[64,16,768]{2,1,0:T(8,128)(2,1)S(1)} %bitcast.15, bf16[16,768]{1,0:T(8,128)(2,1)S(1)} %bitcast.25, ...), custom_call_target="tpu_custom_call" | custom-call | tf_op jit(solution)/shard_map/pallas_call | solution.py:169
  174.5 5.8 %all-to-all-done.4.refs_1_.refs_8_ = bf16[8,1,16,4096]{3,2,1,0:T(8,128)(2,1)S(1)} async-done(((bf16[8,1,16,4096]{3,2,1,0:T(8,128)(2,1)}), bf16[8,1,16,4096]{3,2,1,0:T(8,128)(2,1)S(1)}, u32[]{:S(2)}, u32[]{:S(2)}) %all-to-all-start.4) | async-done | bytes 1048608 | tf_op jit(solution)/shard_map/all_to_all | solution.py:294
  181.2 18.1 %all_to_all.40.got = bf16[8,16,608]{2,1,0:T(8,128)(2,1)} all-to-all(bf16[8,16,608]{2,1,0:T(8,128)(2,1)S(1)} %get-tuple-element.32), channel_id=1, replica_groups=mesh['dp'=8,'x'=4,'y'=8,'core'=2] {'dp'}, dimensions={0} | all-to-all | bytes 311296 | tf_op jit(solution)/shard_map/all_to_all | solution.py:315
  201.0 5.9 %all-to-all-start.6 = ((bf16[8,16,608]{2,1,0:T(8,128)(2,1)}), bf16[8,16,608]{2,1,0:T(8,128)(2,1)S(1)}, u32[]{:S(2)}, u32[]{:S(2)}) async-start(bf16[8,16,608]{2,1,0:T(8,128)(2,1)} %shard_map.124), calls=%async_computation.6 | async-start | bytes 327680 | tf_op jit(solution)/shard_map/all_to_all | solution.py:316
  207.5 4.9 %all-to-all-done.6.got = bf16[8,16,608]{2,1,0:T(8,128)(2,1)S(1)} async-done(((bf16[8,16,608]{2,1,0:T(8,128)(2,1)}), bf16[8,16,608]{2,1,0:T(8,128)(2,1)S(1)}, u32[]{:S(2)}, u32[]{:S(2)}) %all-to-all-start.6) | async-done | bytes 155680 | tf_op jit(solution)/shard_map/all_to_all | solution.py:316
  215.2 12.8 %all_to_all.41.got = bf16[8,16,608]{2,1,0:T(8,128)(2,1)} all-to-all(bf16[8,16,608]{2,1,0:T(8,128)(2,1)} %shard_map.125), channel_id=1, replica_groups=mesh['dp'=8,'x'=4,'y'=8,'core'=2] {'y'}, dimensions={0} | all-to-all | bytes 311296 | tf_op jit(solution)/shard_map/all_to_all | solution.py:317
  228.0 2.2 shard_map.126
  231.8 2.8 %copy-done.9 = bf16[8,768,512]{2,1,0:T(8,128)(2,1)S(1)} copy-done((bf16[8,768,512]{2,1,0:T(8,128)(2,1)S(1)}, bf16[8,768,512]{2,1,0:T(8,128)(2,1)}, u32[]{:S(2)}) %copy-start.9) | copy-done | bytes 6291480
  234.6 12.5 %shard_map.123 = bf16[64,16,768]{2,1,0:T(8,128)(2,1)} custom-call(s32[1]{0:T(128)} %bitcast.me.refs_0_, bf16[8,768,512]{2,1,0:T(8,128)(2,1)S(1)} %copy-done.9, bf16[16,768]{1,0:T(8,128)(2,1)S(1)} %bitcast.27, bf16[8,1,16,4096]{3,2,1,0:T(8,128)(2,1)S(1)} %copy-done.6, bf16[128,16]{1,0:T(8,128)(2,1)S(1)} %get-tuple-element.19.refs_1_, ...), custom_call_target="tpu_custom_call" | custom-call | tf_op jit(solution)/shard_map/pallas_call | solution.py:196
  (61 shorter events, 31.9 us)
Async XLA Ops:
  7.2 223.1 %all-gather.2.cloned.1.call-start = ((), (), s32[]{:S(2)}) async-start(), calls=%async_computation.8 | async-start | bytes 7077888 | tf_op jit(solution)/shard_map/all_gather | solution.py:287
  7.9 1.2 copy-start.15
  11.3 24.4 %collective-permute-start = (bf16[128,4224]{1,0:T(8,128)(2,1)S(1)}, bf16[128,4224]{1,0:T(8,128)(2,1)S(1)}, u32[]{:S(2)}, u32[]{:S(2)}) collective-permute-start(bf16[128,4224]{1,0:T(8,128)(2,1)S(1)} %shard_map.112.refs_0_), channel_id=1, source_target_pairs={{0,2},{2,4},{4,6},{6,8},{8,10},{10,12},{12,14},{14,0},{1,3},{3,5},... | collective-permute-start | bytes 3244040 | tf_op jit(solution)/shard_map/ppermute | solution.py:300
  15.3 22.6 %collective-permute-start.1 = (bf16[128,4224]{1,0:T(8,128)(2,1)S(1)}, bf16[128,4224]{1,0:T(8,128)(2,1)}, u32[]{:S(2)}, u32[]{:S(2)}) collective-permute-start(bf16[128,4224]{1,0:T(8,128)(2,1)S(1)} %shard_map.112.refs_0_), channel_id=1, source_target_pairs={{0,14},{2,0},{4,2},{6,4},{8,6},{10,8},{12,10},{14,12},{1,15},{3,1}... | collective-permute-start | bytes 3244040 | tf_op jit(solution)/shard_map/ppermute | solution.py:301
  20.6 24.7 %all-to-all-start = ((bf16[8,1,16,4096]{3,2,1,0:T(8,128)(2,1)}), bf16[8,1,16,4096]{3,2,1,0:T(8,128)(2,1)S(1)}, u32[]{:S(2)}, u32[]{:S(2)}) async-start(bf16[8,1,16,4096]{3,2,1,0:T(8,128)(2,1)} %shard_map.113), calls=%async_computation | async-start | bytes 2097152 | tf_op jit(solution)/shard_map/all_to_all | solution.py:294
  40.0 1.4 copy-start.7
  45.2 1.0 copy-start.4
  46.3 42.2 %all-to-all-start.1 = ((bf16[8,2,16,4096]{3,2,1,0:T(8,128)(2,1)}), bf16[8,2,16,4096]{3,2,1,0:T(8,128)(2,1)S(1)}, u32[]{:S(2)}, u32[]{:S(2)}) async-start(bf16[8,2,16,4096]{3,2,1,0:T(8,128)(2,1)} %copy-done.7), calls=%async_computation.1 | async-start | bytes 4194304 | tf_op jit(solution)/shard_map/all_to_all | solution.py:294
  52.4 29.3 %collective-permute-start.2 = (bf16[128,4224]{1,0:T(8,128)(2,1)S(1)}, bf16[128,4224]{1,0:T(8,128)(2,1)S(1)}, u32[]{:S(2)}, u32[]{:S(2)}) collective-permute-start(bf16[128,4224]{1,0:T(8,128)(2,1)S(1)} %collective-permute-done.refs_0_), channel_id=1, source_target_pairs={{0,2},{2,4},{4,6},{6,8},{8,10},{10,12},{12,14},{14,0},{1,3},{3,5},... | collective-permute-start | bytes 3244040 | tf_op jit(solution)/shard_map/ppermute | solution.py:300
  55.6 28.6 %collective-permute-start.3 = (bf16[128,4224]{1,0:T(8,128)(2,1)}, bf16[128,4224]{1,0:T(8,128)(2,1)S(1)}, u32[]{:S(2)}, u32[]{:S(2)}) collective-permute-start(bf16[128,4224]{1,0:T(8,128)(2,1)} %collective-permute-done.1.refs_1_), channel_id=1, source_target_pairs={{0,14},{2,0},{4,2},{6,4},{8,6},{10,8},{12,10},{14,12},{1,15},{3,1}... | collective-permute-start | bytes 3244040 | tf_op jit(solution)/shard_map/ppermute | solution.py:301
  84.2 1.0 copy-start.14
  86.0 1.4 copy-start.8
  87.4 1.0 copy-start.12
  88.4 1.3 copy-start.1
  88.4 6.4 %copy-start.13 = (bf16[128,4224]{1,0:T(8,128)(2,1)S(1)}, bf16[128,4224]{1,0:T(8,128)(2,1)}, u32[]{:S(2)}) copy-start(bf16[128,4224]{1,0:T(8,128)(2,1)} %copy-done.12) | copy-start | bytes 3244036
  89.7 39.1 %all-to-all-start.2 = ((bf16[8,2,16,4096]{3,2,1,0:T(8,128)(2,1)}), bf16[8,2,16,4096]{3,2,1,0:T(8,128)(2,1)}, u32[]{:S(2)}, u32[]{:S(2)}) async-start(bf16[8,2,16,4096]{3,2,1,0:T(8,128)(2,1)} %copy-done.8), calls=%async_computation.2 | async-start | bytes 4194304 | tf_op jit(solution)/shard_map/all_to_all | solution.py:294
  94.9 28.6 %collective-permute-start.4 = (bf16[128,4224]{1,0:T(8,128)(2,1)S(1)}, bf16[128,4224]{1,0:T(8,128)(2,1)S(1)}, u32[]{:S(2)}, u32[]{:S(2)}) collective-permute-start(bf16[128,4224]{1,0:T(8,128)(2,1)S(1)} %copy-done.13), channel_id=1, source_target_pairs={{0,2},{2,4},{4,6},{6,8},{8,10},{10,12},{12,14},{14,0},{1,3},{3,5},... | collective-permute-start | bytes 3244040 | tf_op jit(solution)/shard_map/ppermute | solution.py:300
  99.5 27.3 %collective-permute-start.5 = (bf16[128,4224]{1,0:T(8,128)(2,1)}, bf16[128,4224]{1,0:T(8,128)(2,1)S(1)}, u32[]{:S(2)}, u32[]{:S(2)}) collective-permute-start(bf16[128,4224]{1,0:T(8,128)(2,1)} %copy-done.14), channel_id=1, source_target_pairs={{0,14},{2,0},{4,2},{6,4},{8,6},{10,8},{12,10},{14,12},{1,15},{3,1}... | collective-permute-start | bytes 3244040 | tf_op jit(solution)/shard_map/ppermute | solution.py:301
  128.9 32.0 %all-to-all-start.3 = ((bf16[8,2,16,4096]{3,2,1,0:T(8,128)(2,1)}), bf16[8,2,16,4096]{3,2,1,0:T(8,128)(2,1)}, u32[]{:S(2)}, u32[]{:S(2)}) async-start(bf16[8,2,16,4096]{3,2,1,0:T(8,128)(2,1)} %shard_map.119), calls=%async_computation.3 | async-start | bytes 4194304 | tf_op jit(solution)/shard_map/all_to_all | solution.py:294
  134.5 17.1 %collective-permute-start.6 = (bf16[64,4224]{1,0:T(8,128)(2,1)S(1)}, bf16[64,4224]{1,0:T(8,128)(2,1)S(1)}, u32[]{:S(2)}, u32[]{:S(2)}) collective-permute-start(bf16[64,4224]{1,0:T(8,128)(2,1)S(1)} %slice.8), channel_id=1, source_target_pairs={{0,2},{2,4},{4,6},{6,8},{8,10},{10,12},{12,14},{14,0},{1,3},{3,5},... | collective-permute-start | bytes 1622024 | tf_op jit(solution)/shard_map/ppermute | solution.py:304
  137.9 15.6 %collective-permute-start.7 = (bf16[64,4224]{1,0:T(8,128)(2,1)S(1)}, bf16[64,4224]{1,0:T(8,128)(2,1)S(1)}, u32[]{:S(2)}, u32[]{:S(2)}) collective-permute-start(bf16[64,4224]{1,0:T(8,128)(2,1)S(1)} %slice.9), channel_id=1, source_target_pairs={{0,14},{2,0},{4,2},{6,4},{8,6},{10,8},{12,10},{14,12},{1,15},{3,1}... | collective-permute-start | bytes 1622024 | tf_op jit(solution)/shard_map/ppermute | solution.py:305
  154.0 1.0 copy-start.10
  154.9 10.3 %copy-start = (bf16[1,1,1024,768]{3,2,1,0:T(8,128)(2,1)S(1)}, bf16[1,1,1024,768]{3,2,1,0:T(8,128)(2,1)}, u32[]{:S(2)}) copy-start(bf16[1,1,1024,768]{3,2,1,0:T(8,128)(2,1)} %param.13) | copy-start | bytes 4718596
  154.9 10.3 %copy-start.11 = (bf16[1,16,4096]{2,1,0:T(8,128)(2,1)S(1)}, bf16[1,16,4096]{2,1,0:T(8,128)(2,1)}, u32[]{:S(2)}) copy-start(bf16[1,16,4096]{2,1,0:T(8,128)(2,1)} %param.16) | copy-start | bytes 393220
  154.9 10.3 %copy-start.16 = (bf16[1,16,768]{2,1,0:T(8,128)(2,1)S(1)}, bf16[1,16,768]{2,1,0:T(8,128)(2,1)}, u32[]{:S(2)}) copy-start(bf16[1,16,768]{2,1,0:T(8,128)(2,1)} %param.15) | copy-start | bytes 73732
  160.9 19.5 %all-to-all-start.4 = ((bf16[8,1,16,4096]{3,2,1,0:T(8,128)(2,1)}), bf16[8,1,16,4096]{3,2,1,0:T(8,128)(2,1)S(1)}, u32[]{:S(2)}, u32[]{:S(2)}) async-start(bf16[8,1,16,4096]{3,2,1,0:T(8,128)(2,1)} %copy-done.10), calls=%async_computation.4 | async-start | bytes 2097152 | tf_op jit(solution)/shard_map/all_to_all | solution.py:294
  165.2 2.2 copy-start.2
  165.2 1.4 copy-start.5
  181.2 49.1 %copy-start.6 = (bf16[8,1,16,4096]{3,2,1,0:T(8,128)(2,1)S(1)}, bf16[8,1,16,4096]{3,2,1,0:T(8,128)(2,1)}, u32[]{:S(2)}) copy-start(bf16[8,1,16,4096]{3,2,1,0:T(8,128)(2,1)} %copy-done.4) | copy-start | bytes 3145732
  201.0 11.5 %all-to-all-start.6 = ((bf16[8,16,608]{2,1,0:T(8,128)(2,1)}), bf16[8,16,608]{2,1,0:T(8,128)(2,1)S(1)}, u32[]{:S(2)}, u32[]{:S(2)}) async-start(bf16[8,16,608]{2,1,0:T(8,128)(2,1)} %shard_map.124), calls=%async_computation.6 | async-start | bytes 327680 | tf_op jit(solution)/shard_map/all_to_all | solution.py:316
  230.2 1.6 copy-start.3
  231.8 2.8 %copy-start.9 = (bf16[8,768,512]{2,1,0:T(8,128)(2,1)S(1)}, bf16[8,768,512]{2,1,0:T(8,128)(2,1)}, u32[]{:S(2)}) copy-start(bf16[8,768,512]{2,1,0:T(8,128)(2,1)} %all-gather.2.cloned.1.call-done.weight) | copy-start | bytes 18874372
  (4 other events, 2.7 us)
Sparse Core Ops, SparseCore 0:
  10.1 83.3 all-gather.1

commit v2 on v1

v2 whole, which is shorter than its diff:
```python
import functools

import jax
import jax.numpy as jnp
from jax import lax
from jax.experimental import pallas as pl
from jax.experimental.pallas import tpu as pltpu
from jax.sharding import Mesh, PartitionSpec as P

ADAPTER_SCALE = 2.0
COST_BUILD, COST_GRADS, COST_BACK = 8, 3, 10
GROUPS, NX, NY, NC = 8, 4, 8, 2
COLS = NX * NC
CAP = 16
META = 128
MIB = 1024 * 1024
VM = pl.BlockSpec(memory_space=pltpu.VMEM)
ANY = pl.BlockSpec(memory_space=pl.ANY)
HBM = pl.BlockSpec(memory_space=pltpu.HBM)
SM = pl.BlockSpec(memory_space=pltpu.SMEM)
NT = (((1,), (1,)), ((), ()))
TN = (((0,), (0,)), ((), ()))
NN = (((1,), (0,)), ((), ()))


def dot(a, b, dims):
    return lax.dot_general(a, b, dims, preferred_element_type=jnp.float32)


def params(mib):
    return pltpu.CompilerParams(vmem_limit_bytes=mib * MIB)


def cost(us):
    return pl.CostEstimate(flops=int(us * 1.0e9), bytes_accessed=int(us * 3.0e6), transcendentals=0)


def copies(pairs, sems):
    started = [pltpu.make_async_copy(src, dst, sems.at[i]) for i, (src, dst) in enumerate(pairs)]
    for copy in started:
        copy.start()
    return started


def pack_kernel(cot, weight, ids, slots, out, w_in, ids_in, slots_in, sems):
    width = cot.shape[1]
    coming = copies([(weight, w_in), (ids, ids_in), (slots, slots_in), (cot, out.at[:, pl.ds(0, width)])], sems)
    out[48:, width:] = jnp.zeros((out.shape[0] - 48, META), jnp.bfloat16)
    for copy in coming[:3]:
        copy.wait()
    w = w_in[...]
    hi = w.astype(jnp.bfloat16)
    rest = w - hi.astype(jnp.float32)
    mid = rest.astype(jnp.bfloat16)
    low = (rest - mid.astype(jnp.float32)).astype(jnp.bfloat16)
    rows = [
        ids_in[...].astype(jnp.float32),
        slots_in[...].astype(jnp.float32),
        hi.astype(jnp.float32),
        mid.astype(jnp.float32),
        low.astype(jnp.float32),
        jnp.zeros(low.shape, jnp.float32),
    ]
    out[0:48, width:] = jnp.concatenate(rows, axis=0).astype(jnp.bfloat16)
    coming[3].wait()


def pack(cot, weight, ids, slots):
    return pl.pallas_call(
        pack_kernel,
        name="pack",
        out_shape=jax.ShapeDtypeStruct((cot.shape[0], cot.shape[1] + META), jnp.bfloat16),
        in_specs=[HBM] * 4,
        out_specs=VM,
        scratch_shapes=[pltpu.VMEM(a.shape, a.dtype) for a in (weight, ids, slots)]
        + [pltpu.SemaphoreType.DMA((4,))],
        compiler_params=params(12),
        cost_estimate=cost(2),
    )(cot, weight, ids, slots)


def gate(values, after):
    return list(lax.optimization_barrier((tuple(values), tuple(after)))[0])


def build_kernel(numbered, me, *refs):
    blocks, (out, made, sems) = refs[:-3], refs[-3:]
    count = made.shape[2]
    for b in range(count):
        block = blocks[b]
        width = block.shape[1] - META
        routes = block[0:48, width:].astype(jnp.float32)
        expert = routes[0:8].astype(jnp.int32)
        slot = routes[8:16].astype(jnp.int32)
        weight = routes[16:24] + routes[24:32] + routes[32:40]
        across = expert % NC if numbered else (expert % NC + me[2]) % NC
        here = ((expert // NC) % NY == me[1]) & (slot < CAP)
        code = jnp.where(here, (expert // (NY * NC) * NC + across) * CAP + slot, -1)
        row = lax.broadcasted_iota(jnp.int32, (COLS * CAP, code.shape[1]), 0)
        pick = jnp.zeros(row.shape, jnp.float32)
        scale = jnp.zeros(row.shape, jnp.float32)
        for k in range(code.shape[0]):
            match = row == code[k : k + 1]
            pick = jnp.where(match, 1.0, pick)
            scale = jnp.where(match, weight[k : k + 1], scale)
        scale = jnp.sum(scale, axis=1, keepdims=True)
        pick = pick.astype(jnp.bfloat16)
        step = 1024
        for at in range(0, width, step):
            rows = (scale * dot(pick, block[:, at : at + step], NN)).astype(jnp.bfloat16)
            for d in range(COLS):
                made[d // NC, d % NC, b, :, at : at + step] = rows[d * CAP : (d + 1) * CAP]
    for copy in copies([(made.at[x], out.at[x]) for x in range(NX)], sems):
        copy.wait()


def build(n, me, blocks, numbered=False):
    width = blocks[0].shape[1] - META
    shape = (NX, NC, len(blocks), CAP, width)
    return pl.pallas_call(
        functools.partial(build_kernel, numbered),
        name=f"build_{n}",
        out_shape=jax.ShapeDtypeStruct(shape, jnp.bfloat16),
        in_specs=[SM] + [VM] * len(blocks),
        out_specs=HBM,
        scratch_shapes=[pltpu.VMEM(shape, jnp.bfloat16), pltpu.SemaphoreType.DMA((NX,))],
        compiler_params=params(8),
        cost_estimate=cost(COST_BUILD),
    )(me, *blocks)


def places(me, offsets):
    whole = offsets == (NY // 2,)
    order = [(x, c) for x in range(NX) for c in range(NC)]
    if not whole:
        order = [(x, (me[2] + dc) % NC) for dc in range(NC) for x in range(NX)]
    return [(x * NY + (me[1] + offset + NY) % NY) * NC + c for x, c in order for offset in offsets]


def grads_kernel(chunk, count, first, last, waits, *refs):
    me, refs = refs[0], refs[1 + waits :]
    parts, (hidden, amap, bmap), refs = refs[:count], refs[count : count + 3], refs[count + 3 :]
    old_a, old_b = (None, None) if first else refs[:2]
    rest = refs if first else refs[2:]
    hid, tok, sems = rest[-3:]
    outs = rest[:-3]
    if count == 1:
        coming = copies([(parts[0], tok)], sems)
    else:
        coming = copies([(parts[0].at[:, 0], tok.at[pl.ds(0, NX)])], sems)
    for i, src in enumerate(places(me, chunk)):
        hid[i * CAP : (i + 1) * CAP] = hidden[src]
    rows, width = hid.shape[0], tok.shape[-1]
    z = dot(hid[...], amap[...], NT).astype(jnp.bfloat16)
    if count == 2:
        tok[NX:] = parts[1][...]
    for copy in coming:
        copy.wait()
    tokens = tok[...].reshape(rows, width)
    rb = (ADAPTER_SCALE * dot(tokens, bmap[...], NT)).astype(jnp.bfloat16)
    outs[0][...] = rb
    grad_b = ADAPTER_SCALE * dot(z, tokens, TN)
    grad_a = dot(rb, hid[...], TN)
    if old_a is not None:
        grad_b = grad_b + old_b[...]
        grad_a = grad_a + old_a[...]
    if not last:
        outs[1][...] = grad_a
        outs[2][...] = grad_b
    else:
        sent = outs[1]
        wide_b = width // GROUPS
        wide_a = hid.shape[1] // GROUPS
        for z_to in range(GROUPS):
            sent[z_to, :, :wide_b] = grad_b[:, z_to * wide_b : (z_to + 1) * wide_b].astype(jnp.bfloat16)
            sent[z_to, :, wide_b : wide_b + wide_a] = grad_a[:, z_to * wide_a : (z_to + 1) * wide_a].astype(
                jnp.bfloat16
            )


def grads(n, me, parts, hidden, amap, bmap, old, chunk, last, after=()):
    pieces = COLS * len(chunk)
    rows = pieces * CAP
    rank, width = bmap.shape
    hidden_width = amap.shape[1]
    shapes = [jax.ShapeDtypeStruct((rows, rank), jnp.bfloat16)]
    if last:
        piece = width // GROUPS + hidden_width // GROUPS
        shapes += [jax.ShapeDtypeStruct((GROUPS, rank, piece), jnp.bfloat16)]
    else:
        shapes += [
            jax.ShapeDtypeStruct((rank, hidden_width), jnp.float32),
            jax.ShapeDtypeStruct((rank, width), jnp.float32),
        ]
    args = [hidden, amap, bmap] + list(old)
    return pl.pallas_call(
        functools.partial(grads_kernel, chunk, len(parts), not old, last, len(after)),
        name=f"grads_{n}",
        out_shape=shapes,
        in_specs=[SM] + [ANY] * len(after) + [HBM] + [VM] * (len(parts) - 1 + len(args)),
        out_specs=[VM] * len(shapes),
        scratch_shapes=[
            pltpu.VMEM((rows, hidden_width), jnp.bfloat16),
            pltpu.VMEM((COLS, len(chunk), CAP, width), jnp.bfloat16),
            pltpu.SemaphoreType.DMA((1,)),
        ],
        compiler_params=params(10),
        cost_estimate=cost(COST_GRADS),
    )(me, *after, *parts, *args)


def back_kernel(chunks, counts, more, me, weight, *refs):
    count = len(chunks)
    straights, refs = refs[:count], refs[count:]
    crosseds, refs = refs[: sum(counts) - count], refs[sum(counts) - count :]
    rbs, amap, refs = refs[:count], refs[count], refs[count + 1 + more :]
    out, toks, done = refs[0], refs[1 : 1 + count], refs[1 + count : 1 + 2 * count]
    sems, sems_out = refs[-2:]
    pairs = []
    for n in range(count):
        pairs.append((straights[n] if counts[n] == 1 else straights[n].at[:, 0], toks[n]))
    coming = copies(pairs, sems)
    going = []
    for n, chunk in enumerate(chunks):
        wide = weight.shape[-1]
        total = dot(rbs[n][...], amap[...], NN)
        coming[n].wait()
        parts = [toks[n]] + ([crosseds[n]] if counts[n] == 2 else [])
        for z in range(GROUPS):
            g = [part[:, :, :, z * wide : (z + 1) * wide].reshape(-1, wide) for part in parts]
            total = total + dot(jnp.concatenate(g, axis=0), weight[z], NT)
        done[n][...] = total.astype(jnp.bfloat16).reshape(done[n].shape)
        for i, src in enumerate(places(me, chunk)):
            copy = pltpu.make_async_copy(done[n].at[i], out.at[src], sems_out.at[len(going)])
            copy.start()
            going.append(copy)
    for copy in going:
        copy.wait()


def back(n, me, weight, amap, work, chunks, old=()):
    straights = [parts[0] for parts, rb in work]
    crosseds = [parts[1] for parts, rb in work if len(parts) == 2]
    rbs = [rb for parts, rb in work]
    counts = [len(parts) for parts, rb in work]
    hidden_width = amap.shape[1]
    pieces = [rb.shape[0] // CAP for rb in rbs]
    toks = [(COLS // len(parts),) + parts[0].shape[-3:] for parts, rb in work]
    return pl.pallas_call(
        functools.partial(back_kernel, chunks, counts, len(old)),
        name=f"back_{n}",
        out_shape=jax.ShapeDtypeStruct((NX * NY * NC, CAP, hidden_width), jnp.bfloat16),
        in_specs=[SM, VM] + [HBM] * len(work) + [VM] * (len(crosseds) + len(rbs) + 1) + [HBM] * len(old),
        out_specs=HBM,
        input_output_aliases={3 + sum(counts) + len(rbs): 0} if old else {},
        scratch_shapes=[pltpu.VMEM(tok, jnp.bfloat16) for tok in toks]
        + [pltpu.VMEM((piece, CAP, hidden_width), jnp.bfloat16) for piece in pieces]
        + [pltpu.SemaphoreType.DMA((len(work),)), pltpu.SemaphoreType.DMA((sum(pieces),))],
        compiler_params=params(14),
        cost_estimate=cost(COST_BACK),
    )(me, weight, *straights, *crosseds, *rbs, amap, *old)


def spread_kernel(got, out):
    total = jnp.sum(got[...].astype(jnp.float32), axis=0).astype(jnp.bfloat16)
    for d in range(COLS):
        out[d] = total


def spread(got):
    return pl.pallas_call(
        spread_kernel,
        name="spread",
        out_shape=jax.ShapeDtypeStruct((COLS,) + got.shape[1:], got.dtype),
        in_specs=[VM],
        out_specs=VM,
    )(got)


def turn_kernel(where, got, out):
    for y_to in range(NY):
        out[y_to] = got[where[y_to]]


def turn(where, got):
    return pl.pallas_call(
        turn_kernel,
        name="turn",
        out_shape=jax.ShapeDtypeStruct((NY,) + got.shape[1:], got.dtype),
        in_specs=[SM, VM],
        out_specs=VM,
    )(where, got)


def take_kernel(wide_b, where, got, out_a, out_b):
    row = got[where[NY]]
    out_b[...] = row[:, :wide_b]
    out_a[...] = row[:, wide_b:]


def take(where, got, wide_a, wide_b):
    rank = got.shape[1]
    return pl.pallas_call(
        functools.partial(take_kernel, wide_b),
        name="take",
        out_shape=[
            jax.ShapeDtypeStruct((rank, wide_a), got.dtype),
            jax.ShapeDtypeStruct((rank, wide_b), got.dtype),
        ],
        in_specs=[SM, VM],
        out_specs=[VM, VM],
    )(where, got)


def per_device(
    cotangent,
    route_weight,
    expert_ids,
    slot_ids,
    hidden_saved,
    down_weight,
    adapter_a,
    adapter_out_maps,
    rollout_owner,
):
    width = cotangent.shape[1]
    hidden_width = adapter_a.shape[2]
    x = lax.axis_index("x").astype(jnp.int32)
    y = lax.axis_index("y").astype(jnp.int32)
    c = lax.axis_index("core").astype(jnp.int32)
    me = jnp.stack([x, y, c])
    up = [(i, (i + 1) % NY) for i in range(NY)]
    down = [(i, (i - 1) % NY) for i in range(NY)]
    row = ("x", "core")
    experts = jnp.arange(NX * NY * NC, dtype=jnp.int32)
    takers = (x * NY + jnp.append(jnp.arange(NY, dtype=jnp.int32), y)) * NC + c
    taken = jnp.sum(jnp.where(rollout_owner[None, :] == takers[:, None], experts[None, :], 0), axis=1)
    beside = taken // (NY * NC) * NC + taken % NC
    where = jnp.where(jnp.arange(NY + 1) < NY, beside, taken // NC % NY)

    def send(built):
        return lax.all_to_all(built, "x", 0, 0, tiled=True)

    def cross(straight):
        return straight, lax.ppermute(straight[:, 1], "core", [(0, 1), (1, 0)])

    own = pack(cotangent, route_weight.T, expert_ids.T, slot_ids.T)
    weight = lax.all_gather(down_weight[0], "dp")
    hidden = hidden_saved.reshape(NX * NY * NC, CAP, hidden_width)
    amap = adapter_a[0]
    bmap = adapter_out_maps[0]

    chunks = [(0,)] + [(-d, d) for d in range(1, NY // 2)] + [(NY // 2,)]
    last = len(chunks) - 1
    old = ()
    work = []
    whole = []

    def settle(after=()):
        nonlocal old
        n = len(work)
        parts = whole[n]
        rb, *old = grads(n, me, parts, hidden, amap, bmap, old, chunks[n], n == last, after)
        work.append((parts, rb))
        return rb

    either = [(i * NC, (i + 1) % NY * NC) for i in range(NY)] + [(i * NC + 1, (i - 1) % NY * NC + 1) for i in range(NY)]
    held = [own]
    for w in range(1, last + 1):
        low, high = held[0], held[-1]
        if w < last:
            ahead = [lax.ppermute(low, "y", up), lax.ppermute(high, "y", down)]
        else:
            ahead = [lax.ppermute(jnp.where(c == 0, low, high), ("y", "core"), either)]
        done = []
        if w >= 3:
            done.append(settle())
        built = build(w - 1, me, held)
        straight = send(built)
        if w < last:
            whole.append(cross(straight))
        held = [gate([block], done + [built, where])[0] for block in ahead]
    built = build(last, me, held, True)
    final = lax.all_to_all(built.reshape((COLS,) + built.shape[2:]), row, 0, 0, tiled=True)
    rb = settle()
    whole.append(cross(gate([straight], [built, rb])[0]))
    rb = settle()
    whole.append(gate([final], [rb]))
    settle()

    def turn_back(n, begin, end, filled):
        return back(n, me, weight, amap, work[begin:end], chunks[begin:end], filled)

    got = lax.all_to_all(old[0], "dp", 0, 0, tiled=True)
    filled = turn_back(0, 0, 2, [])
    got, filled = gate([got, filled], [])
    row_items = lax.all_to_all(spread(got), row, 0, 0, tiled=True)
    filled = turn_back(1, 2, 3, [filled])
    row_items, filled = gate([row_items, filled], [])
    column_items = lax.all_to_all(turn(where, row_items), "y", 0, 0, tiled=True)
    filled = turn_back(2, 3, 5, [filled])
    column_items, grad_hidden = gate([column_items, filled], [])
    out_a, out_b = take(where, column_items, hidden_width // GROUPS, width // GROUPS)
    return (
        grad_hidden.reshape(1, 1, NX * NY * NC * CAP, hidden_width),
        out_a[None],
        out_b[None],
    )


def solution(mesh):
    parts = Mesh(mesh.devices.reshape(GROUPS, NX, NY, NC), ("dp", "x", "y", "core"))
    every = ("dp", "x", "y", "core")
    expert = ("x", "y", "core")
    return jax.shard_map(
        per_device,
        mesh=parts,
        in_specs=(
            P(every, None),
            P(every, None),
            P(every, None),
            P(every, None),
            P("dp", expert, None, None),
            P(expert, None, "dp"),
            P(expert, None, None),
            P(expert, None, None),
            P(),
        ),
        out_specs=(P("dp", expert, None, None), P(expert, None, "dp"), P(expert, None, "dp")),
        check_vma=False,
    )
```

time: 255 us -> 240 us (0.941)
  waiting for transfers between devices: 91.6 us -> 41.2 us
  blocking collectives: 30.9 us -> 0 us
  Pallas kernels: 34.3 us -> 56.6 us
  starting transfers between devices: 64.4 us -> 86 us
  local copies, waits for them, and re-layouts: 17.8 us -> 36.1 us
  other arithmetic: 0.65 us -> 3.2 us
    ppermute x8 -> x11, waiting for transfers between devices: 70.4 us -> 28.6 us  [the longest x6 26.7 us: per_device(): ahead = [lax.ppermute(low, 'y', up), lax.ppermute(high, 'y', down)]]
    all_to_all x2 -> x0, blocking collectives: 30.9 us -> none  [the longest x1 18.1 us: per_device(): got = lax.all_to_all(sent, 'dp', 0, 0, tiled=True)]
    pallas_call x15 -> x17, Pallas kernels: 34.3 us -> 56.6 us  [the longest x3 24.5 us: back(): pl.pallas_call(functools.partial(back_kernel, chunks, counts, len(old)),...]
    ppermute x8 -> x11, starting transfers between devices: 27.8 us -> 44.4 us  [the longest x4 23.7 us: cross(): return (straight, lax.ppermute(straight[:, 1], 'core', [(0, 1), (1, 0)]))]
    unnamed x42 -> x68, local copies, waits for them, and re-layouts: 17.8 us -> 30.4 us
    all_to_all x5 -> x7, starting transfers between devices: 30.7 us -> 37.2 us  [the longest x4 18.6 us: send(): return lax.all_to_all(built, 'x', 0, 0, tiled=True)]
    squeeze x0 -> x4, local copies, waits for them, and re-layouts: none -> 5.62 us  [cross(): return (straight, lax.ppermute(straight[:, 1], 'core', [(0, 1), (1, 0)]))]
    all_to_all x1, waiting for transfers between devices: 4.95 us -> 0.01 us  [per_device(): row_items = lax.all_to_all(spread(got), row, 0, 0, tiled=True)]
  transfers between devices with their start and end apart: 15 -> 20, of which waited for: 12 -> 9; matrix products, arithmetic and copies ran while one was open for 0% -> 4% of each run, Pallas kernels for 9% -> 22%
where the time goes in v2:
time: 240 us; the launch traced here: 238 us
  starting transfers between devices  86 us (36%)
  Pallas kernels  56.6 us (24%)
  waiting for transfers between devices  41.2 us (17%)
  local copies, waits for them, and re-layouts  36.1 us (15%)
  between operations  14.5 us (6%)
  other arithmetic  3.2 us (1%)
    unnamed x68, local copies, waits for them, and re-layouts  30.4 us
    ppermute x6, waiting for transfers between devices, per_device(): ahead = [lax.ppermute(low, 'y', up), lax.ppermute(high, 'y', down)]  26.7 us
    pallas_call x3, Pallas kernels, back(): pl.pallas_call(functools.partial(back_kernel, chunks, counts, len(old)),...  24.5 us
    ppermute x4, starting transfers between devices, cross(): return (straight, lax.ppermute(straight[:, 1], 'core', [(0, 1), (1, 0)]))  23.7 us
    ppermute x6, starting transfers between devices, per_device(): ahead = [lax.ppermute(low, 'y', up), lax.ppermute(high, 'y', down)]  18.7 us
    all_to_all x4, starting transfers between devices, send(): return lax.all_to_all(built, 'x', 0, 0, tiled=True)  18.6 us
    pallas_call x5, Pallas kernels, grads(): pl.pallas_call(functools.partial(grads_kernel, chunk, len(parts), not old...  15.6 us
    pallas_call x5, Pallas kernels, build(): pl.pallas_call(functools.partial(build_kernel, numbered), name=f'build_{n...  11.6 us
  transfers between devices with their start and end apart: 20, of which 9 were waited for; matrix products, arithmetic and copies ran while one was open for 4% of the time, Pallas kernels for 22%

profile of v2, /device:TPU:1, one launch (start us, length us, event | category | flops | bytes accessed | tf_op | source)
XLA Modules:
  0.0 237.6 jit_solution(18147321491616040077)
XLA Ops:
  10.6 5.9 %collective-permute-start.2 = (bf16[128,4224]{1,0:T(8,128)(2,1)S(1)}, bf16[128,4224]{1,0:T(8,128)(2,1)}, u32[]{:S(2)}, u32[]{:S(2)}) collective-permute-start(bf16[128,4224]{1,0:T(8,128)(2,1)S(1)} %pack.1.refs_0_), channel_id=1, source_target_pairs={{0,14},{2,0},{4,2},{6,4},{8,6},{10,8},{12,10},{14,12},{1,15},{3,1}... | collective-permute-start | bytes 3244040 | tf_op jit(solution)/shard_map/ppermute | solution.py:372
  20.6 4.0 %all-to-all-start = ((bf16[4,2,1,16,4096]{4,3,2,1,0:T(8,128)(2,1)}), bf16[4,2,1,16,4096]{4,3,2,1,0:T(8,128)(2,1)S(1)}, u32[]{:S(2)}, u32[]{:S(2)}) async-start(bf16[4,2,1,16,4096]{4,3,2,1,0:T(8,128)(2,1)} %build_0.1), calls=%async_computation | async-start | bytes 2097152 | tf_op jit(solution)/shard_map/all_to_all | solution.py:342
  26.1 10.9 %collective-permute-done.2.refs_1_ = bf16[128,4224]{1,0:T(8,128)(2,1)} collective-permute-done((bf16[128,4224]{1,0:T(8,128)(2,1)S(1)}, bf16[128,4224]{1,0:T(8,128)(2,1)}, u32[]{:S(2)}, u32[]{:S(2)}) %collective-permute-start.2) | collective-permute-done | bytes 1081376 | tf_op jit(solution)/shard_map/ppermute | solution.py:372
  37.1 5.2 %collective-permute-done.refs_0_ = bf16[128,4224]{1,0:T(8,128)(2,1)} collective-permute-done((bf16[128,4224]{1,0:T(8,128)(2,1)S(1)}, bf16[128,4224]{1,0:T(8,128)(2,1)}, u32[]{:S(2)}, u32[]{:S(2)}) %collective-permute-start) | collective-permute-done | bytes 1081376 | tf_op jit(solution)/shard_map/ppermute | solution.py:372
  42.2 3.7 %collective-permute-start.5 = (bf16[128,4224]{1,0:T(8,128)(2,1)}, bf16[128,4224]{1,0:T(8,128)(2,1)}, u32[]{:S(2)}, u32[]{:S(2)}) collective-permute-start(bf16[128,4224]{1,0:T(8,128)(2,1)} %collective-permute-done.2.refs_1_), channel_id=1, source_target_pairs={{0,14},{2,0},{4,2},{6,4},{8,6},{10,8},{12,10},{14,12},{1,15},{3,1}... | collective-permute-start | bytes 3244040 | tf_op jit(solution)/shard_map/ppermute | solution.py:372
  51.8 5.7 %all-to-all-start.1 = ((bf16[4,2,2,16,4096]{4,3,2,1,0:T(8,128)(2,1)}), bf16[4,2,2,16,4096]{4,3,2,1,0:T(8,128)(2,1)S(1)}, u32[]{:S(2)}, u32[]{:S(2)}) async-start(bf16[4,2,2,16,4096]{4,3,2,1,0:T(8,128)(2,1)} %copy-done.1), calls=%async_computation.1 | async-start | bytes 4194304 | tf_op jit(solution)/shard_map/all_to_all | solution.py:342
  58.4 4.6 %collective-permute-start.4 = (bf16[4,1,16,4096]{3,2,1,0:T(8,128)(2,1)}, bf16[4,1,16,4096]{3,2,1,0:T(8,128)(2,1)}, u32[]{:S(2)}, u32[]{:S(2)}) collective-permute-start(bf16[4,1,16,4096]{3,2,1,0:T(8,128)(2,1)} %slice_bitcast_fusion.3), channel_id=1, source_target_pairs={{0,1},{1,0},{2,3},{3,2},{4,5},{5,4},{6,7},{7,6},{8,9},{9,8},{10,11... | collective-permute-start | bytes 1572872 | tf_op jit(solution)/shard_map/ppermute | solution.py:345
  69.1 3.4 %collective-permute-done.1.refs_0_ = bf16[128,4224]{1,0:T(8,128)(2,1)} collective-permute-done((bf16[128,4224]{1,0:T(8,128)(2,1)}, bf16[128,4224]{1,0:T(8,128)(2,1)}, u32[]{:S(2)}, u32[]{:S(2)}) %collective-permute-start.1) | collective-permute-done | bytes 1081376 | tf_op jit(solution)/shard_map/ppermute | solution.py:372
  74.5 3.4 %collective-permute-start.3 = (bf16[128,4224]{1,0:T(8,128)(2,1)}, bf16[128,4224]{1,0:T(8,128)(2,1)}, u32[]{:S(2)}, u32[]{:S(2)}) collective-permute-start(bf16[128,4224]{1,0:T(8,128)(2,1)} %collective-permute-done.1.refs_0_), channel_id=1, source_target_pairs={{0,2},{2,4},{4,6},{6,8},{8,10},{10,12},{12,14},{14,0},{1,3},{3,5},... | collective-permute-start | bytes 3244040 | tf_op jit(solution)/shard_map/ppermute | solution.py:372
  81.8 4.4 %all-to-all-start.4 = ((bf16[4,2,2,16,4096]{4,3,2,1,0:T(8,128)(2,1)}), bf16[4,2,2,16,4096]{4,3,2,1,0:T(8,128)(2,1)}, u32[]{:S(2)}, u32[]{:S(2)}) async-start(bf16[4,2,2,16,4096]{4,3,2,1,0:T(8,128)(2,1)} %copy-done.2), calls=%async_computation.4 | async-start | bytes 4194304 | tf_op jit(solution)/shard_map/all_to_all | solution.py:342
  87.3 5.5 %collective-permute-start.8 = (bf16[4,2,16,4096]{3,2,1,0:T(8,128)(2,1)}, bf16[4,2,16,4096]{3,2,1,0:T(8,128)(2,1)}, u32[]{:S(2)}, u32[]{:S(2)}) collective-permute-start(bf16[4,2,16,4096]{3,2,1,0:T(8,128)(2,1)} %slice_bitcast_fusion.2), channel_id=1, source_target_pairs={{0,1},{1,0},{2,3},{3,2},{4,5},{5,4},{6,7},{7,6},{8,9},{9,8},{10,11... | collective-permute-start | bytes 3145736 | tf_op jit(solution)/shard_map/ppermute | solution.py:345
  92.8 4.2 %collective-permute-done.6.refs_1_ = bf16[128,4224]{1,0:T(8,128)(2,1)} collective-permute-done((bf16[128,4224]{1,0:T(8,128)(2,1)}, bf16[128,4224]{1,0:T(8,128)(2,1)}, u32[]{:S(2)}, u32[]{:S(2)}) %collective-permute-start.6) | collective-permute-done | bytes 1081376 | tf_op jit(solution)/shard_map/ppermute | solution.py:372
  97.0 3.0 %collective-permute-done.3.refs_0_ = bf16[128,4224]{1,0:T(8,128)(2,1)} collective-permute-done((bf16[128,4224]{1,0:T(8,128)(2,1)}, bf16[128,4224]{1,0:T(8,128)(2,1)}, u32[]{:S(2)}, u32[]{:S(2)}) %collective-permute-start.3) | collective-permute-done | bytes 1081376 | tf_op jit(solution)/shard_map/ppermute | solution.py:372
  109.3 4.4 %all-to-all-start.3 = ((bf16[4,2,2,16,4096]{4,3,2,1,0:T(8,128)(2,1)}), bf16[4,2,2,16,4096]{4,3,2,1,0:T(8,128)(2,1)}, u32[]{:S(2)}, u32[]{:S(2)}) async-start(bf16[4,2,2,16,4096]{4,3,2,1,0:T(8,128)(2,1)} %copy-done), calls=%async_computation.3 | async-start | bytes 4194304 | tf_op jit(solution)/shard_map/all_to_all | solution.py:342
  115.2 6.4 %collective-permute-start.9 = (bf16[4,2,16,4096]{3,2,1,0:T(8,128)(2,1)S(1)}, bf16[4,2,16,4096]{3,2,1,0:T(8,128)(2,1)S(1)}, u32[]{:S(2)}, u32[]{:S(2)}) collective-permute-start(bf16[4,2,16,4096]{3,2,1,0:T(8,128)(2,1)S(1)} %slice_bitcast_fusion.1), channel_id=1, source_target_pairs={{0,1},{1,0},{2,3},{3,2},{4,5},{5,4},{6,7},{7,6},{8,9},{9,8},{10,11... | collective-permute-start | bytes 3145736 | tf_op jit(solution)/shard_map/ppermute | solution.py:345
  121.6 3.0 %grads_1.1 = (bf16[256,16]{1,0:T(8,128)(2,1)S(1)}, f32[16,768]{1,0:T(8,128)S(1)}, f32[16,4096]{1,0:T(8,128)S(1)}) custom-call(s32[3]{0:T(128)S(1)} %pad_add_fusion.me.refs_0_, bf16[4,2,2,16,4096]{4,3,2,1,0:T(8,128)(2,1)S(1)} %all-to-all-done.1.refs_1_, bf16[4,2,16,4096]{3,2,1,0:T(8,128)(2,1)} %collective-permute-done.8.refs_2_.refs_3_, ...), custom_call_target="tpu_custom_call" | custom-call | flops 3000000000 | bytes 9000000 | tf_op jit(solution)/shard_map/grads_1/pallas_call | solution.py:196
  127.4 3.2 %grads_2.1 = (bf16[256,16]{1,0:T(8,128)(2,1)S(1)}, f32[16,768]{1,0:T(8,128)S(1)}, f32[16,4096]{1,0:T(8,128)S(1)}) custom-call(s32[3]{0:T(128)S(1)} %pad_add_fusion.me.refs_0_, bf16[4,2,2,16,4096]{4,3,2,1,0:T(8,128)(2,1)} %all-to-all-done.4.refs_1_.refs_0_, bf16[4,2,16,4096]{3,2,1,0:T(8,128)(2,1)S(1)} %collective-permute-done.9.refs_2_.refs_1_, ...), custom_call_target="tpu_custom_call" | custom-call | flops 3000000000 | bytes 9000000 | tf_op jit(solution)/shard_map/grads_2/pallas_call | solution.py:196
  132.3 3.4 %all-to-all-done.3.refs_1_.refs_0_ = bf16[4,2,2,16,4096]{4,3,2,1,0:T(8,128)(2,1)} async-done(((bf16[4,2,2,16,4096]{4,3,2,1,0:T(8,128)(2,1)}), bf16[4,2,2,16,4096]{4,3,2,1,0:T(8,128)(2,1)}, u32[]{:S(2)}, u32[]{:S(2)}) %all-to-all-start.3) | async-done | bytes 2097184 | tf_op jit(solution)/shard_map/all_to_all | solution.py:342
  138.0 7.3 %collective-permute-start.10 = (bf16[4,2,16,4096]{3,2,1,0:T(8,128)(2,1)}, bf16[4,2,16,4096]{3,2,1,0:T(8,128)(2,1)}, u32[]{:S(2)}, u32[]{:S(2)}) collective-permute-start(bf16[4,2,16,4096]{3,2,1,0:T(8,128)(2,1)} %slice_bitcast_fusion), channel_id=1, source_target_pairs={{0,1},{1,0},{2,3},{3,2},{4,5},{5,4},{6,7},{7,6},{8,9},{9,8},{10,11... | collective-permute-start | bytes 3145736 | tf_op jit(solution)/shard_map/ppermute | solution.py:345
  145.3 4.2 %all-to-all-start.2 = ((bf16[8,1,16,4096]{3,2,1,0:T(8,128)(2,1)}), bf16[8,1,16,4096]{3,2,1,0:T(8,128)(2,1)}, u32[]{:S(2)}, u32[]{:S(2)}) async-start(bf16[8,1,16,4096]{3,2,1,0:T(8,128)(2,1)} %bitcast.27), calls=%async_computation.2 | async-start | bytes 2097152 | tf_op jit(solution)/shard_map/all_to_all | solution.py:384
  151.8 3.9 %grads_3.1 = (bf16[256,16]{1,0:T(8,128)(2,1)S(1)}, f32[16,768]{1,0:T(8,128)S(1)}, f32[16,4096]{1,0:T(8,128)S(1)}) custom-call(s32[3]{0:T(128)S(1)} %pad_add_fusion.me.refs_0_, bf16[4,2,2,16,4096]{4,3,2,1,0:T(8,128)(2,1)} %all-to-all-done.3.refs_1_.refs_0_, bf16[4,2,16,4096]{3,2,1,0:T(8,128)(2,1)} %collective-permute-done.10.refs_2_, ...), custom_call_target="tpu_custom_call" | custom-call | flops 3000000000 | bytes 9000000 | tf_op jit(solution)/shard_map/grads_3/pallas_call | solution.py:196
  157.1 7.5 %all-to-all-done.2.refs_1_ = bf16[8,1,16,4096]{3,2,1,0:T(8,128)(2,1)} async-done(((bf16[8,1,16,4096]{3,2,1,0:T(8,128)(2,1)}), bf16[8,1,16,4096]{3,2,1,0:T(8,128)(2,1)}, u32[]{:S(2)}, u32[]{:S(2)}) %all-to-all-start.2) | async-done | bytes 1048608 | tf_op jit(solution)/shard_map/all_to_all | solution.py:384
  167.8 3.3 %grads_4.1 = (bf16[128,16]{1,0:T(8,128)(2,1)S(1)}, bf16[8,16,608]{2,1,0:T(8,128)(2,1)}) custom-call(s32[3]{0:T(128)S(1)} %pad_add_fusion.me.refs_0_, bf16[8,1,16,4096]{3,2,1,0:T(8,128)(2,1)} %all-to-all-done.2.refs_1_, bf16[64,16,768]{2,1,0:T(8,128)(2,1)S(1)} %bitcast.32, bf16[16,768]{1,0:T(8,128)(2,1)S(1)} %bitcast.42, bf16[16,4096]{1,0:T(8,128)(2,1)S(1)} %bitcast.37, ...), custom_call_target="tpu_custom_call" | custom-call | flops 3000000000 | bytes 9000000 | tf_op jit(solution)/shard_map/grads_4/pallas_call | solution.py:196
  171.7 10.2 %all-to-all-start.5 = ((bf16[8,16,608]{2,1,0:T(8,128)(2,1)}), bf16[8,16,608]{2,1,0:T(8,128)(2,1)}, u32[]{:S(2)}, u32[]{:S(2)}) async-start(bf16[8,16,608]{2,1,0:T(8,128)(2,1)} %get-tuple-element.55), calls=%async_computation.5 | async-start | bytes 327680 | tf_op jit(solution)/shard_map/all_to_all | solution.py:394
  182.0 2.8 %copy-done.4 = bf16[8,768,512]{2,1,0:T(8,128)(2,1)S(1)} copy-done((bf16[8,768,512]{2,1,0:T(8,128)(2,1)S(1)}, bf16[8,768,512]{2,1,0:T(8,128)(2,1)}, u32[]{:S(2)}) %copy-start.4) | copy-done | bytes 6291480
  184.8 9.6 %back_0.1.refs_4_ = bf16[64,16,768]{2,1,0:T(8,128)(2,1)} custom-call(s32[3]{0:T(128)S(1)} %pad_add_fusion.me.refs_0_, bf16[8,768,512]{2,1,0:T(8,128)(2,1)S(1)} %copy-done.4, bf16[4,2,1,16,4096]{4,3,2,1,0:T(8,128)(2,1)S(1)} %all-to-all-done.refs_1_.refs_0_, bf16[4,2,2,16,4096]{4,3,2,1,0:T(8,128)(2,1)S(1)} %all-to-all-done.1.refs_1_, ...), custom_call_target="tpu_custom_call" | custom-call | flops 10000000000 | bytes 30000000 | tf_op jit(solution)/shard_map/back_0/pallas_call | solution.py:249
  196.0 4.4 %all-to-all-start.6 = ((bf16[8,16,608]{2,1,0:T(8,128)(2,1)}), bf16[8,16,608]{2,1,0:T(8,128)(2,1)S(1)}, u32[]{:S(2)}, u32[]{:S(2)}) async-start(bf16[8,16,608]{2,1,0:T(8,128)(2,1)} %spread.1), calls=%async_computation.6 | async-start | bytes 327680 | tf_op jit(solution)/shard_map/all_to_all | solution.py:397
  200.4 2.8 %copy-done.5 = bf16[8,768,512]{2,1,0:T(8,128)(2,1)S(1)} copy-done((bf16[8,768,512]{2,1,0:T(8,128)(2,1)S(1)}, bf16[8,768,512]{2,1,0:T(8,128)(2,1)}, u32[]{:S(2)}) %copy-start.5) | copy-done | bytes 6291480
  204.5 4.5 %back_1.1.refs_6_ = bf16[64,16,768]{2,1,0:T(8,128)(2,1)} custom-call(s32[3]{0:T(128)S(1)} %pad_add_fusion.me.refs_0_, bf16[8,768,512]{2,1,0:T(8,128)(2,1)S(1)} %copy-done.5, bf16[4,2,2,16,4096]{4,3,2,1,0:T(8,128)(2,1)} %all-to-all-done.4.refs_1_.refs_0_, bf16[4,2,16,4096]{3,2,1,0:T(8,128)(2,1)S(1)} %copy-done.13, ...), custom_call_target="tpu_custom_call", output_to_operand_aliasing={{}: (6, {})} | custom-call | flops 10000000000 | bytes 30000000 | tf_op jit(solution)/shard_map/back_1/pallas_call | solution.py:249
  211.3 4.1 %all-to-all-start.7 = ((bf16[8,16,608]{2,1,0:T(8,128)(2,1)}), bf16[8,16,608]{2,1,0:T(8,128)(2,1)S(1)}, u32[]{:S(2)}, u32[]{:S(2)}) async-start(bf16[8,16,608]{2,1,0:T(8,128)(2,1)} %turn.1), calls=%async_computation.7 | async-start | bytes 327680 | tf_op jit(solution)/shard_map/all_to_all | solution.py:400
  215.4 2.8 %copy-done.6 = bf16[8,768,512]{2,1,0:T(8,128)(2,1)S(1)} copy-done((bf16[8,768,512]{2,1,0:T(8,128)(2,1)S(1)}, bf16[8,768,512]{2,1,0:T(8,128)(2,1)}, u32[]{:S(2)}) %copy-start.6) | copy-done | bytes 6291480
  218.2 10.4 %back_2.1 = bf16[64,16,768]{2,1,0:T(8,128)(2,1)} custom-call(s32[3]{0:T(128)S(1)} %pad_add_fusion.me.refs_0_, bf16[8,768,512]{2,1,0:T(8,128)(2,1)S(1)} %copy-done.6, bf16[4,2,2,16,4096]{4,3,2,1,0:T(8,128)(2,1)} %all-to-all-done.3.refs_1_.refs_0_, bf16[8,1,16,4096]{3,2,1,0:T(8,128)(2,1)} %all-to-all-done.2.refs_1_, ...), custom_call_target="tpu_custom_call", output_to_operand_aliasing={{}: (8, {})} | custom-call | flops 10000000000 | bytes 30000000 | tf_op jit(solution)/shard_map/back_2/pallas_call | solution.py:249
  (104 shorter events, 60.8 us)
Async XLA Ops:
  10.6 26.5 %collective-permute-start.2 = (bf16[128,4224]{1,0:T(8,128)(2,1)S(1)}, bf16[128,4224]{1,0:T(8,128)(2,1)}, u32[]{:S(2)}, u32[]{:S(2)}) collective-permute-start(bf16[128,4224]{1,0:T(8,128)(2,1)S(1)} %pack.1.refs_0_), channel_id=1, source_target_pairs={{0,14},{2,0},{4,2},{6,4},{8,6},{10,8},{12,10},{14,12},{1,15},{3,1}... | collective-permute-start | bytes 3244040 | tf_op jit(solution)/shard_map/ppermute | solution.py:372
  16.5 25.7 %collective-permute-start = (bf16[128,4224]{1,0:T(8,128)(2,1)S(1)}, bf16[128,4224]{1,0:T(8,128)(2,1)}, u32[]{:S(2)}, u32[]{:S(2)}) collective-permute-start(bf16[128,4224]{1,0:T(8,128)(2,1)S(1)} %pack.1.refs_0_), channel_id=1, source_target_pairs={{0,2},{2,4},{4,6},{6,8},{8,10},{10,12},{12,14},{14,0},{1,3},{3,5},... | collective-permute-start | bytes 3244040 | tf_op jit(solution)/shard_map/ppermute | solution.py:372
  20.6 4.9 %copy-start.33 = (s32[64]{0:T(128)S(1)}, s32[64]{0:T(128)}, u32[]{:S(2)}) copy-start(s32[64]{0:T(128)} %param.17) | copy-start | bytes 772
  20.6 31.2 %all-to-all-start = ((bf16[4,2,1,16,4096]{4,3,2,1,0:T(8,128)(2,1)}), bf16[4,2,1,16,4096]{4,3,2,1,0:T(8,128)(2,1)S(1)}, u32[]{:S(2)}, u32[]{:S(2)}) async-start(bf16[4,2,1,16,4096]{4,3,2,1,0:T(8,128)(2,1)} %build_0.1), calls=%async_computation | async-start | bytes 2097152 | tf_op jit(solution)/shard_map/all_to_all | solution.py:342
  24.6 157.4 %all-gather.2.cloned.1.call-start = ((), (), s32[]{:S(2)}) async-start(), calls=%async_computation.8 | async-start | bytes 7077888 | tf_op jit(solution)/shard_map/all_gather | solution.py:348
  42.2 26.9 %collective-permute-start.5 = (bf16[128,4224]{1,0:T(8,128)(2,1)}, bf16[128,4224]{1,0:T(8,128)(2,1)}, u32[]{:S(2)}, u32[]{:S(2)}) collective-permute-start(bf16[128,4224]{1,0:T(8,128)(2,1)} %collective-permute-done.2.refs_1_), channel_id=1, source_target_pairs={{0,14},{2,0},{4,2},{6,4},{8,6},{10,8},{12,10},{14,12},{1,15},{3,1}... | collective-permute-start | bytes 3244040 | tf_op jit(solution)/shard_map/ppermute | solution.py:372
  45.9 26.6 %collective-permute-start.1 = (bf16[128,4224]{1,0:T(8,128)(2,1)}, bf16[128,4224]{1,0:T(8,128)(2,1)}, u32[]{:S(2)}, u32[]{:S(2)}) collective-permute-start(bf16[128,4224]{1,0:T(8,128)(2,1)} %collective-permute-done.refs_0_), channel_id=1, source_target_pairs={{0,2},{2,4},{4,6},{6,8},{8,10},{10,12},{12,14},{14,0},{1,3},{3,5},... | collective-permute-start | bytes 3244040 | tf_op jit(solution)/shard_map/ppermute | solution.py:372
  51.8 13.0 %copy-start.14 = (bf16[1,16,4096]{2,1,0:T(8,128)(2,1)S(1)}, bf16[1,16,4096]{2,1,0:T(8,128)(2,1)}, u32[]{:S(2)}) copy-start(bf16[1,16,4096]{2,1,0:T(8,128)(2,1)} %param.16) | copy-start | bytes 393220
  51.8 13.0 %copy-start.15 = (bf16[1,16,768]{2,1,0:T(8,128)(2,1)S(1)}, bf16[1,16,768]{2,1,0:T(8,128)(2,1)}, u32[]{:S(2)}) copy-start(bf16[1,16,768]{2,1,0:T(8,128)(2,1)} %param.15) | copy-start | bytes 73732
  51.8 30.0 %all-to-all-start.1 = ((bf16[4,2,2,16,4096]{4,3,2,1,0:T(8,128)(2,1)}), bf16[4,2,2,16,4096]{4,3,2,1,0:T(8,128)(2,1)S(1)}, u32[]{:S(2)}, u32[]{:S(2)}) async-start(bf16[4,2,2,16,4096]{4,3,2,1,0:T(8,128)(2,1)} %copy-done.1), calls=%async_computation.1 | async-start | bytes 4194304 | tf_op jit(solution)/shard_map/all_to_all | solution.py:342
  58.4 6.5 %collective-permute-start.4 = (bf16[4,1,16,4096]{3,2,1,0:T(8,128)(2,1)}, bf16[4,1,16,4096]{3,2,1,0:T(8,128)(2,1)}, u32[]{:S(2)}, u32[]{:S(2)}) collective-permute-start(bf16[4,1,16,4096]{3,2,1,0:T(8,128)(2,1)} %slice_bitcast_fusion.3), channel_id=1, source_target_pairs={{0,1},{1,0},{2,3},{3,2},{4,5},{5,4},{6,7},{7,6},{8,9},{9,8},{10,11... | collective-permute-start | bytes 1572872 | tf_op jit(solution)/shard_map/ppermute | solution.py:345
  69.1 11.3 %copy-start.27 = (bf16[128,16]{1,0:T(8,128)(2,1)}, bf16[128,16]{1,0:T(8,128)(2,1)S(1)}, u32[]{:S(2)}) copy-start(bf16[128,16]{1,0:T(8,128)(2,1)S(1)} %get-tuple-element.37.refs_4_) | copy-start | bytes 12292
  72.5 24.5 %collective-permute-start.6 = (bf16[128,4224]{1,0:T(8,128)(2,1)}, bf16[128,4224]{1,0:T(8,128)(2,1)}, u32[]{:S(2)}, u32[]{:S(2)}) collective-permute-start(bf16[128,4224]{1,0:T(8,128)(2,1)} %collective-permute-done.5.refs_1_), channel_id=1, source_target_pairs={{0,14},{2,0},{4,2},{6,4},{8,6},{10,8},{12,10},{14,12},{1,15},{3,1}... | collective-permute-start | bytes 3244040 | tf_op jit(solution)/shard_map/ppermute | solution.py:372
  74.5 25.6 %collective-permute-start.3 = (bf16[128,4224]{1,0:T(8,128)(2,1)}, bf16[128,4224]{1,0:T(8,128)(2,1)}, u32[]{:S(2)}, u32[]{:S(2)}) collective-permute-start(bf16[128,4224]{1,0:T(8,128)(2,1)} %collective-permute-done.1.refs_0_), channel_id=1, source_target_pairs={{0,2},{2,4},{4,6},{6,8},{8,10},{10,12},{12,14},{14,0},{1,3},{3,5},... | collective-permute-start | bytes 3244040 | tf_op jit(solution)/shard_map/ppermute | solution.py:372
  81.8 27.5 %all-to-all-start.4 = ((bf16[4,2,2,16,4096]{4,3,2,1,0:T(8,128)(2,1)}), bf16[4,2,2,16,4096]{4,3,2,1,0:T(8,128)(2,1)}, u32[]{:S(2)}, u32[]{:S(2)}) async-start(bf16[4,2,2,16,4096]{4,3,2,1,0:T(8,128)(2,1)} %copy-done.2), calls=%async_computation.4 | async-start | bytes 4194304 | tf_op jit(solution)/shard_map/all_to_all | solution.py:342
  87.3 34.3 %collective-permute-start.8 = (bf16[4,2,16,4096]{3,2,1,0:T(8,128)(2,1)}, bf16[4,2,16,4096]{3,2,1,0:T(8,128)(2,1)}, u32[]{:S(2)}, u32[]{:S(2)}) collective-permute-start(bf16[4,2,16,4096]{3,2,1,0:T(8,128)(2,1)} %slice_bitcast_fusion.2), channel_id=1, source_target_pairs={{0,1},{1,0},{2,3},{3,2},{4,5},{5,4},{6,7},{7,6},{8,9},{9,8},{10,11... | collective-permute-start | bytes 3145736 | tf_op jit(solution)/shard_map/ppermute | solution.py:345
  105.0 1.4 copy-start
  106.4 18.1 %collective-permute-start.7 = (bf16[128,4224]{1,0:T(8,128)(2,1)}, bf16[128,4224]{1,0:T(8,128)(2,1)}, u32[]{:S(2)}, u32[]{:S(2)}) collective-permute-start(bf16[128,4224]{1,0:T(8,128)(2,1)} %broadcast_select_fusion), channel_id=1, source_target_pairs={{0,2},{2,4},{4,6},{6,8},{8,10},{10,12},{12,14},{14,0},{1,15},{3,1}... | collective-permute-start | bytes 3244040 | tf_op jit(solution)/shard_map/ppermute | solution.py:374
  109.3 26.4 %all-to-all-start.3 = ((bf16[4,2,2,16,4096]{4,3,2,1,0:T(8,128)(2,1)}), bf16[4,2,2,16,4096]{4,3,2,1,0:T(8,128)(2,1)}, u32[]{:S(2)}, u32[]{:S(2)}) async-start(bf16[4,2,2,16,4096]{4,3,2,1,0:T(8,128)(2,1)} %copy-done), calls=%async_computation.3 | async-start | bytes 4194304 | tf_op jit(solution)/shard_map/all_to_all | solution.py:342
  113.7 7.8 %copy-start.8 = (bf16[1,1,1024,768]{3,2,1,0:T(8,128)(2,1)S(1)}, bf16[1,1,1024,768]{3,2,1,0:T(8,128)(2,1)}, u32[]{:S(2)}) copy-start(bf16[1,1,1024,768]{3,2,1,0:T(8,128)(2,1)} %param.13) | copy-start | bytes 4718596
  113.7 7.8 %copy-start.20 = (f32[16,4096]{1,0:T(8,128)S(1)}, f32[16,4096]{1,0:T(8,128)}, u32[]{:S(2)}) copy-start(f32[16,4096]{1,0:T(8,128)} %copy-done.19) | copy-start | bytes 786436
  115.2 12.2 %collective-permute-start.9 = (bf16[4,2,16,4096]{3,2,1,0:T(8,128)(2,1)S(1)}, bf16[4,2,16,4096]{3,2,1,0:T(8,128)(2,1)S(1)}, u32[]{:S(2)}, u32[]{:S(2)}) collective-permute-start(bf16[4,2,16,4096]{3,2,1,0:T(8,128)(2,1)S(1)} %slice_bitcast_fusion.1), channel_id=1, source_target_pairs={{0,1},{1,0},{2,3},{3,2},{4,5},{5,4},{6,7},{7,6},{8,9},{9,8},{10,11... | collective-permute-start | bytes 3145736 | tf_op jit(solution)/shard_map/ppermute | solution.py:345
  138.0 11.5 %collective-permute-start.10 = (bf16[4,2,16,4096]{3,2,1,0:T(8,128)(2,1)}, bf16[4,2,16,4096]{3,2,1,0:T(8,128)(2,1)}, u32[]{:S(2)}, u32[]{:S(2)}) collective-permute-start(bf16[4,2,16,4096]{3,2,1,0:T(8,128)(2,1)} %slice_bitcast_fusion), channel_id=1, source_target_pairs={{0,1},{1,0},{2,3},{3,2},{4,5},{5,4},{6,7},{7,6},{8,9},{9,8},{10,11... | collective-permute-start | bytes 3145736 | tf_op jit(solution)/shard_map/ppermute | solution.py:345
  145.3 19.4 %all-to-all-start.2 = ((bf16[8,1,16,4096]{3,2,1,0:T(8,128)(2,1)}), bf16[8,1,16,4096]{3,2,1,0:T(8,128)(2,1)}, u32[]{:S(2)}, u32[]{:S(2)}) async-start(bf16[8,1,16,4096]{3,2,1,0:T(8,128)(2,1)} %bitcast.27), calls=%async_computation.2 | async-start | bytes 2097152 | tf_op jit(solution)/shard_map/all_to_all | solution.py:384
  167.8 14.2 %copy-start.28 = (bf16[128,16]{1,0:T(8,128)(2,1)S(1)}, bf16[128,16]{1,0:T(8,128)(2,1)}, u32[]{:S(2)}) copy-start(bf16[128,16]{1,0:T(8,128)(2,1)} %copy-done.27) | copy-start | bytes 12292
  171.7 22.7 %all-to-all-start.5 = ((bf16[8,16,608]{2,1,0:T(8,128)(2,1)}), bf16[8,16,608]{2,1,0:T(8,128)(2,1)}, u32[]{:S(2)}, u32[]{:S(2)}) async-start(bf16[8,16,608]{2,1,0:T(8,128)(2,1)} %get-tuple-element.55), calls=%async_computation.5 | async-start | bytes 327680 | tf_op jit(solution)/shard_map/all_to_all | solution.py:394
  182.0 2.8 %copy-start.4 = (bf16[8,768,512]{2,1,0:T(8,128)(2,1)S(1)}, bf16[8,768,512]{2,1,0:T(8,128)(2,1)}, u32[]{:S(2)}) copy-start(bf16[8,768,512]{2,1,0:T(8,128)(2,1)} %all-gather.2.cloned.1.call-done.weight) | copy-start | bytes 18874372
  196.0 13.0 %all-to-all-start.6 = ((bf16[8,16,608]{2,1,0:T(8,128)(2,1)}), bf16[8,16,608]{2,1,0:T(8,128)(2,1)S(1)}, u32[]{:S(2)}, u32[]{:S(2)}) async-start(bf16[8,16,608]{2,1,0:T(8,128)(2,1)} %spread.1), calls=%async_computation.6 | async-start | bytes 327680 | tf_op jit(solution)/shard_map/all_to_all | solution.py:397
  200.4 2.8 %copy-start.5 = (bf16[8,768,512]{2,1,0:T(8,128)(2,1)S(1)}, bf16[8,768,512]{2,1,0:T(8,128)(2,1)}, u32[]{:S(2)}) copy-start(bf16[8,768,512]{2,1,0:T(8,128)(2,1)} %all-gather.2.cloned.1.call-done.weight) | copy-start | bytes 18874372
  204.5 10.9 %copy-start.30 = (bf16[128,16]{1,0:T(8,128)(2,1)S(1)}, bf16[128,16]{1,0:T(8,128)(2,1)}, u32[]{:S(2)}) copy-start(bf16[128,16]{1,0:T(8,128)(2,1)} %copy-done.29) | copy-start | bytes 12292
  211.3 17.3 %all-to-all-start.7 = ((bf16[8,16,608]{2,1,0:T(8,128)(2,1)}), bf16[8,16,608]{2,1,0:T(8,128)(2,1)S(1)}, u32[]{:S(2)}, u32[]{:S(2)}) async-start(bf16[8,16,608]{2,1,0:T(8,128)(2,1)} %turn.1), calls=%async_computation.7 | async-start | bytes 327680 | tf_op jit(solution)/shard_map/all_to_all | solution.py:400
  215.4 2.8 %copy-start.6 = (bf16[8,768,512]{2,1,0:T(8,128)(2,1)S(1)}, bf16[8,768,512]{2,1,0:T(8,128)(2,1)}, u32[]{:S(2)}) copy-start(bf16[8,768,512]{2,1,0:T(8,128)(2,1)} %all-gather.2.cloned.1.call-done.weight) | copy-start | bytes 18874372
  (22 other events, 20.7 us)
Sparse Core Ops, SparseCore 0:
  27.5 82.1 all-gather.1

commit v3 on v2

v3 whole, which is shorter than its diff:
```python
import functools

import jax
import jax.numpy as jnp
from jax import lax
from jax.experimental import pallas as pl
from jax.experimental.pallas import tpu as pltpu
from jax.sharding import Mesh, PartitionSpec as P

ADAPTER_SCALE = 2.0
COST_BUILD, COST_GRADS, COST_BACK = 8, 3, 10
GROUPS, NX, NY, NC = 8, 4, 8, 2
COLS = NX * NC
CAP = 16
META = 128
WHOLE, CROSS, SPLIT = 0, 1, 2
PARTS = {WHOLE: 1, CROSS: 2, SPLIT: COLS}
MIB = 1024 * 1024
VM = pl.BlockSpec(memory_space=pltpu.VMEM)
ANY = pl.BlockSpec(memory_space=pl.ANY)
HBM = pl.BlockSpec(memory_space=pltpu.HBM)
SM = pl.BlockSpec(memory_space=pltpu.SMEM)
NT = (((1,), (1,)), ((), ()))
TN = (((0,), (0,)), ((), ()))
NN = (((1,), (0,)), ((), ()))


def dot(a, b, dims):
    return lax.dot_general(a, b, dims, preferred_element_type=jnp.float32)


def params(mib):
    return pltpu.CompilerParams(vmem_limit_bytes=mib * MIB)


def cost(us):
    return pl.CostEstimate(flops=int(us * 1.0e9), bytes_accessed=int(us * 3.0e6), transcendentals=0)


def far_memory(array):
    return pltpu.with_memory_space_constraint(array, pltpu.HBM)


def copies(pairs, sems, first=0):
    started = [pltpu.make_async_copy(src, dst, sems.at[first + i]) for i, (src, dst) in enumerate(pairs)]
    for copy in started:
        copy.start()
    return started


def pack_kernel(cot, weight, ids, slots, out, w_in, ids_in, slots_in, sems):
    width = cot.shape[1]
    coming = copies([(weight, w_in), (ids, ids_in), (slots, slots_in), (cot, out.at[:, pl.ds(0, width)])], sems)
    out[48:, width:] = jnp.zeros((out.shape[0] - 48, META), jnp.bfloat16)
    for copy in coming[:3]:
        copy.wait()
    w = w_in[...]
    hi = w.astype(jnp.bfloat16)
    rest = w - hi.astype(jnp.float32)
    mid = rest.astype(jnp.bfloat16)
    low = (rest - mid.astype(jnp.float32)).astype(jnp.bfloat16)
    rows = [
        ids_in[...].astype(jnp.float32),
        slots_in[...].astype(jnp.float32),
        hi.astype(jnp.float32),
        mid.astype(jnp.float32),
        low.astype(jnp.float32),
        jnp.zeros(low.shape, jnp.float32),
    ]
    out[0:48, width:] = jnp.concatenate(rows, axis=0).astype(jnp.bfloat16)
    coming[3].wait()


def pack(cot, weight, ids, slots):
    return pl.pallas_call(
        pack_kernel,
        name="pack",
        out_shape=jax.ShapeDtypeStruct((cot.shape[0], cot.shape[1] + META), jnp.bfloat16),
        in_specs=[HBM] * 4,
        out_specs=VM,
        scratch_shapes=[pltpu.VMEM(a.shape, a.dtype) for a in (weight, ids, slots)]
        + [pltpu.SemaphoreType.DMA((4,))],
        compiler_params=params(12),
        cost_estimate=cost(2),
    )(*(far_memory(a) for a in (cot, weight, ids, slots)))


def gate(values, after):
    return list(lax.optimization_barrier((tuple(values), tuple(after)))[0])


def build_kernel(kind, me, *refs):
    made, sems = refs[-2:]
    count = made.shape[1]
    blocks, outs = refs[:count], refs[count:-2]
    going = []
    for b in range(count):
        block = blocks[b]
        width = block.shape[1] - META
        routes = block[0:48, width:].astype(jnp.float32)
        expert = routes[0:8].astype(jnp.int32)
        slot = routes[8:16].astype(jnp.int32)
        weight = routes[16:24] + routes[24:32] + routes[32:40]
        x, c = expert // (NY * NC), expert % NC
        if kind == SPLIT:
            x = (x - me[0] + NX) % NX
        if kind != WHOLE:
            c = (c + me[2]) % NC
        here = ((expert // NC) % NY == me[1]) & (slot < CAP)
        code = jnp.where(here, (x * NC + c) * CAP + slot, -1)
        row = lax.broadcasted_iota(jnp.int32, (COLS * CAP, code.shape[1]), 0)
        pick = jnp.zeros(row.shape, jnp.float32)
        scale = jnp.zeros(row.shape, jnp.float32)
        for k in range(code.shape[0]):
            match = row == code[k : k + 1]
            pick = jnp.where(match, 1.0, pick)
            scale = jnp.where(match, weight[k : k + 1], scale)
        scale = jnp.sum(scale, axis=1, keepdims=True)
        pick = pick.astype(jnp.bfloat16)
        step = width // 4
        for at in range(0, width, step):
            rows = (scale * dot(pick, block[:, at : at + step], NN)).astype(jnp.bfloat16)
            for d in range(COLS):
                made[d, b, :, at : at + step] = rows[d * CAP : (d + 1) * CAP]
            if kind != SPLIT:
                cut = (slice(None), b, slice(None), pl.ds(at, step))
                going += copies([(made.at[cut], outs[0].at[cut])], sems, len(going))
    if kind == SPLIT:
        going = copies([(made.at[d], outs[d]) for d in range(COLS)], sems)
    for copy in going:
        copy.wait()


def build(n, me, blocks, kind):
    width = blocks[0].shape[1] - META
    shape = (len(blocks), CAP, width)
    outs = [pltpu.HBM(shape, jnp.bfloat16)] * COLS if kind == SPLIT else [pltpu.HBM((COLS,) + shape, jnp.bfloat16)]
    return pl.pallas_call(
        functools.partial(build_kernel, kind),
        name=f"build_{n}",
        out_shape=outs,
        in_specs=[SM] + [VM] * len(blocks),
        out_specs=[HBM] * len(outs),
        scratch_shapes=[pltpu.VMEM((COLS,) + shape, jnp.bfloat16), pltpu.SemaphoreType.DMA((8,))],
        compiler_params=params(8),
        cost_estimate=cost(COST_BUILD),
    )(me, *blocks)


def places(me, chunk):
    kind, offsets = chunk
    order = [(x, c) for x in range(NX) for c in range(NC)]
    if kind == CROSS:
        order = [(x, (me[2] + dc) % NC) for dc in range(NC) for x in range(NX)]
    if kind == SPLIT:
        order = [((me[0] - x + NX) % NX, (me[2] + c) % NC) for x, c in order]
    return [(x * NY + (me[1] + offset + NY) % NY) * NC + c for x, c in order for offset in offsets]


def fetches(chunk, parts, rows):
    kind, offsets = chunk
    if kind == WHOLE:
        return [(parts[0], rows)]
    if kind == CROSS:
        return [
            (parts[0].at[pl.ds(x * NC, 1)], rows.at[pl.ds(x, 1)]) for x in range(NX)
        ] + [(parts[1], rows.at[pl.ds(NX, NX)])]
    return [(parts[d], rows.at[d]) for d in range(COLS)]


def grads_kernel(chunk, first, last, waits, *refs):
    me, refs = refs[0], refs[1 + waits :]
    count = PARTS[chunk[0]]
    parts, (hidden, amap, bmap), refs = refs[:count], refs[count : count + 3], refs[count + 3 :]
    old_a, old_b = (None, None) if first else refs[:2]
    rest = refs if first else refs[2:]
    hid, tok, a_in, b_in, sems = rest[-5:]
    outs = rest[:-5]
    pairs = [(amap, a_in), (bmap, b_in)]
    pairs += [(hidden.at[src], hid.at[pl.ds(i * CAP, CAP)]) for i, src in enumerate(places(me, chunk))]
    small = len(pairs)
    coming = copies(pairs + fetches(chunk, parts, tok), sems)
    for copy in coming[:small]:
        copy.wait()
    rows, width = hid.shape[0], tok.shape[-1]
    z = dot(hid[...], a_in[...], NT).astype(jnp.bfloat16)
    for copy in coming[small:]:
        copy.wait()
    tokens = tok[...].reshape(rows, width)
    rb = (ADAPTER_SCALE * dot(tokens, b_in[...], NT)).astype(jnp.bfloat16)
    outs[0][...] = rb
    grad_b = ADAPTER_SCALE * dot(z, tokens, TN)
    grad_a = dot(rb, hid[...], TN)
    if old_a is not None:
        grad_b = grad_b + old_b[...]
        grad_a = grad_a + old_a[...]
    if not last:
        outs[1][...] = grad_a
        outs[2][...] = grad_b
    else:
        sent = outs[1]
        wide_b = width // GROUPS
        wide_a = hid.shape[1] // GROUPS
        for z_to in range(GROUPS):
            sent[z_to, :, :wide_b] = grad_b[:, z_to * wide_b : (z_to + 1) * wide_b].astype(jnp.bfloat16)
            sent[z_to, :, wide_b : wide_b + wide_a] = grad_a[:, z_to * wide_a : (z_to + 1) * wide_a].astype(
                jnp.bfloat16
            )


def grads(n, me, parts, hidden, amap, bmap, old, chunk, last, after=()):
    pieces = COLS * len(chunk[1])
    rows = pieces * CAP
    rank, width = bmap.shape
    hidden_width = amap.shape[1]
    shapes = [pltpu.VMEM((rows, rank), jnp.bfloat16)]
    if last:
        piece = width // GROUPS + hidden_width // GROUPS
        shapes += [pltpu.HBM((GROUPS, rank, piece), jnp.bfloat16)]
    else:
        shapes += [
            pltpu.VMEM((rank, hidden_width), jnp.float32),
            pltpu.VMEM((rank, width), jnp.float32),
        ]
    loaded = [far_memory(array) for array in (*parts, hidden, amap, bmap)]
    return pl.pallas_call(
        functools.partial(grads_kernel, chunk, not old, last, len(after)),
        name=f"grads_{n}",
        out_shape=shapes,
        in_specs=[SM] + [ANY] * len(after) + [HBM] * len(loaded) + [VM] * len(old),
        out_specs=[VM] * len(shapes),
        scratch_shapes=[
            pltpu.VMEM((rows, hidden_width), jnp.bfloat16),
            pltpu.VMEM((COLS, len(chunk[1]), CAP, width), jnp.bfloat16),
            pltpu.VMEM(amap.shape, jnp.bfloat16),
            pltpu.VMEM(bmap.shape, jnp.bfloat16),
            pltpu.SemaphoreType.DMA((pieces + 2 + COLS,)),
        ],
        compiler_params=params(10),
        cost_estimate=cost(COST_GRADS),
    )(me, *after, *loaded, *old)


def back_kernel(chunks, more, me, *refs):
    counts = [PARTS[chunk[0]] for chunk in chunks]
    weight, refs = refs[:GROUPS], refs[GROUPS:]
    flat, refs = refs[: sum(counts)], refs[sum(counts) :]
    rbs, amap, refs = refs[: len(chunks)], refs[len(chunks)], refs[len(chunks) + 1 + more :]
    out, wide_w, tok, rb, done, sems, sems_out = refs
    pairs = []
    begin = 0
    for n, chunk in enumerate(chunks):
        pieces = len(chunk[1]) * COLS
        rows = tok.at[pl.ds(begin, pieces)]
        at = sum(counts[:n])
        pairs += fetches(chunk, flat[at : at + counts[n]], rows.reshape(COLS, len(chunk[1]), CAP, tok.shape[-1]))
        rb[begin * CAP : (begin + pieces) * CAP] = rbs[n][...]
        begin += pieces
    coming = copies(pairs + [(weight[d], wide_w.at[d]) for d in range(GROUPS)], sems)
    total = dot(rb[...], amap[...], NN)
    for copy in coming[: len(pairs)]:
        copy.wait()
    rows, wide = rb.shape[0], wide_w.shape[-1]
    for d in range(GROUPS):
        coming[len(pairs) + d].wait()
        z = (me[3] - d + GROUPS) % GROUPS
        g = tok[:, :, pl.ds(pl.multiple_of(z * wide, wide), wide)].reshape(rows, wide)
        total = total + dot(g, wide_w[d], NT)
    done[...] = total.astype(jnp.bfloat16).reshape(done.shape)
    where = [src for chunk in chunks for src in places(me, chunk)]
    for copy in copies([(done.at[i], out.at[src]) for i, src in enumerate(where)], sems_out):
        copy.wait()


def back(n, me, weight, amap, work, chunks, old=()):
    flat = [part for parts, rb in work for part in parts]
    rbs = [rb for parts, rb in work]
    hidden_width = amap.shape[1]
    width = flat[0].shape[-1]
    pieces = sum(COLS * len(chunk[1]) for chunk in chunks)
    return pl.pallas_call(
        functools.partial(back_kernel, chunks, len(old)),
        name=f"back_{n}",
        out_shape=pltpu.HBM((NX * NY * NC, CAP, hidden_width), jnp.bfloat16),
        in_specs=[SM] + [HBM] * (GROUPS + len(flat)) + [VM] * (len(rbs) + 1) + [HBM] * len(old),
        out_specs=HBM,
        input_output_aliases={2 + GROUPS + len(flat) + len(rbs): 0} if old else {},
        scratch_shapes=[
            pltpu.VMEM((GROUPS,) + weight[0].shape, jnp.bfloat16),
            pltpu.VMEM((pieces, CAP, width), jnp.bfloat16),
            pltpu.VMEM((pieces * CAP, amap.shape[0]), jnp.bfloat16),
            pltpu.VMEM((pieces, CAP, hidden_width), jnp.bfloat16),
            pltpu.SemaphoreType.DMA((GROUPS + 2 * COLS * len(work),)),
            pltpu.SemaphoreType.DMA((pieces,)),
        ],
        compiler_params=params(26),
        cost_estimate=cost(COST_BACK),
    )(me, *(far_memory(array) for array in (*weight, *flat)), *rbs, amap, *old)


def spread_kernel(got, out):
    total = jnp.sum(got[...].astype(jnp.float32), axis=0).astype(jnp.bfloat16)
    for d in range(COLS):
        out[d] = total


def spread(got):
    return pl.pallas_call(
        spread_kernel,
        name="spread",
        out_shape=jax.ShapeDtypeStruct((COLS,) + got.shape[1:], got.dtype),
        in_specs=[VM],
        out_specs=VM,
    )(got)


def turn_kernel(where, got, out):
    for y_to in range(NY):
        out[y_to] = got[where[y_to]]


def turn(where, got):
    return pl.pallas_call(
        turn_kernel,
        name="turn",
        out_shape=jax.ShapeDtypeStruct((NY,) + got.shape[1:], got.dtype),
        in_specs=[SM, VM],
        out_specs=VM,
    )(where, got)


def take_kernel(wide_b, where, got, out_a, out_b):
    row = got[where[NY]]
    out_b[...] = row[:, :wide_b]
    out_a[...] = row[:, wide_b:]


def take(where, got, wide_a, wide_b):
    rank = got.shape[1]
    return pl.pallas_call(
        functools.partial(take_kernel, wide_b),
        name="take",
        out_shape=[
            jax.ShapeDtypeStruct((rank, wide_a), got.dtype),
            jax.ShapeDtypeStruct((rank, wide_b), got.dtype),
        ],
        in_specs=[SM, VM],
        out_specs=[VM, VM],
    )(where, got)


def per_device(
    cotangent,
    route_weight,
    expert_ids,
    slot_ids,
    hidden_saved,
    down_weight,
    adapter_a,
    adapter_out_maps,
    rollout_owner,
):
    width = cotangent.shape[1]
    hidden_width = adapter_a.shape[2]
    x = lax.axis_index("x").astype(jnp.int32)
    y = lax.axis_index("y").astype(jnp.int32)
    c = lax.axis_index("core").astype(jnp.int32)
    me = jnp.stack([x, y, c, lax.axis_index("dp").astype(jnp.int32)])
    up = [(i, (i + 1) % NY) for i in range(NY)]
    down = [(i, (i - 1) % NY) for i in range(NY)]
    row = ("x", "core")
    experts = jnp.arange(NX * NY * NC, dtype=jnp.int32)
    takers = (x * NY + jnp.append(jnp.arange(NY, dtype=jnp.int32), y)) * NC + c
    taken = jnp.sum(jnp.where(rollout_owner[None, :] == takers[:, None], experts[None, :], 0), axis=1)
    beside = taken // (NY * NC) * NC + taken % NC
    where = jnp.where(jnp.arange(NY + 1) < NY, beside, taken // NC % NY)

    def steps(dx, dc):
        return [(i * NC + j, (i + dx) % NX * NC + (j + dc) % NC) for i in range(NX) for j in range(NC)]

    def send(built, kind):
        if kind == WHOLE:
            return [lax.all_to_all(built[0], row, 0, 0, tiled=True)]
        if kind == CROSS:
            return [lax.all_to_all(built[0], "x", 0, 0, tiled=True)]
        return [built[0]] + [lax.ppermute(built[d], row, steps(d // NC, d % NC)) for d in range(1, COLS)]

    def cross(parts):
        return parts + [lax.ppermute(parts[0][1::NC], "core", [(0, 1), (1, 0)])]

    own = pack(cotangent, route_weight.T, expert_ids.T, slot_ids.T)
    weight = [down_weight[0]] + [None] * (GROUPS - 1)
    rise = [(i, (i + 1) % GROUPS) for i in range(GROUPS)]
    fall = [(i, (i - 1) % GROUPS) for i in range(GROUPS)]
    hidden = hidden_saved.reshape(NX * NY * NC, CAP, hidden_width)
    amap = adapter_a[0]
    bmap = adapter_out_maps[0]

    kinds = [WHOLE, CROSS, CROSS, WHOLE, SPLIT]
    offsets = [(0,)] + [(-d, d) for d in range(1, NY // 2)] + [(NY // 2,)]
    last = len(offsets) - 1
    chunks = []
    old = ()
    work = []
    whole = []

    def settle(n, after=()):
        nonlocal old
        chunks.append((kinds[n], offsets[n]))
        rb, *old = grads(n, me, whole[n], hidden, amap, bmap, old, chunks[-1], len(chunks) == last + 1, after)
        work.append((whole[n], rb))
        return rb

    either = [(i * NC, (i + 1) % NY * NC) for i in range(NY)] + [(i * NC + 1, (i - 1) % NY * NC + 1) for i in range(NY)]
    held = [own]
    pending = []
    for w in range(1, last + 1):
        low, high = held[0], held[-1]
        if w < last:
            ahead = [lax.ppermute(low, "y", up), lax.ppermute(high, "y", down)]
        else:
            ahead = [lax.ppermute(jnp.where(c == 0, low, high), ("y", "core"), either)]
        done = []
        if w >= 3:
            whole[w - 3] = gate(whole[w - 3], whole[w - 2][:1])
            done.append(settle(w - 3))
        kind = kinds[w - 1]
        built = build(w - 1, me, held, kind)
        parts = send(built, kind)
        whole.append(cross(parts) if kind == CROSS else parts)
        done += pending
        pending = []
        if w != 2:
            step = max(1, w - 1)
            after = built if w == 1 else whole[w - 2]
            rising, falling = gate([weight[step - 1], weight[(1 - step) % GROUPS]], after[:1])
            weight[step] = lax.ppermute(rising, "dp", rise)
            weight[-step] = lax.ppermute(falling, "dp", fall)
            if w < last:
                pending = [weight[step], weight[-step]]
        held = [gate([block], done + [built[0], where])[0] for block in ahead]
    weight[last] = lax.ppermute(weight[last - 1], "dp", rise)
    built = build(last, me, held, kinds[last])
    whole.append(send(built, kinds[last]))
    whole[2] = gate(whole[2], [built[0]])
    settle(2)
    rb = settle(4)
    whole[3] = gate(whole[3], [rb])
    settle(3)

    def turn_back(n, begin, end, filled):
        return back(n, me, weight, amap, work[begin:end], chunks[begin:end], filled)

    got = lax.all_to_all(old[0], "dp", 0, 0, tiled=True)
    filled = turn_back(0, 0, 2, [])
    got, filled = gate([got, filled], [])
    row_items = lax.all_to_all(spread(got), row, 0, 0, tiled=True)
    filled = turn_back(1, 2, 3, [filled])
    row_items, filled = gate([row_items, filled], [])
    column_items = lax.all_to_all(turn(where, row_items), "y", 0, 0, tiled=True)
    grad_hidden = turn_back(2, 3, 5, [filled])
    column_items, grad_hidden = gate([column_items, grad_hidden], [])
    out_a, out_b = take(where, column_items, hidden_width // GROUPS, width // GROUPS)
    return (
        grad_hidden.reshape(1, 1, NX * NY * NC * CAP, hidden_width),
        out_a[None],
        out_b[None],
    )


def solution(mesh):
    parts = Mesh(mesh.devices.reshape(GROUPS, NX, NY, NC), ("dp", "x", "y", "core"))
    every = ("dp", "x", "y", "core")
    expert = ("x", "y", "core")
    return jax.shard_map(
        per_device,
        mesh=parts,
        in_specs=(
            P(every, None),
            P(every, None),
            P(every, None),
            P(every, None),
            P("dp", expert, None, None),
            P(expert, None, "dp"),
            P(expert, None, None),
            P(expert, None, None),
            P(),
        ),
        out_specs=(P("dp", expert, None, None), P(expert, None, "dp"), P(expert, None, "dp")),
        check_vma=False,
    )
```

time: 240 us -> 219 us (0.912)
  starting transfers between devices: 86 us -> 125 us
  local copies, waits for them, and re-layouts: 36.1 us -> 7.83 us
  waiting for transfers between devices: 41.2 us -> 16.8 us
  between operations: 14.5 us -> 1.3 us
  Pallas kernels: 56.6 us -> 64.5 us
    ppermute x4 -> x16, starting transfers between devices: 23.7 us -> 60.9 us  [the longest x3 22.4 us: per_device(): weight[-step] = lax.ppermute(falling, 'dp', fall)]
    unnamed x68 -> x34, local copies, waits for them, and re-layouts: 30.4 us -> 4.25 us
    ppermute x6, waiting for transfers between devices: 26.7 us -> 10.5 us  [per_device(): ahead = [lax.ppermute(low, 'y', up), lax.ppermute(high, 'y', down)]]
    all_to_all x5 -> x4, waiting for transfers between devices: 11.9 us -> 1.68 us  [the longest x2 1.67 us: send(): return [lax.all_to_all(built[0], 'x', 0, 0, tiled=True)]]
    pallas_call x13, Pallas kernels: 51.7 us -> 57.4 us  [the longest x3 24.1 us: back(): pl.pallas_call(functools.partial(back_kernel, chunks, len(old)), name=f'b...]
    squeeze x4 -> x0, local copies, waits for them, and re-layouts: 5.62 us -> none  [cross(): return (straight, lax.ppermute(straight[:, 1], 'core', [(0, 1), (1, 0)]))]
    all_to_all x1, starting transfers between devices: 10.2 us -> 6.53 us  [per_device(): got = lax.all_to_all(old[0], 'dp', 0, 0, tiled=True)]
    slice x0 -> x2, local copies, waits for them, and re-layouts: none -> 3.58 us  [cross(): return parts + [lax.ppermute(parts[0][1::NC], 'core', [(0, 1), (1, 0)])]]
  transfers between devices with their start and end apart: 20 -> 30, of which waited for: 9 -> 6; matrix products, arithmetic and copies ran while one was open for 4% -> 3% of each run, Pallas kernels for 22% -> 26%
where the time goes in v3:
time: 219 us; the launch traced here: 217 us
  starting transfers between devices  125 us (57%)
  Pallas kernels  64.5 us (29%)
  waiting for transfers between devices  16.8 us (8%)
  local copies, waits for them, and re-layouts  7.83 us (4%)
    pallas_call x3, Pallas kernels, back(): pl.pallas_call(functools.partial(back_kernel, chunks, len(old)), name=f'b...  24.1 us
    ppermute x3, starting transfers between devices, per_device(): weight[-step] = lax.ppermute(falling, 'dp', fall)  22.4 us
    ppermute x7, starting transfers between devices, send(): lax.ppermute(built[d], row, steps(d // NC, d % NC))  21.7 us
    ppermute x6, starting transfers between devices, per_device(): ahead = [lax.ppermute(low, 'y', up), lax.ppermute(high, 'y', down)]  20.8 us
    pallas_call x5, Pallas kernels, grads(): pl.pallas_call(functools.partial(grads_kernel, chunk, not old, last, len(...  18.4 us
    all_to_all x2, starting transfers between devices, send(): return [lax.all_to_all(built[0], row, 0, 0, tiled=True)]  15.3 us
    pallas_call x5, Pallas kernels, build(): pl.pallas_call(functools.partial(build_kernel, kind), name=f'build_{n}',...  14.9 us
    ppermute x6, waiting for transfers between devices, per_device(): ahead = [lax.ppermute(low, 'y', up), lax.ppermute(high, 'y', down)]  10.5 us
  transfers between devices with their start and end apart: 30, of which 6 were waited for; matrix products, arithmetic and copies ran while one was open for 3% of the time, Pallas kernels for 26%

profile of v3, /device:TPU:1, one launch (start us, length us, event | category | flops | bytes accessed | tf_op | source)
XLA Modules:
  0.0 217.0 jit_solution(14742916580181058990)
XLA Ops:
  2.9 4.0 %collective-permute-start = (bf16[128,4224]{1,0:T(8,128)(2,1)}, bf16[128,4224]{1,0:T(8,128)(2,1)S(1)}, u32[]{:S(2)}, u32[]{:S(2)}) collective-permute-start(bf16[128,4224]{1,0:T(8,128)(2,1)} %pack.1.refs_0_), channel_id=1, source_target_pairs={{0,2},{2,4},{4,6},{6,8},{8,10},{10,12},{12,14},{14,0},{1,3},{3,5},... | collective-permute-start | bytes 3244040 | tf_op jit(solution)/shard_map/ppermute | solution.py:420
  7.0 3.8 %collective-permute-start.4 = (bf16[128,4224]{1,0:T(8,128)(2,1)}, bf16[128,4224]{1,0:T(8,128)(2,1)S(1)}, u32[]{:S(2)}, u32[]{:S(2)}) collective-permute-start(bf16[128,4224]{1,0:T(8,128)(2,1)} %pack.1.refs_0_), channel_id=1, source_target_pairs={{0,14},{2,0},{4,2},{6,4},{8,6},{10,8},{12,10},{14,12},{1,15},{3,1}... | collective-permute-start | bytes 3244040 | tf_op jit(solution)/shard_map/ppermute | solution.py:420
  13.5 10.2 %all-to-all-start = ((bf16[8,1,16,4096]{3,2,1,0:T(8,128)(2,1)}), bf16[8,1,16,4096]{3,2,1,0:T(8,128)(2,1)}, u32[]{:S(2)}, u32[]{:S(2)}) async-start(bf16[8,1,16,4096]{3,2,1,0:T(8,128)(2,1)} %build_0.1), calls=%async_computation | async-start | bytes 2097152 | tf_op jit(solution)/shard_map/all_to_all | solution.py:383
  25.6 5.7 %collective-permute-start.3 = (bf16[768,512]{1,0:T(8,128)(2,1)}, bf16[768,512]{1,0:T(8,128)(2,1)}, u32[]{:S(2)}, u32[]{:S(2)}) collective-permute-start(bf16[768,512]{1,0:T(8,128)(2,1)} %bitcast.7.refs_0_), channel_id=1, source_target_pairs={{0,448},{64,0},{128,64},{192,128},{256,192},{320,256},{384,320},{4... | collective-permute-start | bytes 2359304 | tf_op jit(solution)/shard_map/ppermute | solution.py:438
  34.1 4.6 %collective-permute-start.6 = (bf16[128,4224]{1,0:T(8,128)(2,1)S(1)}, bf16[128,4224]{1,0:T(8,128)(2,1)}, u32[]{:S(2)}, u32[]{:S(2)}) collective-permute-start(bf16[128,4224]{1,0:T(8,128)(2,1)S(1)} %collective-permute-done.4.refs_1_), channel_id=1, source_target_pairs={{0,14},{2,0},{4,2},{6,4},{8,6},{10,8},{12,10},{14,12},{1,15},{3,1}... | collective-permute-start | bytes 3244040 | tf_op jit(solution)/shard_map/ppermute | solution.py:420
  38.7 3.2 %build_1.1 = bf16[8,2,16,4096]{3,2,1,0:T(8,128)(2,1)} custom-call(s32[4]{0:T(128)S(1)} %pad_add_fusion.me.refs_0_, bf16[128,4224]{1,0:T(8,128)(2,1)S(1)} %collective-permute-done.refs_0_, bf16[128,4224]{1,0:T(8,128)(2,1)S(1)} %collective-permute-done.4.refs_1_), custom_call_target="tpu_custom_call" | custom-call | flops 8000000000 | bytes 24000000 | tf_op jit(solution)/shard_map/build_1/pallas_call | solution.py:138
  41.9 4.6 %all-to-all-start.1 = ((bf16[8,2,16,4096]{3,2,1,0:T(8,128)(2,1)}), bf16[8,2,16,4096]{3,2,1,0:T(8,128)(2,1)}, u32[]{:S(2)}, u32[]{:S(2)}) async-start(bf16[8,2,16,4096]{3,2,1,0:T(8,128)(2,1)} %build_1.1), calls=%async_computation.1 | async-start | bytes 4194304 | tf_op jit(solution)/shard_map/all_to_all | solution.py:385
  48.6 10.5 %collective-permute-done.1.refs_0_ = bf16[128,4224]{1,0:T(8,128)(2,1)S(1)} collective-permute-done((bf16[128,4224]{1,0:T(8,128)(2,1)S(1)}, bf16[128,4224]{1,0:T(8,128)(2,1)S(1)}, u32[]{:S(2)}, u32[]{:S(2)}) %collective-permute-start.1) | collective-permute-done | bytes 1081376 | tf_op jit(solution)/shard_map/ppermute | solution.py:420
  61.0 4.6 %collective-permute-start.7 = (bf16[128,4224]{1,0:T(8,128)(2,1)}, bf16[128,4224]{1,0:T(8,128)(2,1)S(1)}, u32[]{:S(2)}, u32[]{:S(2)}) collective-permute-start(bf16[128,4224]{1,0:T(8,128)(2,1)} %collective-permute-done.6.refs_1_), channel_id=1, source_target_pairs={{0,14},{2,0},{4,2},{6,4},{8,6},{10,8},{12,10},{14,12},{1,15},{3,1}... | collective-permute-start | bytes 3244040 | tf_op jit(solution)/shard_map/ppermute | solution.py:420
  65.6 3.9 %build_2.1 = bf16[8,2,16,4096]{3,2,1,0:T(8,128)(2,1)} custom-call(s32[4]{0:T(128)S(1)} %pad_add_fusion.me.refs_0_, bf16[128,4224]{1,0:T(8,128)(2,1)S(1)} %collective-permute-done.1.refs_0_, bf16[128,4224]{1,0:T(8,128)(2,1)} %collective-permute-done.6.refs_1_), custom_call_target="tpu_custom_call" | custom-call | flops 8000000000 | bytes 24000000 | tf_op jit(solution)/shard_map/build_2/pallas_call | solution.py:138
  71.2 4.4 %all-to-all-start.3 = ((bf16[8,2,16,4096]{3,2,1,0:T(8,128)(2,1)}), bf16[8,2,16,4096]{3,2,1,0:T(8,128)(2,1)}, u32[]{:S(2)}, u32[]{:S(2)}) async-start(bf16[8,2,16,4096]{3,2,1,0:T(8,128)(2,1)} %build_2.1), calls=%async_computation.3 | async-start | bytes 4194304 | tf_op jit(solution)/shard_map/all_to_all | solution.py:385
  78.0 4.7 %collective-permute-start.9 = (bf16[4,2,16,4096]{3,2,1,0:T(8,128)(2,1)}, bf16[4,2,16,4096]{3,2,1,0:T(8,128)(2,1)}, u32[]{:S(2)}, u32[]{:S(2)}) collective-permute-start(bf16[4,2,16,4096]{3,2,1,0:T(8,128)(2,1)} %slice.6), channel_id=1, source_target_pairs={{0,1},{1,0},{2,3},{3,2},{4,5},{5,4},{6,7},{7,6},{8,9},{9,8},{10,11... | collective-permute-start | bytes 3145736 | tf_op jit(solution)/shard_map/ppermute | solution.py:389
  82.7 4.2 %collective-permute-start.10 = (bf16[768,512]{1,0:T(8,128)(2,1)}, bf16[768,512]{1,0:T(8,128)(2,1)}, u32[]{:S(2)}, u32[]{:S(2)}) collective-permute-start(bf16[768,512]{1,0:T(8,128)(2,1)} %collective-permute-done.2.refs_1_), channel_id=1, source_target_pairs={{0,64},{64,128},{128,192},{192,256},{256,320},{320,384},{384,448},... | collective-permute-start | bytes 2359304 | tf_op jit(solution)/shard_map/ppermute | solution.py:437
  86.9 8.6 %collective-permute-start.11 = (bf16[768,512]{1,0:T(8,128)(2,1)}, bf16[768,512]{1,0:T(8,128)(2,1)}, u32[]{:S(2)}, u32[]{:S(2)}) collective-permute-start(bf16[768,512]{1,0:T(8,128)(2,1)} %collective-permute-done.3.refs_7_), channel_id=1, source_target_pairs={{0,448},{64,0},{128,64},{192,128},{256,192},{320,256},{384,320},{4... | collective-permute-start | bytes 2359304 | tf_op jit(solution)/shard_map/ppermute | solution.py:438
  95.5 2.9 %grads_0.1 = (bf16[128,16]{1,0:T(8,128)(2,1)S(1)}, f32[16,768]{1,0:T(8,128)S(1)}, f32[16,4096]{1,0:T(8,128)S(1)}) custom-call(s32[4]{0:T(128)S(1)} %pad_add_fusion.me.refs_0_, bf16[8,1,16,4096]{3,2,1,0:T(8,128)(2,1)} %all-to-all-done.refs_1_.refs_8_, bf16[64,16,768]{2,1,0:T(8,128)(2,1)} %bitcast.22, bf16[16,768]{1,0:T(8,128)(2,1)} %bitcast.14, ...), custom_call_target="tpu_custom_call" | custom-call | flops 3000000000 | bytes 9000000 | tf_op jit(solution)/shard_map/grads_0/pallas_call | solution.py:226
  102.1 3.2 %build_3.1 = bf16[8,2,16,4096]{3,2,1,0:T(8,128)(2,1)} custom-call(s32[4]{0:T(128)S(1)} %pad_add_fusion.me.refs_0_, bf16[128,4224]{1,0:T(8,128)(2,1)S(1)} %collective-permute-done.5.refs_0_, bf16[128,4224]{1,0:T(8,128)(2,1)S(1)} %collective-permute-done.7.refs_1_), custom_call_target="tpu_custom_call" | custom-call | flops 8000000000 | bytes 24000000 | tf_op jit(solution)/shard_map/build_3/pallas_call | solution.py:138
  105.3 5.0 %all-to-all-start.2 = ((bf16[8,2,16,4096]{3,2,1,0:T(8,128)(2,1)}), bf16[8,2,16,4096]{3,2,1,0:T(8,128)(2,1)}, u32[]{:S(2)}, u32[]{:S(2)}) async-start(bf16[8,2,16,4096]{3,2,1,0:T(8,128)(2,1)} %build_3.1), calls=%async_computation.2 | async-start | bytes 4194304 | tf_op jit(solution)/shard_map/all_to_all | solution.py:383
  115.5 3.9 %grads_1.1 = (bf16[256,16]{1,0:T(8,128)(2,1)S(1)}, f32[16,768]{1,0:T(8,128)S(1)}, f32[16,4096]{1,0:T(8,128)S(1)}) custom-call(s32[4]{0:T(128)S(1)} %pad_add_fusion.me.refs_0_, bf16[8,2,16,4096]{3,2,1,0:T(8,128)(2,1)} %all-to-all-done.1.refs_1_.refs_9_, bf16[4,2,16,4096]{3,2,1,0:T(8,128)(2,1)} %collective-permute-done.9.refs_2_.refs_10_, ...), custom_call_target="tpu_custom_call" | custom-call | flops 3000000000 | bytes 9000000 | tf_op jit(solution)/shard_map/grads_1/pallas_call | solution.py:226
  123.9 3.3 %collective-permute-start.13 = (bf16[1,16,4096]{2,1,0:T(8,128)(2,1)}, bf16[1,16,4096]{2,1,0:T(8,128)(2,1)S(1)}, u32[]{:S(2)}, u32[]{:S(2)}) collective-permute-start(bf16[1,16,4096]{2,1,0:T(8,128)(2,1)} %get-tuple-element.72), channel_id=1, source_target_pairs={{0,16},{1,17},{16,32},{17,33},{32,48},{33,49},{48,0},{49,1},{2,18}... | collective-permute-start | bytes 393224 | tf_op jit(solution)/shard_map/ppermute | solution.py:386
  127.2 3.6 %collective-permute-start.14 = (bf16[1,16,4096]{2,1,0:T(8,128)(2,1)}, bf16[1,16,4096]{2,1,0:T(8,128)(2,1)S(1)}, u32[]{:S(2)}, u32[]{:S(2)}) collective-permute-start(bf16[1,16,4096]{2,1,0:T(8,128)(2,1)} %get-tuple-element.73), channel_id=1, source_target_pairs={{0,17},{1,16},{16,33},{17,32},{32,49},{33,48},{48,1},{49,0},{2,19}... | collective-permute-start | bytes 393224 | tf_op jit(solution)/shard_map/ppermute | solution.py:386
  133.8 8.2 %collective-permute-start.22 = (bf16[768,512]{1,0:T(8,128)(2,1)}, bf16[768,512]{1,0:T(8,128)(2,1)S(1)}, u32[]{:S(2)}, u32[]{:S(2)}) collective-permute-start(bf16[768,512]{1,0:T(8,128)(2,1)} %collective-permute-done.11.refs_6_), channel_id=1, source_target_pairs={{0,448},{64,0},{128,64},{192,128},{256,192},{320,256},{384,320},{4... | collective-permute-start | bytes 2359304 | tf_op jit(solution)/shard_map/ppermute | solution.py:438
  141.9 4.1 %collective-permute-start.16 = (bf16[1,16,4096]{2,1,0:T(8,128)(2,1)}, bf16[1,16,4096]{2,1,0:T(8,128)(2,1)S(1)}, u32[]{:S(2)}, u32[]{:S(2)}) collective-permute-start(bf16[1,16,4096]{2,1,0:T(8,128)(2,1)} %get-tuple-element.75), channel_id=1, source_target_pairs={{0,33},{1,32},{16,49},{17,48},{32,1},{33,0},{48,17},{49,16},{2,35}... | collective-permute-start | bytes 393224 | tf_op jit(solution)/shard_map/ppermute | solution.py:386
  146.1 3.4 %collective-permute-start.17 = (bf16[1,16,4096]{2,1,0:T(8,128)(2,1)}, bf16[1,16,4096]{2,1,0:T(8,128)(2,1)S(1)}, u32[]{:S(2)}, u32[]{:S(2)}) collective-permute-start(bf16[1,16,4096]{2,1,0:T(8,128)(2,1)} %get-tuple-element.76), channel_id=1, source_target_pairs={{0,48},{1,49},{16,0},{17,1},{32,16},{33,17},{48,32},{49,33},{2,50}... | collective-permute-start | bytes 393224 | tf_op jit(solution)/shard_map/ppermute | solution.py:386
  153.7 3.9 %grads_2.1 = (bf16[256,16]{1,0:T(8,128)(2,1)S(1)}, f32[16,768]{1,0:T(8,128)S(1)}, f32[16,4096]{1,0:T(8,128)S(1)}) custom-call(s32[4]{0:T(128)S(1)} %pad_add_fusion.me.refs_0_, bf16[8,2,16,4096]{3,2,1,0:T(8,128)(2,1)} %all-to-all-done.3.refs_1_.refs_8_, bf16[4,2,16,4096]{3,2,1,0:T(8,128)(2,1)} %copy-done.6, bf16[64,16,768]{2,1,0:T(8,128)(2,1)} %bitcast.24, ...), custom_call_target="tpu_custom_call" | custom-call | flops 3000000000 | bytes 9000000 | tf_op jit(solution)/shard_map/grads_2/pallas_call | solution.py:226
  158.4 2.9 %grads_4.1 = (bf16[128,16]{1,0:T(8,128)(2,1)S(1)}, f32[16,768]{1,0:T(8,128)S(1)}, f32[16,4096]{1,0:T(8,128)S(1)}) custom-call(s32[4]{0:T(128)S(1)} %pad_add_fusion.me.refs_0_, bf16[1,16,4096]{2,1,0:T(8,128)(2,1)} %get-tuple-element.70.refs_1_.refs_8_, bf16[1,16,4096]{2,1,0:T(8,128)(2,1)} %copy-done.9, bf16[1,16,4096]{2,1,0:T(8,128)(2,1)} %copy-done.10, ...), custom_call_target="tpu_custom_call" | custom-call | flops 3000000000 | bytes 9000000 | tf_op jit(solution)/shard_map/grads_4/pallas_call | solution.py:226
  161.4 4.7 %grads_3.1 = (bf16[256,16]{1,0:T(8,128)(2,1)S(1)}, bf16[8,16,608]{2,1,0:T(8,128)(2,1)}) custom-call(s32[4]{0:T(128)S(1)} %pad_add_fusion.me.refs_0_, bf16[8,2,16,4096]{3,2,1,0:T(8,128)(2,1)} %all-to-all-done.2.refs_1_.refs_16_, bf16[64,16,768]{2,1,0:T(8,128)(2,1)} %bitcast.26, bf16[16,768]{1,0:T(8,128)(2,1)} %bitcast.18, bf16[16,4096]{1,0:T(8,128)(2,1)} %bitcast.31, ...), custom_call_target="tpu_custom_call" | custom-call | flops 3000000000 | bytes 9000000 | tf_op jit(solution)/shard_map/grads_3/pallas_call | solution.py:226
  166.1 6.5 %all-to-all-start.4 = ((bf16[8,16,608]{2,1,0:T(8,128)(2,1)}), bf16[8,16,608]{2,1,0:T(8,128)(2,1)S(1)}, u32[]{:S(2)}, u32[]{:S(2)}) async-start(bf16[8,16,608]{2,1,0:T(8,128)(2,1)} %get-tuple-element.88), calls=%async_computation.4 | async-start | bytes 327680 | tf_op jit(solution)/shard_map/all_to_all | solution.py:454
  175.6 8.6 %back_0.1.refs_12_ = bf16[64,16,768]{2,1,0:T(8,128)(2,1)} custom-call(s32[4]{0:T(128)S(1)} %pad_add_fusion.me.refs_0_, bf16[768,512]{1,0:T(8,128)(2,1)} %bitcast.7.refs_0_, bf16[768,512]{1,0:T(8,128)(2,1)} %collective-permute-done.2.refs_1_, bf16[768,512]{1,0:T(8,128)(2,1)} %collective-permute-done.10.refs_2_, ...), custom_call_target="tpu_custom_call" | custom-call | flops 10000000000 | bytes 30000000 | tf_op jit(solution)/shard_map/back_0/pallas_call | solution.py:281
  186.6 4.4 %all-to-all-start.5 = ((bf16[8,16,608]{2,1,0:T(8,128)(2,1)}), bf16[8,16,608]{2,1,0:T(8,128)(2,1)S(1)}, u32[]{:S(2)}, u32[]{:S(2)}) async-start(bf16[8,16,608]{2,1,0:T(8,128)(2,1)} %spread.1), calls=%async_computation.5 | async-start | bytes 327680 | tf_op jit(solution)/shard_map/all_to_all | solution.py:457
  190.9 6.7 %back_1.1.refs_20_ = bf16[64,16,768]{2,1,0:T(8,128)(2,1)} custom-call(s32[4]{0:T(128)S(1)} %pad_add_fusion.me.refs_0_, bf16[768,512]{1,0:T(8,128)(2,1)} %bitcast.7.refs_0_, bf16[768,512]{1,0:T(8,128)(2,1)} %collective-permute-done.2.refs_1_, bf16[768,512]{1,0:T(8,128)(2,1)} %collective-permute-done.10.refs_2_, ...), custom_call_target="tpu_custom_call", output_to_operand_aliasing={{}: (13, {})} | custom-call | flops 10000000000 | bytes 30000000 | tf_op jit(solution)/shard_map/back_1/pallas_call | solution.py:281
  199.9 5.7 %all-to-all-start.6 = ((bf16[8,16,608]{2,1,0:T(8,128)(2,1)}), bf16[8,16,608]{2,1,0:T(8,128)(2,1)S(1)}, u32[]{:S(2)}, u32[]{:S(2)}) async-start(bf16[8,16,608]{2,1,0:T(8,128)(2,1)} %turn.1), calls=%async_computation.6 | async-start | bytes 327680 | tf_op jit(solution)/shard_map/all_to_all | solution.py:460
  205.6 8.8 %back_2.1 = bf16[64,16,768]{2,1,0:T(8,128)(2,1)} custom-call(s32[4]{0:T(128)S(1)} %pad_add_fusion.me.refs_0_, bf16[768,512]{1,0:T(8,128)(2,1)} %bitcast.7.refs_0_, bf16[768,512]{1,0:T(8,128)(2,1)} %collective-permute-done.2.refs_1_, bf16[768,512]{1,0:T(8,128)(2,1)} %collective-permute-done.10.refs_2_, ...), custom_call_target="tpu_custom_call", output_to_operand_aliasing={{}: (21, {})} | custom-call | flops 10000000000 | bytes 30000000 | tf_op jit(solution)/shard_map/back_2/pallas_call | solution.py:281
  (87 shorter events, 48.8 us)
Async XLA Ops:
  2.9 29.3 %collective-permute-start = (bf16[128,4224]{1,0:T(8,128)(2,1)}, bf16[128,4224]{1,0:T(8,128)(2,1)S(1)}, u32[]{:S(2)}, u32[]{:S(2)}) collective-permute-start(bf16[128,4224]{1,0:T(8,128)(2,1)} %pack.1.refs_0_), channel_id=1, source_target_pairs={{0,2},{2,4},{4,6},{6,8},{8,10},{10,12},{12,14},{14,0},{1,3},{3,5},... | collective-permute-start | bytes 3244040 | tf_op jit(solution)/shard_map/ppermute | solution.py:420
  7.0 27.2 %collective-permute-start.4 = (bf16[128,4224]{1,0:T(8,128)(2,1)}, bf16[128,4224]{1,0:T(8,128)(2,1)S(1)}, u32[]{:S(2)}, u32[]{:S(2)}) collective-permute-start(bf16[128,4224]{1,0:T(8,128)(2,1)} %pack.1.refs_0_), channel_id=1, source_target_pairs={{0,14},{2,0},{4,2},{6,4},{8,6},{10,8},{12,10},{14,12},{1,15},{3,1}... | collective-permute-start | bytes 3244040 | tf_op jit(solution)/shard_map/ppermute | solution.py:420
  13.5 28.4 %all-to-all-start = ((bf16[8,1,16,4096]{3,2,1,0:T(8,128)(2,1)}), bf16[8,1,16,4096]{3,2,1,0:T(8,128)(2,1)}, u32[]{:S(2)}, u32[]{:S(2)}) async-start(bf16[8,1,16,4096]{3,2,1,0:T(8,128)(2,1)} %build_0.1), calls=%async_computation | async-start | bytes 2097152 | tf_op jit(solution)/shard_map/all_to_all | solution.py:383
  23.7 23.9 %collective-permute-start.2 = (bf16[768,512]{1,0:T(8,128)(2,1)}, bf16[768,512]{1,0:T(8,128)(2,1)}, u32[]{:S(2)}, u32[]{:S(2)}) collective-permute-start(bf16[768,512]{1,0:T(8,128)(2,1)} %bitcast.7.refs_0_), channel_id=1, source_target_pairs={{0,64},{64,128},{128,192},{192,256},{256,320},{320,384},{384,448},... | collective-permute-start | bytes 2359304 | tf_op jit(solution)/shard_map/ppermute | solution.py:437
  25.6 23.0 %collective-permute-start.3 = (bf16[768,512]{1,0:T(8,128)(2,1)}, bf16[768,512]{1,0:T(8,128)(2,1)}, u32[]{:S(2)}, u32[]{:S(2)}) collective-permute-start(bf16[768,512]{1,0:T(8,128)(2,1)} %bitcast.7.refs_0_), channel_id=1, source_target_pairs={{0,448},{64,0},{128,64},{192,128},{256,192},{320,256},{384,320},{4... | collective-permute-start | bytes 2359304 | tf_op jit(solution)/shard_map/ppermute | solution.py:438
  32.2 26.9 %collective-permute-start.1 = (bf16[128,4224]{1,0:T(8,128)(2,1)S(1)}, bf16[128,4224]{1,0:T(8,128)(2,1)S(1)}, u32[]{:S(2)}, u32[]{:S(2)}) collective-permute-start(bf16[128,4224]{1,0:T(8,128)(2,1)S(1)} %collective-permute-done.refs_0_), channel_id=1, source_target_pairs={{0,2},{2,4},{4,6},{6,8},{8,10},{10,12},{12,14},{14,0},{1,3},{3,5},... | collective-permute-start | bytes 3244040 | tf_op jit(solution)/shard_map/ppermute | solution.py:420
  34.1 26.9 %collective-permute-start.6 = (bf16[128,4224]{1,0:T(8,128)(2,1)S(1)}, bf16[128,4224]{1,0:T(8,128)(2,1)}, u32[]{:S(2)}, u32[]{:S(2)}) collective-permute-start(bf16[128,4224]{1,0:T(8,128)(2,1)S(1)} %collective-permute-done.4.refs_1_), channel_id=1, source_target_pairs={{0,14},{2,0},{4,2},{6,4},{8,6},{10,8},{12,10},{14,12},{1,15},{3,1}... | collective-permute-start | bytes 3244040 | tf_op jit(solution)/shard_map/ppermute | solution.py:420
  41.9 29.3 %all-to-all-start.1 = ((bf16[8,2,16,4096]{3,2,1,0:T(8,128)(2,1)}), bf16[8,2,16,4096]{3,2,1,0:T(8,128)(2,1)}, u32[]{:S(2)}, u32[]{:S(2)}) async-start(bf16[8,2,16,4096]{3,2,1,0:T(8,128)(2,1)} %build_1.1), calls=%async_computation.1 | async-start | bytes 4194304 | tf_op jit(solution)/shard_map/all_to_all | solution.py:385
  59.1 40.0 %collective-permute-start.5 = (bf16[128,4224]{1,0:T(8,128)(2,1)S(1)}, bf16[128,4224]{1,0:T(8,128)(2,1)S(1)}, u32[]{:S(2)}, u32[]{:S(2)}) collective-permute-start(bf16[128,4224]{1,0:T(8,128)(2,1)S(1)} %collective-permute-done.1.refs_0_), channel_id=1, source_target_pairs={{0,2},{2,4},{4,6},{6,8},{8,10},{10,12},{12,14},{14,0},{1,3},{3,5},... | collective-permute-start | bytes 3244040 | tf_op jit(solution)/shard_map/ppermute | solution.py:420
  61.0 38.0 %collective-permute-start.7 = (bf16[128,4224]{1,0:T(8,128)(2,1)}, bf16[128,4224]{1,0:T(8,128)(2,1)S(1)}, u32[]{:S(2)}, u32[]{:S(2)}) collective-permute-start(bf16[128,4224]{1,0:T(8,128)(2,1)} %collective-permute-done.6.refs_1_), channel_id=1, source_target_pairs={{0,14},{2,0},{4,2},{6,4},{8,6},{10,8},{12,10},{14,12},{1,15},{3,1}... | collective-permute-start | bytes 3244040 | tf_op jit(solution)/shard_map/ppermute | solution.py:420
  71.2 34.0 %all-to-all-start.3 = ((bf16[8,2,16,4096]{3,2,1,0:T(8,128)(2,1)}), bf16[8,2,16,4096]{3,2,1,0:T(8,128)(2,1)}, u32[]{:S(2)}, u32[]{:S(2)}) async-start(bf16[8,2,16,4096]{3,2,1,0:T(8,128)(2,1)} %build_2.1), calls=%async_computation.3 | async-start | bytes 4194304 | tf_op jit(solution)/shard_map/all_to_all | solution.py:385
  78.0 35.6 %collective-permute-start.9 = (bf16[4,2,16,4096]{3,2,1,0:T(8,128)(2,1)}, bf16[4,2,16,4096]{3,2,1,0:T(8,128)(2,1)}, u32[]{:S(2)}, u32[]{:S(2)}) collective-permute-start(bf16[4,2,16,4096]{3,2,1,0:T(8,128)(2,1)} %slice.6), channel_id=1, source_target_pairs={{0,1},{1,0},{2,3},{3,2},{4,5},{5,4},{6,7},{7,6},{8,9},{9,8},{10,11... | collective-permute-start | bytes 3145736 | tf_op jit(solution)/shard_map/ppermute | solution.py:389
  82.7 30.9 %collective-permute-start.10 = (bf16[768,512]{1,0:T(8,128)(2,1)}, bf16[768,512]{1,0:T(8,128)(2,1)}, u32[]{:S(2)}, u32[]{:S(2)}) collective-permute-start(bf16[768,512]{1,0:T(8,128)(2,1)} %collective-permute-done.2.refs_1_), channel_id=1, source_target_pairs={{0,64},{64,128},{128,192},{192,256},{256,320},{320,384},{384,448},... | collective-permute-start | bytes 2359304 | tf_op jit(solution)/shard_map/ppermute | solution.py:437
  86.9 26.7 %collective-permute-start.11 = (bf16[768,512]{1,0:T(8,128)(2,1)}, bf16[768,512]{1,0:T(8,128)(2,1)}, u32[]{:S(2)}, u32[]{:S(2)}) collective-permute-start(bf16[768,512]{1,0:T(8,128)(2,1)} %collective-permute-done.3.refs_7_), channel_id=1, source_target_pairs={{0,448},{64,0},{128,64},{192,128},{256,192},{320,256},{384,320},{4... | collective-permute-start | bytes 2359304 | tf_op jit(solution)/shard_map/ppermute | solution.py:438
  100.2 19.3 %collective-permute-start.8 = (bf16[128,4224]{1,0:T(8,128)(2,1)}, bf16[128,4224]{1,0:T(8,128)(2,1)S(1)}, u32[]{:S(2)}, u32[]{:S(2)}) collective-permute-start(bf16[128,4224]{1,0:T(8,128)(2,1)} %broadcast_select_fusion), channel_id=1, source_target_pairs={{0,2},{2,4},{4,6},{6,8},{8,10},{10,12},{12,14},{14,0},{1,15},{3,1}... | collective-permute-start | bytes 3244040 | tf_op jit(solution)/shard_map/ppermute | solution.py:422
  105.3 56.1 %all-to-all-start.2 = ((bf16[8,2,16,4096]{3,2,1,0:T(8,128)(2,1)}), bf16[8,2,16,4096]{3,2,1,0:T(8,128)(2,1)}, u32[]{:S(2)}, u32[]{:S(2)}) async-start(bf16[8,2,16,4096]{3,2,1,0:T(8,128)(2,1)} %build_3.1), calls=%async_computation.2 | async-start | bytes 4194304 | tf_op jit(solution)/shard_map/all_to_all | solution.py:383
  111.6 19.2 %collective-permute-start.19 = (bf16[4,2,16,4096]{3,2,1,0:T(8,128)(2,1)S(1)}, bf16[4,2,16,4096]{3,2,1,0:T(8,128)(2,1)S(1)}, u32[]{:S(2)}, u32[]{:S(2)}) collective-permute-start(bf16[4,2,16,4096]{3,2,1,0:T(8,128)(2,1)S(1)} %slice.7), channel_id=1, source_target_pairs={{0,1},{1,0},{2,3},{3,2},{4,5},{5,4},{6,7},{7,6},{8,9},{9,8},{10,11... | collective-permute-start | bytes 3145736 | tf_op jit(solution)/shard_map/ppermute | solution.py:389
  113.6 37.9 %collective-permute-start.20 = (bf16[768,512]{1,0:T(8,128)(2,1)}, bf16[768,512]{1,0:T(8,128)(2,1)}, u32[]{:S(2)}, u32[]{:S(2)}) collective-permute-start(bf16[768,512]{1,0:T(8,128)(2,1)} %collective-permute-done.10.refs_2_), channel_id=1, source_target_pairs={{0,64},{64,128},{128,192},{192,256},{256,320},{320,384},{384,448},... | collective-permute-start | bytes 2359304 | tf_op jit(solution)/shard_map/ppermute | solution.py:437
  121.5 12.2 %collective-permute-start.12 = (bf16[1,16,4096]{2,1,0:T(8,128)(2,1)}, bf16[1,16,4096]{2,1,0:T(8,128)(2,1)S(1)}, u32[]{:S(2)}, u32[]{:S(2)}) collective-permute-start(bf16[1,16,4096]{2,1,0:T(8,128)(2,1)} %get-tuple-element.71), channel_id=1, source_target_pairs={{0,1},{1,0},{16,17},{17,16},{32,33},{33,32},{48,49},{49,48},{2,3},... | collective-permute-start | bytes 393224 | tf_op jit(solution)/shard_map/ppermute | solution.py:386
  123.9 18.0 %collective-permute-start.13 = (bf16[1,16,4096]{2,1,0:T(8,128)(2,1)}, bf16[1,16,4096]{2,1,0:T(8,128)(2,1)S(1)}, u32[]{:S(2)}, u32[]{:S(2)}) collective-permute-start(bf16[1,16,4096]{2,1,0:T(8,128)(2,1)} %get-tuple-element.72), channel_id=1, source_target_pairs={{0,16},{1,17},{16,32},{17,33},{32,48},{33,49},{48,0},{49,1},{2,18}... | collective-permute-start | bytes 393224 | tf_op jit(solution)/shard_map/ppermute | solution.py:386
  127.2 18.8 %collective-permute-start.14 = (bf16[1,16,4096]{2,1,0:T(8,128)(2,1)}, bf16[1,16,4096]{2,1,0:T(8,128)(2,1)S(1)}, u32[]{:S(2)}, u32[]{:S(2)}) collective-permute-start(bf16[1,16,4096]{2,1,0:T(8,128)(2,1)} %get-tuple-element.73), channel_id=1, source_target_pairs={{0,17},{1,16},{16,33},{17,32},{32,49},{33,48},{48,1},{49,0},{2,19}... | collective-permute-start | bytes 393224 | tf_op jit(solution)/shard_map/ppermute | solution.py:386
  130.9 22.8 %copy-start.6 = (bf16[4,2,16,4096]{3,2,1,0:T(8,128)(2,1)}, bf16[4,2,16,4096]{3,2,1,0:T(8,128)(2,1)S(1)}, u32[]{:S(2)}) copy-start(bf16[4,2,16,4096]{3,2,1,0:T(8,128)(2,1)S(1)} %collective-permute-done.19.refs_2_.refs_9_) | copy-start | bytes 3145732
  130.9 18.6 %collective-permute-start.15 = (bf16[1,16,4096]{2,1,0:T(8,128)(2,1)}, bf16[1,16,4096]{2,1,0:T(8,128)(2,1)S(1)}, u32[]{:S(2)}, u32[]{:S(2)}) collective-permute-start(bf16[1,16,4096]{2,1,0:T(8,128)(2,1)} %get-tuple-element.74), channel_id=1, source_target_pairs={{0,32},{1,33},{16,48},{17,49},{32,0},{33,1},{48,16},{49,17},{2,34}... | collective-permute-start | bytes 393224 | tf_op jit(solution)/shard_map/ppermute | solution.py:386
  133.7 23.8 %copy-start.9 = (bf16[1,16,4096]{2,1,0:T(8,128)(2,1)}, bf16[1,16,4096]{2,1,0:T(8,128)(2,1)S(1)}, u32[]{:S(2)}) copy-start(bf16[1,16,4096]{2,1,0:T(8,128)(2,1)S(1)} %collective-permute-done.12.refs_2_.refs_9_) | copy-start | bytes 393220
  133.8 38.9 %collective-permute-start.22 = (bf16[768,512]{1,0:T(8,128)(2,1)}, bf16[768,512]{1,0:T(8,128)(2,1)S(1)}, u32[]{:S(2)}, u32[]{:S(2)}) collective-permute-start(bf16[768,512]{1,0:T(8,128)(2,1)} %collective-permute-done.11.refs_6_), channel_id=1, source_target_pairs={{0,448},{64,0},{128,64},{192,128},{256,192},{320,256},{384,320},{4... | collective-permute-start | bytes 2359304 | tf_op jit(solution)/shard_map/ppermute | solution.py:438
  141.9 15.7 %collective-permute-start.16 = (bf16[1,16,4096]{2,1,0:T(8,128)(2,1)}, bf16[1,16,4096]{2,1,0:T(8,128)(2,1)S(1)}, u32[]{:S(2)}, u32[]{:S(2)}) collective-permute-start(bf16[1,16,4096]{2,1,0:T(8,128)(2,1)} %get-tuple-element.75), channel_id=1, source_target_pairs={{0,33},{1,32},{16,49},{17,48},{32,1},{33,0},{48,17},{49,16},{2,35}... | collective-permute-start | bytes 393224 | tf_op jit(solution)/shard_map/ppermute | solution.py:386
  146.1 11.6 %collective-permute-start.17 = (bf16[1,16,4096]{2,1,0:T(8,128)(2,1)}, bf16[1,16,4096]{2,1,0:T(8,128)(2,1)S(1)}, u32[]{:S(2)}, u32[]{:S(2)}) collective-permute-start(bf16[1,16,4096]{2,1,0:T(8,128)(2,1)} %get-tuple-element.76), channel_id=1, source_target_pairs={{0,48},{1,49},{16,0},{17,1},{32,16},{33,17},{48,32},{49,33},{2,50}... | collective-permute-start | bytes 393224 | tf_op jit(solution)/shard_map/ppermute | solution.py:386
  149.5 8.2 %collective-permute-start.18 = (bf16[1,16,4096]{2,1,0:T(8,128)(2,1)}, bf16[1,16,4096]{2,1,0:T(8,128)(2,1)S(1)}, u32[]{:S(2)}, u32[]{:S(2)}) collective-permute-start(bf16[1,16,4096]{2,1,0:T(8,128)(2,1)} %get-tuple-element.77), channel_id=1, source_target_pairs={{0,49},{1,48},{16,1},{17,0},{32,17},{33,16},{48,33},{49,32},{2,51}... | collective-permute-start | bytes 393224 | tf_op jit(solution)/shard_map/ppermute | solution.py:386
  151.5 23.2 %collective-permute-start.21 = (bf16[768,512]{1,0:T(8,128)(2,1)}, bf16[768,512]{1,0:T(8,128)(2,1)S(1)}, u32[]{:S(2)}, u32[]{:S(2)}) collective-permute-start(bf16[768,512]{1,0:T(8,128)(2,1)} %collective-permute-done.20.refs_3_), channel_id=1, source_target_pairs={{0,64},{64,128},{128,192},{192,256},{256,320},{320,384},{384,448},... | collective-permute-start | bytes 2359304 | tf_op jit(solution)/shard_map/ppermute | solution.py:442
  166.1 18.2 %all-to-all-start.4 = ((bf16[8,16,608]{2,1,0:T(8,128)(2,1)}), bf16[8,16,608]{2,1,0:T(8,128)(2,1)S(1)}, u32[]{:S(2)}, u32[]{:S(2)}) async-start(bf16[8,16,608]{2,1,0:T(8,128)(2,1)} %get-tuple-element.88), calls=%async_computation.4 | async-start | bytes 327680 | tf_op jit(solution)/shard_map/all_to_all | solution.py:454
  186.6 11.1 %all-to-all-start.5 = ((bf16[8,16,608]{2,1,0:T(8,128)(2,1)}), bf16[8,16,608]{2,1,0:T(8,128)(2,1)S(1)}, u32[]{:S(2)}, u32[]{:S(2)}) async-start(bf16[8,16,608]{2,1,0:T(8,128)(2,1)} %spread.1), calls=%async_computation.5 | async-start | bytes 327680 | tf_op jit(solution)/shard_map/all_to_all | solution.py:457
  199.9 14.9 %all-to-all-start.6 = ((bf16[8,16,608]{2,1,0:T(8,128)(2,1)}), bf16[8,16,608]{2,1,0:T(8,128)(2,1)S(1)}, u32[]{:S(2)}, u32[]{:S(2)}) async-start(bf16[8,16,608]{2,1,0:T(8,128)(2,1)} %turn.1), calls=%async_computation.6 | async-start | bytes 327680 | tf_op jit(solution)/shard_map/all_to_all | solution.py:460
  (15 other events, 80.4 us)

commit v4 on v3

--- a/solution.py
+++ b/solution.py
@@ -8,16 +8,13 @@
 from jax.sharding import Mesh, PartitionSpec as P
 
 ADAPTER_SCALE = 2.0
-COST_BUILD, COST_GRADS, COST_BACK = 8, 3, 10
+COST_BUILD, COST_GRADS, COST_BACK = 16, 3, 10
 GROUPS, NX, NY, NC = 8, 4, 8, 2
 COLS = NX * NC
 CAP = 16
 META = 128
-WHOLE, CROSS, SPLIT = 0, 1, 2
-PARTS = {WHOLE: 1, CROSS: 2, SPLIT: COLS}
 MIB = 1024 * 1024
 VM = pl.BlockSpec(memory_space=pltpu.VMEM)
-ANY = pl.BlockSpec(memory_space=pl.ANY)
 HBM = pl.BlockSpec(memory_space=pltpu.HBM)
 SM = pl.BlockSpec(memory_space=pltpu.SMEM)
 NT = (((1,), (1,)), ((), ()))
@@ -89,10 +86,9 @@
     return list(lax.optimization_barrier((tuple(values), tuple(after)))[0])
 
 
-def build_kernel(kind, me, *refs):
-    made, sems = refs[-2:]
+def build_kernel(me, *refs):
+    blocks, (out, made, sems) = refs[:-3], refs[-3:]
     count = made.shape[1]
-    blocks, outs = refs[:count], refs[count:-2]
     going = []
     for b in range(count):
         block = blocks[b]
@@ -102,10 +98,6 @@
         slot = routes[8:16].astype(jnp.int32)
         weight = routes[16:24] + routes[24:32] + routes[32:40]
         x, c = expert // (NY * NC), expert % NC
-        if kind == SPLIT:
-            x = (x - me[0] + NX) % NX
-        if kind != WHOLE:
-            c = (c + me[2]) % NC
         here = ((expert // NC) % NY == me[1]) & (slot < CAP)
         code = jnp.where(here, (x * NC + c) * CAP + slot, -1)
         row = lax.broadcasted_iota(jnp.int32, (COLS * CAP, code.shape[1]), 0)
@@ -122,56 +114,33 @@
             rows = (scale * dot(pick, block[:, at : at + step], NN)).astype(jnp.bfloat16)
             for d in range(COLS):
                 made[d, b, :, at : at + step] = rows[d * CAP : (d + 1) * CAP]
-            if kind != SPLIT:
-                cut = (slice(None), b, slice(None), pl.ds(at, step))
-                going += copies([(made.at[cut], outs[0].at[cut])], sems, len(going))
-    if kind == SPLIT:
-        going = copies([(made.at[d], outs[d]) for d in range(COLS)], sems)
+            cut = (slice(None), b, slice(None), pl.ds(at, step))
+            going += copies([(made.at[cut], out.at[cut])], sems, len(going))
     for copy in going:
         copy.wait()
 
 
-def build(n, me, blocks, kind):
+def build(n, me, blocks):
     width = blocks[0].shape[1] - META
     shape = (len(blocks), CAP, width)
-    outs = [pltpu.HBM(shape, jnp.bfloat16)] * COLS if kind == SPLIT else [pltpu.HBM((COLS,) + shape, jnp.bfloat16)]
-    return pl.pallas_call(
-        functools.partial(build_kernel, kind),
+    return pl.pallas_call(
+        build_kernel,
         name=f"build_{n}",
-        out_shape=outs,
+        out_shape=pltpu.HBM((COLS,) + shape, jnp.bfloat16),
         in_specs=[SM] + [VM] * len(blocks),
-        out_specs=[HBM] * len(outs),
+        out_specs=HBM,
         scratch_shapes=[pltpu.VMEM((COLS,) + shape, jnp.bfloat16), pltpu.SemaphoreType.DMA((8,))],
         compiler_params=params(8),
         cost_estimate=cost(COST_BUILD),
     )(me, *blocks)
 
 
-def places(me, chunk):
-    kind, offsets = chunk
+def places(me, offsets):
     order = [(x, c) for x in range(NX) for c in range(NC)]
-    if kind == CROSS:
-        order = [(x, (me[2] + dc) % NC) for dc in range(NC) for x in range(NX)]
-    if kind == SPLIT:
-        order = [((me[0] - x + NX) % NX, (me[2] + c) % NC) for x, c in order]
     return [(x * NY + (me[1] + offset + NY) % NY) * NC + c for x, c in order for offset in offsets]
 
 
-def fetches(chunk, parts, rows):
-    kind, offsets = chunk
-    if kind == WHOLE:
-        return [(parts[0], rows)]
-    if kind == CROSS:
-        return [
-            (parts[0].at[pl.ds(x * NC, 1)], rows.at[pl.ds(x, 1)]) for x in range(NX)
-        ] + [(parts[1], rows.at[pl.ds(NX, NX)])]
-    return [(parts[d], rows.at[d]) for d in range(COLS)]
-
-
-def grads_kernel(chunk, first, last, waits, *refs):
-    me, refs = refs[0], refs[1 + waits :]
-    count = PARTS[chunk[0]]
-    parts, (hidden, amap, bmap), refs = refs[:count], refs[count : count + 3], refs[count + 3 :]
+def grads_kernel(chunk, first, last, me, part, hidden, amap, bmap, *refs):
     old_a, old_b = (None, None) if first else refs[:2]
     rest = refs if first else refs[2:]
     hid, tok, a_in, b_in, sems = rest[-5:]
@@ -179,7 +148,7 @@
     pairs = [(amap, a_in), (bmap, b_in)]
     pairs += [(hidden.at[src], hid.at[pl.ds(i * CAP, CAP)]) for i, src in enumerate(places(me, chunk))]
     small = len(pairs)
-    coming = copies(pairs + fetches(chunk, parts, tok), sems)
+    coming = copies(pairs + [(part, tok)], sems)
     for copy in coming[:small]:
         copy.wait()
     rows, width = hid.shape[0], tok.shape[-1]
@@ -208,8 +177,8 @@
             )
 
 
-def grads(n, me, parts, hidden, amap, bmap, old, chunk, last, after=()):
-    pieces = COLS * len(chunk[1])
+def grads(n, me, part, hidden, amap, bmap, old, chunk, last):
+    pieces = COLS * len(chunk)
     rows = pieces * CAP
     rank, width = bmap.shape
     hidden_width = amap.shape[1]
@@ -222,39 +191,36 @@
             pltpu.VMEM((rank, hidden_width), jnp.float32),
             pltpu.VMEM((rank, width), jnp.float32),
         ]
-    loaded = [far_memory(array) for array in (*parts, hidden, amap, bmap)]
-    return pl.pallas_call(
-        functools.partial(grads_kernel, chunk, not old, last, len(after)),
+    loaded = [far_memory(array) for array in (part, hidden, amap, bmap)]
+    return pl.pallas_call(
+        functools.partial(grads_kernel, chunk, not old, last),
         name=f"grads_{n}",
         out_shape=shapes,
-        in_specs=[SM] + [ANY] * len(after) + [HBM] * len(loaded) + [VM] * len(old),
+        in_specs=[SM] + [HBM] * len(loaded) + [VM] * len(old),
         out_specs=[VM] * len(shapes),
         scratch_shapes=[
             pltpu.VMEM((rows, hidden_width), jnp.bfloat16),
-            pltpu.VMEM((COLS, len(chunk[1]), CAP, width), jnp.bfloat16),
+            pltpu.VMEM(part.shape, jnp.bfloat16),
             pltpu.VMEM(amap.shape, jnp.bfloat16),
             pltpu.VMEM(bmap.shape, jnp.bfloat16),
-            pltpu.SemaphoreType.DMA((pieces + 2 + COLS,)),
+            pltpu.SemaphoreType.DMA((pieces + 3,)),
         ],
         compiler_params=params(10),
         cost_estimate=cost(COST_GRADS),
-    )(me, *after, *loaded, *old)
+    )(me, *loaded, *old)
 
 
 def back_kernel(chunks, more, me, *refs):
-    counts = [PARTS[chunk[0]] for chunk in chunks]
-    weight, refs = refs[:GROUPS], refs[GROUPS:]
-    flat, refs = refs[: sum(counts)], refs[sum(counts) :]
-    rbs, amap, refs = refs[: len(chunks)], refs[len(chunks)], refs[len(chunks) + 1 + more :]
+    count = len(chunks)
+    weight, parts, refs = refs[:GROUPS], refs[GROUPS : GROUPS + count], refs[GROUPS + count :]
+    rbs, amap, refs = refs[:count], refs[count], refs[count + 1 + more :]
     out, wide_w, tok, rb, done, sems, sems_out = refs
     pairs = []
     begin = 0
-    for n, chunk in enumerate(chunks):
-        pieces = len(chunk[1]) * COLS
-        rows = tok.at[pl.ds(begin, pieces)]
-        at = sum(counts[:n])
-        pairs += fetches(chunk, flat[at : at + counts[n]], rows.reshape(COLS, len(chunk[1]), CAP, tok.shape[-1]))
-        rb[begin * CAP : (begin + pieces) * CAP] = rbs[n][...]
+    for part, own_rb in zip(parts, rbs):
+        pieces = own_rb.shape[0] // CAP
+        pairs.append((part, tok.at[pl.ds(begin, pieces)].reshape(*part.shape)))
+        rb[begin * CAP : (begin + pieces) * CAP] = own_rb[...]
         begin += pieces
     coming = copies(pairs + [(weight[d], wide_w.at[d]) for d in range(GROUPS)], sems)
     total = dot(rb[...], amap[...], NN)
@@ -273,29 +239,29 @@
 
 
 def back(n, me, weight, amap, work, chunks, old=()):
-    flat = [part for parts, rb in work for part in parts]
+    parts = [part for part, rb in work]
     rbs = [rb for parts, rb in work]
     hidden_width = amap.shape[1]
-    width = flat[0].shape[-1]
-    pieces = sum(COLS * len(chunk[1]) for chunk in chunks)
+    width = parts[0].shape[-1]
+    pieces = sum(COLS * len(chunk) for chunk in chunks)
     return pl.pallas_call(
         functools.partial(back_kernel, chunks, len(old)),
         name=f"back_{n}",
         out_shape=pltpu.HBM((NX * NY * NC, CAP, hidden_width), jnp.bfloat16),
-        in_specs=[SM] + [HBM] * (GROUPS + len(flat)) + [VM] * (len(rbs) + 1) + [HBM] * len(old),
+        in_specs=[SM] + [HBM] * (GROUPS + len(parts)) + [VM] * (len(rbs) + 1) + [HBM] * len(old),
         out_specs=HBM,
-        input_output_aliases={2 + GROUPS + len(flat) + len(rbs): 0} if old else {},
+        input_output_aliases={2 + GROUPS + len(parts) + len(rbs): 0} if old else {},
         scratch_shapes=[
             pltpu.VMEM((GROUPS,) + weight[0].shape, jnp.bfloat16),
             pltpu.VMEM((pieces, CAP, width), jnp.bfloat16),
             pltpu.VMEM((pieces * CAP, amap.shape[0]), jnp.bfloat16),
             pltpu.VMEM((pieces, CAP, hidden_width), jnp.bfloat16),
-            pltpu.SemaphoreType.DMA((GROUPS + 2 * COLS * len(work),)),
+            pltpu.SemaphoreType.DMA((GROUPS + len(parts),)),
             pltpu.SemaphoreType.DMA((pieces,)),
         ],
         compiler_params=params(26),
         cost_estimate=cost(COST_BACK),
-    )(me, *(far_memory(array) for array in (*weight, *flat)), *rbs, amap, *old)
+    )(me, *(far_memory(array) for array in (*weight, *parts)), *rbs, amap, *old)
 
 
 def spread_kernel(got, out):
@@ -375,18 +341,8 @@
     beside = taken // (NY * NC) * NC + taken % NC
     where = jnp.where(jnp.arange(NY + 1) < NY, beside, taken // NC % NY)
 
-    def steps(dx, dc):
-        return [(i * NC + j, (i + dx) % NX * NC + (j + dc) % NC) for i in range(NX) for j in range(NC)]
-
-    def send(built, kind):
-        if kind == WHOLE:
-            return [lax.all_to_all(built[0], row, 0, 0, tiled=True)]
-        if kind == CROSS:
-            return [lax.all_to_all(built[0], "x", 0, 0, tiled=True)]
-        return [built[0]] + [lax.ppermute(built[d], row, steps(d // NC, d % NC)) for d in range(1, COLS)]
-
-    def cross(parts):
-        return parts + [lax.ppermute(parts[0][1::NC], "core", [(0, 1), (1, 0)])]
+    def send(built):
+        return lax.all_to_all(built, row, 0, 0, tiled=True)
 
     own = pack(cotangent, route_weight.T, expert_ids.T, slot_ids.T)
     weight = [down_weight[0]] + [None] * (GROUPS - 1)
@@ -396,19 +352,16 @@
     amap = adapter_a[0]
     bmap = adapter_out_maps[0]
 
-    kinds = [WHOLE, CROSS, CROSS, WHOLE, SPLIT]
-    offsets = [(0,)] + [(-d, d) for d in range(1, NY // 2)] + [(NY // 2,)]
-    last = len(offsets) - 1
-    chunks = []
+    chunks = [(0,)] + [(-d, d) for d in range(1, NY // 2)] + [(NY // 2,)]
+    last = len(chunks) - 1
     old = ()
     work = []
-    whole = []
-
-    def settle(n, after=()):
+    sent = []
+
+    def settle(n):
         nonlocal old
-        chunks.append((kinds[n], offsets[n]))
-        rb, *old = grads(n, me, whole[n], hidden, amap, bmap, old, chunks[-1], len(chunks) == last + 1, after)
-        work.append((whole[n], rb))
+        rb, *old = grads(n, me, sent[n], hidden, amap, bmap, old, chunks[n], n == last)
+        work.append((sent[n], rb))
         return rb
 
     either = [(i * NC, (i + 1) % NY * NC) for i in range(NY)] + [(i * NC + 1, (i - 1) % NY * NC + 1) for i in range(NY)]
@@ -422,31 +375,29 @@
             ahead = [lax.ppermute(jnp.where(c == 0, low, high), ("y", "core"), either)]
         done = []
         if w >= 3:
-            whole[w - 3] = gate(whole[w - 3], whole[w - 2][:1])
+            sent[w - 3] = gate([sent[w - 3]], [sent[w - 2]])[0]
             done.append(settle(w - 3))
-        kind = kinds[w - 1]
-        built = build(w - 1, me, held, kind)
-        parts = send(built, kind)
-        whole.append(cross(parts) if kind == CROSS else parts)
+        built = build(w - 1, me, held)
+        sent.append(send(built))
         done += pending
         pending = []
         if w != 2:
             step = max(1, w - 1)
-            after = built if w == 1 else whole[w - 2]
-            rising, falling = gate([weight[step - 1], weight[(1 - step) % GROUPS]], after[:1])
+            after = built if w == 1 else sent[w - 2]
+            rising, falling = gate([weight[step - 1], weight[(1 - step) % GROUPS]], [after])
             weight[step] = lax.ppermute(rising, "dp", rise)
             weight[-step] = lax.ppermute(falling, "dp", fall)
             if w < last:
                 pending = [weight[step], weight[-step]]
-        held = [gate([block], done + [built[0], where])[0] for block in ahead]
+        held = [gate([block], done + [built, where])[0] for block in ahead]
     weight[last] = lax.ppermute(weight[last - 1], "dp", rise)
-    built = build(last, me, held, kinds[last])
-    whole.append(send(built, kinds[last]))
-    whole[2] = gate(whole[2], [built[0]])
-    settle(2)
-    rb = settle(4)
-    whole[3] = gate(whole[3], [rb])
-    settle(3)
+    rb = settle(2)
+    built = build(last, me, gate(held, [rb]))
+    sent.append(send(built))
+    sent[3] = gate([sent[3]], [weight[-3]])[0]
+    rb = settle(3)
+    sent[4] = gate([sent[4]], [rb])[0]
+    settle(4)
 
     def turn_back(n, begin, end, filled):
         return back(n, me, weight, amap, work[begin:end], chunks[begin:end], filled)

time: 219 us -> 215 us (0.982)
  waiting for transfers between devices: 16.8 us -> 33.9 us
  starting transfers between devices: 125 us -> 110 us
  local copies, waits for them, and re-layouts: 7.83 us -> 4.58 us
  Pallas kernels: 64.5 us -> 61.6 us
    ppermute x9 -> x0, starting transfers between devices: 28.3 us -> none  [the longest x7 21.7 us: send(): lax.ppermute(built[d], row, steps(d // NC, d % NC))]
    all_to_all x4 -> x5, waiting for transfers between devices: 1.68 us -> 21.6 us  [send(): return lax.all_to_all(built, row, 0, 0, tiled=True)]
    all_to_all x4 -> x5, starting transfers between devices: 24.3 us -> 31.8 us  [send(): return lax.all_to_all(built, row, 0, 0, tiled=True)]
    slice x2 -> x0, local copies, waits for them, and re-layouts: 3.58 us -> none  [cross(): return parts + [lax.ppermute(parts[0][1::NC], 'core', [(0, 1), (1, 0)])]]
    all_to_all x1, starting transfers between devices: 6.53 us -> 10 us  [per_device(): got = lax.all_to_all(old[0], 'dp', 0, 0, tiled=True)]
    ppermute x3, starting transfers between devices: 22.4 us -> 25 us  [per_device(): weight[-step] = lax.ppermute(falling, 'dp', fall)]
    unnamed x34 -> x18, local copies, waits for them, and re-layouts: 4.25 us -> 4.58 us
  transfers between devices with their start and end apart: 30 -> 22, of which waited for: 6 -> 7; matrix products, arithmetic and copies ran while one was open for 3% -> 1% of each run, Pallas kernels for 26% -> 26%
where the time goes in v4:
time: 215 us; the launch traced here: 214 us
  starting transfers between devices  110 us (51%)
  Pallas kernels  61.6 us (29%)
  waiting for transfers between devices  33.9 us (16%)
  local copies, waits for them, and re-layouts  4.58 us (2%)
    all_to_all x5, starting transfers between devices, send(): return lax.all_to_all(built, row, 0, 0, tiled=True)  31.8 us
    ppermute x3, starting transfers between devices, per_device(): weight[-step] = lax.ppermute(falling, 'dp', fall)  25 us
    pallas_call x3, Pallas kernels, back(): pl.pallas_call(functools.partial(back_kernel, chunks, len(old)), name=f'b...  23.3 us
    all_to_all x5, waiting for transfers between devices, send(): return lax.all_to_all(built, row, 0, 0, tiled=True)  21.6 us
    ppermute x6, starting transfers between devices, per_device(): ahead = [lax.ppermute(low, 'y', up), lax.ppermute(high, 'y', down)]  20.8 us
    pallas_call x5, Pallas kernels, grads(): pl.pallas_call(functools.partial(grads_kernel, chunk, not old, last), nam...  18.2 us
    pallas_call x5, Pallas kernels, build(): pl.pallas_call(build_kernel, name=f'build_{n}', out_shape=pltpu.HBM((COLS...  14 us
    all_to_all x1, starting transfers between devices, per_device(): got = lax.all_to_all(old[0], 'dp', 0, 0, tiled=True)  10 us
  transfers between devices with their start and end apart: 22, of which 7 were waited for; matrix products, arithmetic and copies ran while one was open for 1% of the time, Pallas kernels for 26%

profile of v4, /device:TPU:1, one launch (start us, length us, event | category | flops | bytes accessed | tf_op | source)
XLA Modules:
  0.0 213.6 jit_solution(17732662331291324461)
XLA Ops:
  1.9 4.0 %collective-permute-start = (bf16[128,4224]{1,0:T(8,128)(2,1)S(1)}, bf16[128,4224]{1,0:T(8,128)(2,1)S(1)}, u32[]{:S(2)}, u32[]{:S(2)}) collective-permute-start(bf16[128,4224]{1,0:T(8,128)(2,1)S(1)} %pack.1.refs_0_), channel_id=1, source_target_pairs={{0,2},{2,4},{4,6},{6,8},{8,10},{10,12},{12,14},{14,0},{1,3},{3,5},... | collective-permute-start | bytes 3244040 | tf_op jit(solution)/shard_map/ppermute | solution.py:373
  6.0 3.8 %collective-permute-start.4 = (bf16[128,4224]{1,0:T(8,128)(2,1)S(1)}, bf16[128,4224]{1,0:T(8,128)(2,1)S(1)}, u32[]{:S(2)}, u32[]{:S(2)}) collective-permute-start(bf16[128,4224]{1,0:T(8,128)(2,1)S(1)} %pack.1.refs_0_), channel_id=1, source_target_pairs={{0,14},{2,0},{4,2},{6,4},{8,6},{10,8},{12,10},{14,12},{1,15},{3,1}... | collective-permute-start | bytes 3244040 | tf_op jit(solution)/shard_map/ppermute | solution.py:373
  11.8 10.2 %all-to-all-start = ((bf16[8,1,16,4096]{3,2,1,0:T(8,128)(2,1)}), bf16[8,1,16,4096]{3,2,1,0:T(8,128)(2,1)}, u32[]{:S(2)}, u32[]{:S(2)}) async-start(bf16[8,1,16,4096]{3,2,1,0:T(8,128)(2,1)} %build_0.1), calls=%async_computation | async-start | bytes 2097152 | tf_op jit(solution)/shard_map/all_to_all | solution.py:345
  23.9 5.7 %collective-permute-start.3 = (bf16[768,512]{1,0:T(8,128)(2,1)}, bf16[768,512]{1,0:T(8,128)(2,1)}, u32[]{:S(2)}, u32[]{:S(2)}) collective-permute-start(bf16[768,512]{1,0:T(8,128)(2,1)} %bitcast.28), channel_id=1, source_target_pairs={{0,448},{64,0},{128,64},{192,128},{256,192},{320,256},{384,320},{4... | collective-permute-start | bytes 2359304 | tf_op jit(solution)/shard_map/ppermute | solution.py:389
  32.4 4.6 %collective-permute-start.6 = (bf16[128,4224]{1,0:T(8,128)(2,1)S(1)}, bf16[128,4224]{1,0:T(8,128)(2,1)S(1)}, u32[]{:S(2)}, u32[]{:S(2)}) collective-permute-start(bf16[128,4224]{1,0:T(8,128)(2,1)S(1)} %collective-permute-done.4.refs_1_), channel_id=1, source_target_pairs={{0,14},{2,0},{4,2},{6,4},{8,6},{10,8},{12,10},{14,12},{1,15},{3,1}... | collective-permute-start | bytes 3244040 | tf_op jit(solution)/shard_map/ppermute | solution.py:373
  37.0 3.2 %build_1.1 = bf16[8,2,16,4096]{3,2,1,0:T(8,128)(2,1)} custom-call(s32[4]{0:T(128)S(1)} %pad_add_fusion.me, bf16[128,4224]{1,0:T(8,128)(2,1)S(1)} %collective-permute-done.refs_0_, bf16[128,4224]{1,0:T(8,128)(2,1)S(1)} %collective-permute-done.4.refs_1_), custom_call_target="tpu_custom_call" | custom-call | flops 16000000000 | bytes 48000000 | tf_op jit(solution)/shard_map/build_1/pallas_call | solution.py:126
  40.2 7.0 %all-to-all-start.1 = ((bf16[8,2,16,4096]{3,2,1,0:T(8,128)(2,1)}), bf16[8,2,16,4096]{3,2,1,0:T(8,128)(2,1)}, u32[]{:S(2)}, u32[]{:S(2)}) async-start(bf16[8,2,16,4096]{3,2,1,0:T(8,128)(2,1)} %build_1.1), calls=%async_computation.1 | async-start | bytes 4194304 | tf_op jit(solution)/shard_map/all_to_all | solution.py:345
  47.2 9.7 %collective-permute-done.1.refs_0_ = bf16[128,4224]{1,0:T(8,128)(2,1)} collective-permute-done((bf16[128,4224]{1,0:T(8,128)(2,1)S(1)}, bf16[128,4224]{1,0:T(8,128)(2,1)}, u32[]{:S(2)}, u32[]{:S(2)}) %collective-permute-start.1) | collective-permute-done | bytes 1081376 | tf_op jit(solution)/shard_map/ppermute | solution.py:373
  58.8 4.6 %collective-permute-start.7 = (bf16[128,4224]{1,0:T(8,128)(2,1)S(1)}, bf16[128,4224]{1,0:T(8,128)(2,1)S(1)}, u32[]{:S(2)}, u32[]{:S(2)}) collective-permute-start(bf16[128,4224]{1,0:T(8,128)(2,1)S(1)} %collective-permute-done.6.refs_1_), channel_id=1, source_target_pairs={{0,14},{2,0},{4,2},{6,4},{8,6},{10,8},{12,10},{14,12},{1,15},{3,1}... | collective-permute-start | bytes 3244040 | tf_op jit(solution)/shard_map/ppermute | solution.py:373
  63.4 3.9 %build_2.1 = bf16[8,2,16,4096]{3,2,1,0:T(8,128)(2,1)} custom-call(s32[4]{0:T(128)S(1)} %pad_add_fusion.me, bf16[128,4224]{1,0:T(8,128)(2,1)} %collective-permute-done.1.refs_0_, bf16[128,4224]{1,0:T(8,128)(2,1)S(1)} %collective-permute-done.6.refs_1_), custom_call_target="tpu_custom_call" | custom-call | flops 16000000000 | bytes 48000000 | tf_op jit(solution)/shard_map/build_2/pallas_call | solution.py:126
  67.3 6.3 %all-to-all-done.1.part.refs_9_ = bf16[8,2,16,4096]{3,2,1,0:T(8,128)(2,1)} async-done(((bf16[8,2,16,4096]{3,2,1,0:T(8,128)(2,1)}), bf16[8,2,16,4096]{3,2,1,0:T(8,128)(2,1)}, u32[]{:S(2)}, u32[]{:S(2)}) %all-to-all-start.1) | async-done | bytes 2097184 | tf_op jit(solution)/shard_map/all_to_all | solution.py:345
  73.7 5.1 %all-to-all-start.2 = ((bf16[8,2,16,4096]{3,2,1,0:T(8,128)(2,1)}), bf16[8,2,16,4096]{3,2,1,0:T(8,128)(2,1)}, u32[]{:S(2)}, u32[]{:S(2)}) async-start(bf16[8,2,16,4096]{3,2,1,0:T(8,128)(2,1)} %build_2.1), calls=%async_computation.2 | async-start | bytes 4194304 | tf_op jit(solution)/shard_map/all_to_all | solution.py:345
  78.8 4.0 %collective-permute-start.9 = (bf16[768,512]{1,0:T(8,128)(2,1)}, bf16[768,512]{1,0:T(8,128)(2,1)}, u32[]{:S(2)}, u32[]{:S(2)}) collective-permute-start(bf16[768,512]{1,0:T(8,128)(2,1)} %collective-permute-done.2.refs_1_), channel_id=1, source_target_pairs={{0,64},{64,128},{128,192},{192,256},{256,320},{320,384},{384,448},... | collective-permute-start | bytes 2359304 | tf_op jit(solution)/shard_map/ppermute | solution.py:388
  82.8 8.6 %collective-permute-start.10 = (bf16[768,512]{1,0:T(8,128)(2,1)}, bf16[768,512]{1,0:T(8,128)(2,1)}, u32[]{:S(2)}, u32[]{:S(2)}) collective-permute-start(bf16[768,512]{1,0:T(8,128)(2,1)} %collective-permute-done.3.refs_7_), channel_id=1, source_target_pairs={{0,448},{64,0},{128,64},{192,128},{256,192},{320,256},{384,320},{4... | collective-permute-start | bytes 2359304 | tf_op jit(solution)/shard_map/ppermute | solution.py:389
  91.4 2.9 %grads_0.1 = (bf16[128,16]{1,0:T(8,128)(2,1)S(1)}, f32[16,768]{1,0:T(8,128)S(1)}, f32[16,4096]{1,0:T(8,128)S(1)}) custom-call(s32[4]{0:T(128)S(1)} %pad_add_fusion.me, bf16[8,1,16,4096]{3,2,1,0:T(8,128)(2,1)} %all-to-all-done.part.refs_8_, bf16[64,16,768]{2,1,0:T(8,128)(2,1)} %bitcast.22, bf16[16,768]{1,0:T(8,128)(2,1)} %bitcast.14, bf16[16,4096]{1,0:T(8,128)(2,1)} %bitcast.32), custom_call_target="tpu_custom_call" | custom-call | flops 3000000000 | bytes 9000000 | tf_op jit(solution)/shard_map/grads_0/pallas_call | solution.py:195
  98.1 3.2 %build_3.1 = bf16[8,2,16,4096]{3,2,1,0:T(8,128)(2,1)} custom-call(s32[4]{0:T(128)S(1)} %pad_add_fusion.me, bf16[128,4224]{1,0:T(8,128)(2,1)S(1)} %collective-permute-done.5.refs_0_, bf16[128,4224]{1,0:T(8,128)(2,1)S(1)} %collective-permute-done.7.refs_1_), custom_call_target="tpu_custom_call" | custom-call | flops 16000000000 | bytes 48000000 | tf_op jit(solution)/shard_map/build_3/pallas_call | solution.py:126
  101.3 3.9 %all-to-all-done.2.part.refs_8_ = bf16[8,2,16,4096]{3,2,1,0:T(8,128)(2,1)} async-done(((bf16[8,2,16,4096]{3,2,1,0:T(8,128)(2,1)}), bf16[8,2,16,4096]{3,2,1,0:T(8,128)(2,1)}, u32[]{:S(2)}, u32[]{:S(2)}) %all-to-all-start.2) | async-done | bytes 2097184 | tf_op jit(solution)/shard_map/all_to_all | solution.py:345
  105.2 5.1 %all-to-all-start.4 = ((bf16[8,2,16,4096]{3,2,1,0:T(8,128)(2,1)}), bf16[8,2,16,4096]{3,2,1,0:T(8,128)(2,1)}, u32[]{:S(2)}, u32[]{:S(2)}) async-start(bf16[8,2,16,4096]{3,2,1,0:T(8,128)(2,1)} %build_3.1), calls=%async_computation.4 | async-start | bytes 4194304 | tf_op jit(solution)/shard_map/all_to_all | solution.py:345
  110.3 10.7 %collective-permute-start.11 = (bf16[768,512]{1,0:T(8,128)(2,1)}, bf16[768,512]{1,0:T(8,128)(2,1)}, u32[]{:S(2)}, u32[]{:S(2)}) collective-permute-start(bf16[768,512]{1,0:T(8,128)(2,1)} %collective-permute-done.10.refs_6_), channel_id=1, source_target_pairs={{0,448},{64,0},{128,64},{192,128},{256,192},{320,256},{384,320},{4... | collective-permute-start | bytes 2359304 | tf_op jit(solution)/shard_map/ppermute | solution.py:389
  122.9 3.9 %grads_1.1 = (bf16[256,16]{1,0:T(8,128)(2,1)S(1)}, f32[16,768]{1,0:T(8,128)S(1)}, f32[16,4096]{1,0:T(8,128)S(1)}) custom-call(s32[4]{0:T(128)S(1)} %pad_add_fusion.me, bf16[8,2,16,4096]{3,2,1,0:T(8,128)(2,1)} %all-to-all-done.1.part.refs_9_, bf16[64,16,768]{2,1,0:T(8,128)(2,1)} %bitcast.23, bf16[16,768]{1,0:T(8,128)(2,1)} %bitcast.15, ...), custom_call_target="tpu_custom_call" | custom-call | flops 3000000000 | bytes 9000000 | tf_op jit(solution)/shard_map/grads_1/pallas_call | solution.py:195
  126.9 3.9 %grads_2.1 = (bf16[256,16]{1,0:T(8,128)(2,1)S(1)}, f32[16,768]{1,0:T(8,128)S(1)}, f32[16,4096]{1,0:T(8,128)S(1)}) custom-call(s32[4]{0:T(128)S(1)} %pad_add_fusion.me, bf16[8,2,16,4096]{3,2,1,0:T(8,128)(2,1)} %all-to-all-done.2.part.refs_8_, bf16[64,16,768]{2,1,0:T(8,128)(2,1)} %bitcast.24, bf16[16,768]{1,0:T(8,128)(2,1)} %bitcast.16, ...), custom_call_target="tpu_custom_call" | custom-call | flops 3000000000 | bytes 9000000 | tf_op jit(solution)/shard_map/grads_2/pallas_call | solution.py:195
  132.6 4.1 %all-to-all-done.4.part.refs_8_ = bf16[8,2,16,4096]{3,2,1,0:T(8,128)(2,1)} async-done(((bf16[8,2,16,4096]{3,2,1,0:T(8,128)(2,1)}), bf16[8,2,16,4096]{3,2,1,0:T(8,128)(2,1)}, u32[]{:S(2)}, u32[]{:S(2)}) %all-to-all-start.4) | async-done | bytes 2097184 | tf_op jit(solution)/shard_map/all_to_all | solution.py:345
  136.8 4.3 %all-to-all-start.3 = ((bf16[8,1,16,4096]{3,2,1,0:T(8,128)(2,1)}), bf16[8,1,16,4096]{3,2,1,0:T(8,128)(2,1)S(1)}, u32[]{:S(2)}, u32[]{:S(2)}) async-start(bf16[8,1,16,4096]{3,2,1,0:T(8,128)(2,1)} %build_4.1), calls=%async_computation.3 | async-start | bytes 2097152 | tf_op jit(solution)/shard_map/all_to_all | solution.py:345
  145.1 3.9 %grads_3.1 = (bf16[256,16]{1,0:T(8,128)(2,1)S(1)}, f32[16,768]{1,0:T(8,128)S(1)}, f32[16,4096]{1,0:T(8,128)S(1)}) custom-call(s32[4]{0:T(128)S(1)} %pad_add_fusion.me, bf16[8,2,16,4096]{3,2,1,0:T(8,128)(2,1)} %all-to-all-done.4.part.refs_8_, bf16[64,16,768]{2,1,0:T(8,128)(2,1)} %bitcast.25, bf16[16,768]{1,0:T(8,128)(2,1)} %bitcast.17, ...), custom_call_target="tpu_custom_call" | custom-call | flops 3000000000 | bytes 9000000 | tf_op jit(solution)/shard_map/grads_3/pallas_call | solution.py:195
  149.0 7.2 %all-to-all-done.3.part.refs_9_ = bf16[8,1,16,4096]{3,2,1,0:T(8,128)(2,1)S(1)} async-done(((bf16[8,1,16,4096]{3,2,1,0:T(8,128)(2,1)}), bf16[8,1,16,4096]{3,2,1,0:T(8,128)(2,1)S(1)}, u32[]{:S(2)}, u32[]{:S(2)}) %all-to-all-start.3) | async-done | bytes 1048608 | tf_op jit(solution)/shard_map/all_to_all | solution.py:345
  157.2 3.6 %grads_4.1 = (bf16[128,16]{1,0:T(8,128)(2,1)S(1)}, bf16[8,16,608]{2,1,0:T(8,128)(2,1)}) custom-call(s32[4]{0:T(128)S(1)} %pad_add_fusion.me, bf16[8,1,16,4096]{3,2,1,0:T(8,128)(2,1)} %copy-done.3, bf16[64,16,768]{2,1,0:T(8,128)(2,1)} %bitcast.26, bf16[16,768]{1,0:T(8,128)(2,1)} %bitcast.18, bf16[16,4096]{1,0:T(8,128)(2,1)} %bitcast.36, ...), custom_call_target="tpu_custom_call" | custom-call | flops 3000000000 | bytes 9000000 | tf_op jit(solution)/shard_map/grads_4/pallas_call | solution.py:195
  160.8 10.0 %all-to-all-start.5 = ((bf16[8,16,608]{2,1,0:T(8,128)(2,1)}), bf16[8,16,608]{2,1,0:T(8,128)(2,1)S(1)}, u32[]{:S(2)}, u32[]{:S(2)}) async-start(bf16[8,16,608]{2,1,0:T(8,128)(2,1)} %get-tuple-element.72), calls=%async_computation.5 | async-start | bytes 327680 | tf_op jit(solution)/shard_map/all_to_all | solution.py:405
  171.9 8.4 %back_0.1.refs_11_ = bf16[64,16,768]{2,1,0:T(8,128)(2,1)} custom-call(s32[4]{0:T(128)S(1)} %pad_add_fusion.me, bf16[768,512]{1,0:T(8,128)(2,1)} %bitcast.29, bf16[768,512]{1,0:T(8,128)(2,1)} %collective-permute-done.2.refs_1_, bf16[768,512]{1,0:T(8,128)(2,1)} %collective-permute-done.9.refs_2_, bf16[768,512]{1,0:T(8,128)(2,1)} %collective-permute-done.12.refs_3_, ...), custom_call_target="tpu_custom_call" | custom-call | flops 10000000000 | bytes 30000000 | tf_op jit(solution)/shard_map/back_0/pallas_call | solution.py:247
  182.6 4.6 %all-to-all-start.6 = ((bf16[8,16,608]{2,1,0:T(8,128)(2,1)}), bf16[8,16,608]{2,1,0:T(8,128)(2,1)S(1)}, u32[]{:S(2)}, u32[]{:S(2)}) async-start(bf16[8,16,608]{2,1,0:T(8,128)(2,1)} %spread.1), calls=%async_computation.6 | async-start | bytes 327680 | tf_op jit(solution)/shard_map/all_to_all | solution.py:408
  187.2 6.6 %back_1.1.refs_13_ = bf16[64,16,768]{2,1,0:T(8,128)(2,1)} custom-call(s32[4]{0:T(128)S(1)} %pad_add_fusion.me, bf16[768,512]{1,0:T(8,128)(2,1)} %bitcast.30, bf16[768,512]{1,0:T(8,128)(2,1)} %collective-permute-done.2.refs_1_, bf16[768,512]{1,0:T(8,128)(2,1)} %collective-permute-done.9.refs_2_, ...), custom_call_target="tpu_custom_call", output_to_operand_aliasing={{}: (12, {})} | custom-call | flops 10000000000 | bytes 30000000 | tf_op jit(solution)/shard_map/back_1/pallas_call | solution.py:247
  196.1 6.3 %all-to-all-start.7 = ((bf16[8,16,608]{2,1,0:T(8,128)(2,1)}), bf16[8,16,608]{2,1,0:T(8,128)(2,1)S(1)}, u32[]{:S(2)}, u32[]{:S(2)}) async-start(bf16[8,16,608]{2,1,0:T(8,128)(2,1)} %turn.1), calls=%async_computation.7 | async-start | bytes 327680 | tf_op jit(solution)/shard_map/all_to_all | solution.py:411
  202.3 8.4 %back_2.1 = bf16[64,16,768]{2,1,0:T(8,128)(2,1)} custom-call(s32[4]{0:T(128)S(1)} %pad_add_fusion.me, bf16[768,512]{1,0:T(8,128)(2,1)} %bitcast.31, bf16[768,512]{1,0:T(8,128)(2,1)} %collective-permute-done.2.refs_1_, bf16[768,512]{1,0:T(8,128)(2,1)} %collective-permute-done.9.refs_2_, ...), custom_call_target="tpu_custom_call", output_to_operand_aliasing={{}: (14, {})} | custom-call | flops 10000000000 | bytes 30000000 | tf_op jit(solution)/shard_map/back_2/pallas_call | solution.py:247
  (53 shorter events, 30.9 us)
Async XLA Ops:
  1.9 28.6 %collective-permute-start = (bf16[128,4224]{1,0:T(8,128)(2,1)S(1)}, bf16[128,4224]{1,0:T(8,128)(2,1)S(1)}, u32[]{:S(2)}, u32[]{:S(2)}) collective-permute-start(bf16[128,4224]{1,0:T(8,128)(2,1)S(1)} %pack.1.refs_0_), channel_id=1, source_target_pairs={{0,2},{2,4},{4,6},{6,8},{8,10},{10,12},{12,14},{14,0},{1,3},{3,5},... | collective-permute-start | bytes 3244040 | tf_op jit(solution)/shard_map/ppermute | solution.py:373
  6.0 26.4 %collective-permute-start.4 = (bf16[128,4224]{1,0:T(8,128)(2,1)S(1)}, bf16[128,4224]{1,0:T(8,128)(2,1)S(1)}, u32[]{:S(2)}, u32[]{:S(2)}) collective-permute-start(bf16[128,4224]{1,0:T(8,128)(2,1)S(1)} %pack.1.refs_0_), channel_id=1, source_target_pairs={{0,14},{2,0},{4,2},{6,4},{8,6},{10,8},{12,10},{14,12},{1,15},{3,1}... | collective-permute-start | bytes 3244040 | tf_op jit(solution)/shard_map/ppermute | solution.py:373
  11.8 18.0 %copy-start.8 = (s32[64]{0:T(128)S(1)}, s32[64]{0:T(128)}, u32[]{:S(2)}) copy-start(s32[64]{0:T(128)} %param.17) | copy-start | bytes 772
  11.8 28.4 %all-to-all-start = ((bf16[8,1,16,4096]{3,2,1,0:T(8,128)(2,1)}), bf16[8,1,16,4096]{3,2,1,0:T(8,128)(2,1)}, u32[]{:S(2)}, u32[]{:S(2)}) async-start(bf16[8,1,16,4096]{3,2,1,0:T(8,128)(2,1)} %build_0.1), calls=%async_computation | async-start | bytes 2097152 | tf_op jit(solution)/shard_map/all_to_all | solution.py:345
  22.0 25.3 %collective-permute-start.2 = (bf16[768,512]{1,0:T(8,128)(2,1)}, bf16[768,512]{1,0:T(8,128)(2,1)}, u32[]{:S(2)}, u32[]{:S(2)}) collective-permute-start(bf16[768,512]{1,0:T(8,128)(2,1)} %bitcast.27), channel_id=1, source_target_pairs={{0,64},{64,128},{128,192},{192,256},{256,320},{320,384},{384,448},... | collective-permute-start | bytes 2359304 | tf_op jit(solution)/shard_map/ppermute | solution.py:388
  23.9 23.3 %collective-permute-start.3 = (bf16[768,512]{1,0:T(8,128)(2,1)}, bf16[768,512]{1,0:T(8,128)(2,1)}, u32[]{:S(2)}, u32[]{:S(2)}) collective-permute-start(bf16[768,512]{1,0:T(8,128)(2,1)} %bitcast.28), channel_id=1, source_target_pairs={{0,448},{64,0},{128,64},{192,128},{256,192},{320,256},{384,320},{4... | collective-permute-start | bytes 2359304 | tf_op jit(solution)/shard_map/ppermute | solution.py:389
  30.5 26.4 %collective-permute-start.1 = (bf16[128,4224]{1,0:T(8,128)(2,1)S(1)}, bf16[128,4224]{1,0:T(8,128)(2,1)}, u32[]{:S(2)}, u32[]{:S(2)}) collective-permute-start(bf16[128,4224]{1,0:T(8,128)(2,1)S(1)} %collective-permute-done.refs_0_), channel_id=1, source_target_pairs={{0,2},{2,4},{4,6},{6,8},{8,10},{10,12},{12,14},{14,0},{1,3},{3,5},... | collective-permute-start | bytes 3244040 | tf_op jit(solution)/shard_map/ppermute | solution.py:373
  32.4 26.4 %collective-permute-start.6 = (bf16[128,4224]{1,0:T(8,128)(2,1)S(1)}, bf16[128,4224]{1,0:T(8,128)(2,1)S(1)}, u32[]{:S(2)}, u32[]{:S(2)}) collective-permute-start(bf16[128,4224]{1,0:T(8,128)(2,1)S(1)} %collective-permute-done.4.refs_1_), channel_id=1, source_target_pairs={{0,14},{2,0},{4,2},{6,4},{8,6},{10,8},{12,10},{14,12},{1,15},{3,1}... | collective-permute-start | bytes 3244040 | tf_op jit(solution)/shard_map/ppermute | solution.py:373
  40.2 33.5 %all-to-all-start.1 = ((bf16[8,2,16,4096]{3,2,1,0:T(8,128)(2,1)}), bf16[8,2,16,4096]{3,2,1,0:T(8,128)(2,1)}, u32[]{:S(2)}, u32[]{:S(2)}) async-start(bf16[8,2,16,4096]{3,2,1,0:T(8,128)(2,1)} %build_1.1), calls=%async_computation.1 | async-start | bytes 4194304 | tf_op jit(solution)/shard_map/all_to_all | solution.py:345
  56.9 38.0 %collective-permute-start.5 = (bf16[128,4224]{1,0:T(8,128)(2,1)}, bf16[128,4224]{1,0:T(8,128)(2,1)S(1)}, u32[]{:S(2)}, u32[]{:S(2)}) collective-permute-start(bf16[128,4224]{1,0:T(8,128)(2,1)} %collective-permute-done.1.refs_0_), channel_id=1, source_target_pairs={{0,2},{2,4},{4,6},{6,8},{8,10},{10,12},{12,14},{14,0},{1,3},{3,5},... | collective-permute-start | bytes 3244040 | tf_op jit(solution)/shard_map/ppermute | solution.py:373
  58.8 36.0 %collective-permute-start.7 = (bf16[128,4224]{1,0:T(8,128)(2,1)S(1)}, bf16[128,4224]{1,0:T(8,128)(2,1)S(1)}, u32[]{:S(2)}, u32[]{:S(2)}) collective-permute-start(bf16[128,4224]{1,0:T(8,128)(2,1)S(1)} %collective-permute-done.6.refs_1_), channel_id=1, source_target_pairs={{0,14},{2,0},{4,2},{6,4},{8,6},{10,8},{12,10},{14,12},{1,15},{3,1}... | collective-permute-start | bytes 3244040 | tf_op jit(solution)/shard_map/ppermute | solution.py:373
  73.7 31.5 %all-to-all-start.2 = ((bf16[8,2,16,4096]{3,2,1,0:T(8,128)(2,1)}), bf16[8,2,16,4096]{3,2,1,0:T(8,128)(2,1)}, u32[]{:S(2)}, u32[]{:S(2)}) async-start(bf16[8,2,16,4096]{3,2,1,0:T(8,128)(2,1)} %build_2.1), calls=%async_computation.2 | async-start | bytes 4194304 | tf_op jit(solution)/shard_map/all_to_all | solution.py:345
  78.8 31.5 %collective-permute-start.9 = (bf16[768,512]{1,0:T(8,128)(2,1)}, bf16[768,512]{1,0:T(8,128)(2,1)}, u32[]{:S(2)}, u32[]{:S(2)}) collective-permute-start(bf16[768,512]{1,0:T(8,128)(2,1)} %collective-permute-done.2.refs_1_), channel_id=1, source_target_pairs={{0,64},{64,128},{128,192},{192,256},{256,320},{320,384},{384,448},... | collective-permute-start | bytes 2359304 | tf_op jit(solution)/shard_map/ppermute | solution.py:388
  82.8 27.6 %collective-permute-start.10 = (bf16[768,512]{1,0:T(8,128)(2,1)}, bf16[768,512]{1,0:T(8,128)(2,1)}, u32[]{:S(2)}, u32[]{:S(2)}) collective-permute-start(bf16[768,512]{1,0:T(8,128)(2,1)} %collective-permute-done.3.refs_7_), channel_id=1, source_target_pairs={{0,448},{64,0},{128,64},{192,128},{256,192},{320,256},{384,320},{4... | collective-permute-start | bytes 2359304 | tf_op jit(solution)/shard_map/ppermute | solution.py:389
  94.3 0.6 copy-start.1
  96.0 34.8 %collective-permute-start.8 = (bf16[128,4224]{1,0:T(8,128)(2,1)}, bf16[128,4224]{1,0:T(8,128)(2,1)S(1)}, u32[]{:S(2)}, u32[]{:S(2)}) collective-permute-start(bf16[128,4224]{1,0:T(8,128)(2,1)} %broadcast_select_fusion), channel_id=1, source_target_pairs={{0,2},{2,4},{4,6},{6,8},{8,10},{10,12},{12,14},{14,0},{1,15},{3,1}... | collective-permute-start | bytes 3244040 | tf_op jit(solution)/shard_map/ppermute | solution.py:375
  101.3 21.6 %copy-start.2 = (f32[16,768]{1,0:T(8,128)S(1)}, f32[16,768]{1,0:T(8,128)}, u32[]{:S(2)}) copy-start(f32[16,768]{1,0:T(8,128)} %copy-done.1) | copy-start | bytes 147460
  105.2 31.5 %all-to-all-start.4 = ((bf16[8,2,16,4096]{3,2,1,0:T(8,128)(2,1)}), bf16[8,2,16,4096]{3,2,1,0:T(8,128)(2,1)}, u32[]{:S(2)}, u32[]{:S(2)}) async-start(bf16[8,2,16,4096]{3,2,1,0:T(8,128)(2,1)} %build_3.1), calls=%async_computation.4 | async-start | bytes 4194304 | tf_op jit(solution)/shard_map/all_to_all | solution.py:345
  110.3 34.8 %collective-permute-start.11 = (bf16[768,512]{1,0:T(8,128)(2,1)}, bf16[768,512]{1,0:T(8,128)(2,1)}, u32[]{:S(2)}, u32[]{:S(2)}) collective-permute-start(bf16[768,512]{1,0:T(8,128)(2,1)} %collective-permute-done.10.refs_6_), channel_id=1, source_target_pairs={{0,448},{64,0},{128,64},{192,128},{256,192},{320,256},{384,320},{4... | collective-permute-start | bytes 2359304 | tf_op jit(solution)/shard_map/ppermute | solution.py:389
  121.0 22.1 %collective-permute-start.12 = (bf16[768,512]{1,0:T(8,128)(2,1)}, bf16[768,512]{1,0:T(8,128)(2,1)}, u32[]{:S(2)}, u32[]{:S(2)}) collective-permute-start(bf16[768,512]{1,0:T(8,128)(2,1)} %collective-permute-done.9.refs_2_), channel_id=1, source_target_pairs={{0,64},{64,128},{128,192},{192,256},{256,320},{320,384},{384,448},... | collective-permute-start | bytes 2359304 | tf_op jit(solution)/shard_map/ppermute | solution.py:388
  136.8 19.5 %all-to-all-start.3 = ((bf16[8,1,16,4096]{3,2,1,0:T(8,128)(2,1)}), bf16[8,1,16,4096]{3,2,1,0:T(8,128)(2,1)S(1)}, u32[]{:S(2)}, u32[]{:S(2)}) async-start(bf16[8,1,16,4096]{3,2,1,0:T(8,128)(2,1)} %build_4.1), calls=%async_computation.3 | async-start | bytes 2097152 | tf_op jit(solution)/shard_map/all_to_all | solution.py:345
  143.1 27.8 %collective-permute-start.13 = (bf16[768,512]{1,0:T(8,128)(2,1)}, bf16[768,512]{1,0:T(8,128)(2,1)S(1)}, u32[]{:S(2)}, u32[]{:S(2)}) collective-permute-start(bf16[768,512]{1,0:T(8,128)(2,1)} %collective-permute-done.12.refs_3_), channel_id=1, source_target_pairs={{0,64},{64,128},{128,192},{192,256},{256,320},{320,384},{384,448},... | collective-permute-start | bytes 2359304 | tf_op jit(solution)/shard_map/ppermute | solution.py:393
  156.2 1.0 copy-start.3
  157.2 14.7 %copy-start = (bf16[1,16,768]{2,1,0:T(8,128)(2,1)S(1)}, bf16[1,16,768]{2,1,0:T(8,128)(2,1)}, u32[]{:S(2)}) copy-start(bf16[1,16,768]{2,1,0:T(8,128)(2,1)} %param.15) | copy-start | bytes 73732
  160.8 19.4 %all-to-all-start.5 = ((bf16[8,16,608]{2,1,0:T(8,128)(2,1)}), bf16[8,16,608]{2,1,0:T(8,128)(2,1)S(1)}, u32[]{:S(2)}, u32[]{:S(2)}) async-start(bf16[8,16,608]{2,1,0:T(8,128)(2,1)} %get-tuple-element.72), calls=%async_computation.5 | async-start | bytes 327680 | tf_op jit(solution)/shard_map/all_to_all | solution.py:405
  170.9 1.0 copy-start.7
  180.3 0.7 copy-start.5
  182.6 11.2 %all-to-all-start.6 = ((bf16[8,16,608]{2,1,0:T(8,128)(2,1)}), bf16[8,16,608]{2,1,0:T(8,128)(2,1)S(1)}, u32[]{:S(2)}, u32[]{:S(2)}) async-start(bf16[8,16,608]{2,1,0:T(8,128)(2,1)} %spread.1), calls=%async_computation.6 | async-start | bytes 327680 | tf_op jit(solution)/shard_map/all_to_all | solution.py:408
  193.8 0.7 copy-start.6
  196.1 15.3 %all-to-all-start.7 = ((bf16[8,16,608]{2,1,0:T(8,128)(2,1)}), bf16[8,16,608]{2,1,0:T(8,128)(2,1)S(1)}, u32[]{:S(2)}, u32[]{:S(2)}) async-start(bf16[8,16,608]{2,1,0:T(8,128)(2,1)} %turn.1), calls=%async_computation.7 | async-start | bytes 327680 | tf_op jit(solution)/shard_map/all_to_all | solution.py:411
  211.4 0.7 copy-start.4

commit v5 on v4

--- a/solution.py
+++ b/solution.py
@@ -148,14 +148,14 @@
     pairs = [(amap, a_in), (bmap, b_in)]
     pairs += [(hidden.at[src], hid.at[pl.ds(i * CAP, CAP)]) for i, src in enumerate(places(me, chunk))]
     small = len(pairs)
-    coming = copies(pairs + [(part, tok)], sems)
+    coming = copies(pairs + ([] if last else [(part, tok)]), sems)
     for copy in coming[:small]:
         copy.wait()
     rows, width = hid.shape[0], tok.shape[-1]
     z = dot(hid[...], a_in[...], NT).astype(jnp.bfloat16)
     for copy in coming[small:]:
         copy.wait()
-    tokens = tok[...].reshape(rows, width)
+    tokens = (part if last else tok)[...].reshape(rows, width)
     rb = (ADAPTER_SCALE * dot(tokens, b_in[...], NT)).astype(jnp.bfloat16)
     outs[0][...] = rb
     grad_b = ADAPTER_SCALE * dot(z, tokens, TN)
@@ -191,12 +191,12 @@
             pltpu.VMEM((rank, hidden_width), jnp.float32),
             pltpu.VMEM((rank, width), jnp.float32),
         ]
-    loaded = [far_memory(array) for array in (part, hidden, amap, bmap)]
+    loaded = [part if last else far_memory(part)] + [far_memory(array) for array in (hidden, amap, bmap)]
     return pl.pallas_call(
         functools.partial(grads_kernel, chunk, not old, last),
         name=f"grads_{n}",
         out_shape=shapes,
-        in_specs=[SM] + [HBM] * len(loaded) + [VM] * len(old),
+        in_specs=[SM] + [VM if last else HBM] + [HBM] * 3 + [VM] * len(old),
         out_specs=[VM] * len(shapes),
         scratch_shapes=[
             pltpu.VMEM((rows, hidden_width), jnp.bfloat16),

time: 215 us -> 215 us (level)
  transfers between devices with their start and end apart: 22 -> 22, of which waited for: 7 -> 8; matrix products, arithmetic and copies ran while one was open for 1% -> 1% of each run, Pallas kernels for 26% -> 26%
where the time goes in v5:
time: 215 us; the launch traced here: 213 us
  starting transfers between devices  111 us (52%)
  Pallas kernels  61.1 us (28%)
  waiting for transfers between devices  34.5 us (16%)
  local copies, waits for them, and re-layouts  3.61 us (2%)
    all_to_all x5, starting transfers between devices, send(): return lax.all_to_all(built, row, 0, 0, tiled=True)  31.8 us
    ppermute x3, starting transfers between devices, per_device(): weight[-step] = lax.ppermute(falling, 'dp', fall)  25 us
    pallas_call x3, Pallas kernels, back(): pl.pallas_call(functools.partial(back_kernel, chunks, len(old)), name=f'b...  23.3 us
    all_to_all x5, waiting for transfers between devices, send(): return lax.all_to_all(built, row, 0, 0, tiled=True)  21.6 us
    ppermute x6, starting transfers between devices, per_device(): ahead = [lax.ppermute(low, 'y', up), lax.ppermute(high, 'y', down)]  20.8 us
    pallas_call x5, Pallas kernels, grads(): pl.pallas_call(functools.partial(grads_kernel, chunk, not old, last), nam...  17.7 us
    pallas_call x5, Pallas kernels, build(): pl.pallas_call(build_kernel, name=f'build_{n}', out_shape=pltpu.HBM((COLS...  14 us
    all_to_all x1, starting transfers between devices, per_device(): got = lax.all_to_all(old[0], 'dp', 0, 0, tiled=True)  10 us
  transfers between devices with their start and end apart: 22, of which 8 were waited for; matrix products, arithmetic and copies ran while one was open for 1% of the time, Pallas kernels for 26%

profile of v5, /device:TPU:1, one launch (start us, length us, event | category | flops | bytes accessed | tf_op | source)
XLA Modules:
  0.0 213.2 jit_solution(4415507473516362314)
XLA Ops:
  1.9 4.0 %collective-permute-start = (bf16[128,4224]{1,0:T(8,128)(2,1)S(1)}, bf16[128,4224]{1,0:T(8,128)(2,1)S(1)}, u32[]{:S(2)}, u32[]{:S(2)}) collective-permute-start(bf16[128,4224]{1,0:T(8,128)(2,1)S(1)} %pack.1.refs_0_), channel_id=1, source_target_pairs={{0,2},{2,4},{4,6},{6,8},{8,10},{10,12},{12,14},{14,0},{1,3},{3,5},... | collective-permute-start | bytes 3244040 | tf_op jit(solution)/shard_map/ppermute | solution.py:373
  6.0 3.8 %collective-permute-start.4 = (bf16[128,4224]{1,0:T(8,128)(2,1)S(1)}, bf16[128,4224]{1,0:T(8,128)(2,1)S(1)}, u32[]{:S(2)}, u32[]{:S(2)}) collective-permute-start(bf16[128,4224]{1,0:T(8,128)(2,1)S(1)} %pack.1.refs_0_), channel_id=1, source_target_pairs={{0,14},{2,0},{4,2},{6,4},{8,6},{10,8},{12,10},{14,12},{1,15},{3,1}... | collective-permute-start | bytes 3244040 | tf_op jit(solution)/shard_map/ppermute | solution.py:373
  11.8 10.2 %all-to-all-start = ((bf16[8,1,16,4096]{3,2,1,0:T(8,128)(2,1)}), bf16[8,1,16,4096]{3,2,1,0:T(8,128)(2,1)}, u32[]{:S(2)}, u32[]{:S(2)}) async-start(bf16[8,1,16,4096]{3,2,1,0:T(8,128)(2,1)} %build_0.1), calls=%async_computation | async-start | bytes 2097152 | tf_op jit(solution)/shard_map/all_to_all | solution.py:345
  23.9 5.7 %collective-permute-start.3 = (bf16[768,512]{1,0:T(8,128)(2,1)}, bf16[768,512]{1,0:T(8,128)(2,1)}, u32[]{:S(2)}, u32[]{:S(2)}) collective-permute-start(bf16[768,512]{1,0:T(8,128)(2,1)} %bitcast.28), channel_id=1, source_target_pairs={{0,448},{64,0},{128,64},{192,128},{256,192},{320,256},{384,320},{4... | collective-permute-start | bytes 2359304 | tf_op jit(solution)/shard_map/ppermute | solution.py:389
  32.4 4.6 %collective-permute-start.6 = (bf16[128,4224]{1,0:T(8,128)(2,1)S(1)}, bf16[128,4224]{1,0:T(8,128)(2,1)S(1)}, u32[]{:S(2)}, u32[]{:S(2)}) collective-permute-start(bf16[128,4224]{1,0:T(8,128)(2,1)S(1)} %collective-permute-done.4.refs_1_), channel_id=1, source_target_pairs={{0,14},{2,0},{4,2},{6,4},{8,6},{10,8},{12,10},{14,12},{1,15},{3,1}... | collective-permute-start | bytes 3244040 | tf_op jit(solution)/shard_map/ppermute | solution.py:373
  37.0 3.2 %build_1.1 = bf16[8,2,16,4096]{3,2,1,0:T(8,128)(2,1)} custom-call(s32[4]{0:T(128)S(1)} %pad_add_fusion.me, bf16[128,4224]{1,0:T(8,128)(2,1)S(1)} %collective-permute-done.refs_0_, bf16[128,4224]{1,0:T(8,128)(2,1)S(1)} %collective-permute-done.4.refs_1_), custom_call_target="tpu_custom_call" | custom-call | flops 16000000000 | bytes 48000000 | tf_op jit(solution)/shard_map/build_1/pallas_call | solution.py:126
  40.2 7.0 %all-to-all-start.1 = ((bf16[8,2,16,4096]{3,2,1,0:T(8,128)(2,1)}), bf16[8,2,16,4096]{3,2,1,0:T(8,128)(2,1)}, u32[]{:S(2)}, u32[]{:S(2)}) async-start(bf16[8,2,16,4096]{3,2,1,0:T(8,128)(2,1)} %build_1.1), calls=%async_computation.1 | async-start | bytes 4194304 | tf_op jit(solution)/shard_map/all_to_all | solution.py:345
  47.2 9.7 %collective-permute-done.1.refs_0_ = bf16[128,4224]{1,0:T(8,128)(2,1)} collective-permute-done((bf16[128,4224]{1,0:T(8,128)(2,1)S(1)}, bf16[128,4224]{1,0:T(8,128)(2,1)}, u32[]{:S(2)}, u32[]{:S(2)}) %collective-permute-start.1) | collective-permute-done | bytes 1081376 | tf_op jit(solution)/shard_map/ppermute | solution.py:373
  58.8 4.6 %collective-permute-start.7 = (bf16[128,4224]{1,0:T(8,128)(2,1)S(1)}, bf16[128,4224]{1,0:T(8,128)(2,1)S(1)}, u32[]{:S(2)}, u32[]{:S(2)}) collective-permute-start(bf16[128,4224]{1,0:T(8,128)(2,1)S(1)} %collective-permute-done.6.refs_1_), channel_id=1, source_target_pairs={{0,14},{2,0},{4,2},{6,4},{8,6},{10,8},{12,10},{14,12},{1,15},{3,1}... | collective-permute-start | bytes 3244040 | tf_op jit(solution)/shard_map/ppermute | solution.py:373
  63.4 3.9 %build_2.1 = bf16[8,2,16,4096]{3,2,1,0:T(8,128)(2,1)} custom-call(s32[4]{0:T(128)S(1)} %pad_add_fusion.me, bf16[128,4224]{1,0:T(8,128)(2,1)} %collective-permute-done.1.refs_0_, bf16[128,4224]{1,0:T(8,128)(2,1)S(1)} %collective-permute-done.6.refs_1_), custom_call_target="tpu_custom_call" | custom-call | flops 16000000000 | bytes 48000000 | tf_op jit(solution)/shard_map/build_2/pallas_call | solution.py:126
  67.3 6.3 %all-to-all-done.1.part.refs_9_ = bf16[8,2,16,4096]{3,2,1,0:T(8,128)(2,1)} async-done(((bf16[8,2,16,4096]{3,2,1,0:T(8,128)(2,1)}), bf16[8,2,16,4096]{3,2,1,0:T(8,128)(2,1)}, u32[]{:S(2)}, u32[]{:S(2)}) %all-to-all-start.1) | async-done | bytes 2097184 | tf_op jit(solution)/shard_map/all_to_all | solution.py:345
  73.7 5.1 %all-to-all-start.2 = ((bf16[8,2,16,4096]{3,2,1,0:T(8,128)(2,1)}), bf16[8,2,16,4096]{3,2,1,0:T(8,128)(2,1)}, u32[]{:S(2)}, u32[]{:S(2)}) async-start(bf16[8,2,16,4096]{3,2,1,0:T(8,128)(2,1)} %build_2.1), calls=%async_computation.2 | async-start | bytes 4194304 | tf_op jit(solution)/shard_map/all_to_all | solution.py:345
  78.8 4.0 %collective-permute-start.9 = (bf16[768,512]{1,0:T(8,128)(2,1)}, bf16[768,512]{1,0:T(8,128)(2,1)}, u32[]{:S(2)}, u32[]{:S(2)}) collective-permute-start(bf16[768,512]{1,0:T(8,128)(2,1)} %collective-permute-done.2.refs_1_), channel_id=1, source_target_pairs={{0,64},{64,128},{128,192},{192,256},{256,320},{320,384},{384,448},... | collective-permute-start | bytes 2359304 | tf_op jit(solution)/shard_map/ppermute | solution.py:388
  82.8 8.6 %collective-permute-start.10 = (bf16[768,512]{1,0:T(8,128)(2,1)}, bf16[768,512]{1,0:T(8,128)(2,1)}, u32[]{:S(2)}, u32[]{:S(2)}) collective-permute-start(bf16[768,512]{1,0:T(8,128)(2,1)} %collective-permute-done.3.refs_7_), channel_id=1, source_target_pairs={{0,448},{64,0},{128,64},{192,128},{256,192},{320,256},{384,320},{4... | collective-permute-start | bytes 2359304 | tf_op jit(solution)/shard_map/ppermute | solution.py:389
  91.4 2.9 %grads_0.1 = (bf16[128,16]{1,0:T(8,128)(2,1)S(1)}, f32[16,768]{1,0:T(8,128)S(1)}, f32[16,4096]{1,0:T(8,128)S(1)}) custom-call(s32[4]{0:T(128)S(1)} %pad_add_fusion.me, bf16[8,1,16,4096]{3,2,1,0:T(8,128)(2,1)} %all-to-all-done.part.refs_8_, bf16[64,16,768]{2,1,0:T(8,128)(2,1)} %bitcast.22, bf16[16,768]{1,0:T(8,128)(2,1)} %bitcast.14, bf16[16,4096]{1,0:T(8,128)(2,1)} %bitcast.32), custom_call_target="tpu_custom_call" | custom-call | flops 3000000000 | bytes 9000000 | tf_op jit(solution)/shard_map/grads_0/pallas_call | solution.py:195
  98.1 3.2 %build_3.1 = bf16[8,2,16,4096]{3,2,1,0:T(8,128)(2,1)} custom-call(s32[4]{0:T(128)S(1)} %pad_add_fusion.me, bf16[128,4224]{1,0:T(8,128)(2,1)S(1)} %collective-permute-done.5.refs_0_, bf16[128,4224]{1,0:T(8,128)(2,1)S(1)} %collective-permute-done.7.refs_1_), custom_call_target="tpu_custom_call" | custom-call | flops 16000000000 | bytes 48000000 | tf_op jit(solution)/shard_map/build_3/pallas_call | solution.py:126
  101.3 3.9 %all-to-all-done.2.part.refs_8_ = bf16[8,2,16,4096]{3,2,1,0:T(8,128)(2,1)} async-done(((bf16[8,2,16,4096]{3,2,1,0:T(8,128)(2,1)}), bf16[8,2,16,4096]{3,2,1,0:T(8,128)(2,1)}, u32[]{:S(2)}, u32[]{:S(2)}) %all-to-all-start.2) | async-done | bytes 2097184 | tf_op jit(solution)/shard_map/all_to_all | solution.py:345
  105.2 5.1 %all-to-all-start.4 = ((bf16[8,2,16,4096]{3,2,1,0:T(8,128)(2,1)}), bf16[8,2,16,4096]{3,2,1,0:T(8,128)(2,1)}, u32[]{:S(2)}, u32[]{:S(2)}) async-start(bf16[8,2,16,4096]{3,2,1,0:T(8,128)(2,1)} %build_3.1), calls=%async_computation.4 | async-start | bytes 4194304 | tf_op jit(solution)/shard_map/all_to_all | solution.py:345
  110.3 10.7 %collective-permute-start.11 = (bf16[768,512]{1,0:T(8,128)(2,1)}, bf16[768,512]{1,0:T(8,128)(2,1)}, u32[]{:S(2)}, u32[]{:S(2)}) collective-permute-start(bf16[768,512]{1,0:T(8,128)(2,1)} %collective-permute-done.10.refs_6_), channel_id=1, source_target_pairs={{0,448},{64,0},{128,64},{192,128},{256,192},{320,256},{384,320},{4... | collective-permute-start | bytes 2359304 | tf_op jit(solution)/shard_map/ppermute | solution.py:389
  122.9 3.9 %grads_1.1 = (bf16[256,16]{1,0:T(8,128)(2,1)S(1)}, f32[16,768]{1,0:T(8,128)S(1)}, f32[16,4096]{1,0:T(8,128)S(1)}) custom-call(s32[4]{0:T(128)S(1)} %pad_add_fusion.me, bf16[8,2,16,4096]{3,2,1,0:T(8,128)(2,1)} %all-to-all-done.1.part.refs_9_, bf16[64,16,768]{2,1,0:T(8,128)(2,1)} %bitcast.23, bf16[16,768]{1,0:T(8,128)(2,1)} %bitcast.15, ...), custom_call_target="tpu_custom_call" | custom-call | flops 3000000000 | bytes 9000000 | tf_op jit(solution)/shard_map/grads_1/pallas_call | solution.py:195
  126.9 3.9 %grads_2.1 = (bf16[256,16]{1,0:T(8,128)(2,1)S(1)}, f32[16,768]{1,0:T(8,128)S(1)}, f32[16,4096]{1,0:T(8,128)S(1)}) custom-call(s32[4]{0:T(128)S(1)} %pad_add_fusion.me, bf16[8,2,16,4096]{3,2,1,0:T(8,128)(2,1)} %all-to-all-done.2.part.refs_8_, bf16[64,16,768]{2,1,0:T(8,128)(2,1)} %bitcast.24, bf16[16,768]{1,0:T(8,128)(2,1)} %bitcast.16, ...), custom_call_target="tpu_custom_call" | custom-call | flops 3000000000 | bytes 9000000 | tf_op jit(solution)/shard_map/grads_2/pallas_call | solution.py:195
  132.6 4.1 %all-to-all-done.4.part.refs_8_ = bf16[8,2,16,4096]{3,2,1,0:T(8,128)(2,1)} async-done(((bf16[8,2,16,4096]{3,2,1,0:T(8,128)(2,1)}), bf16[8,2,16,4096]{3,2,1,0:T(8,128)(2,1)}, u32[]{:S(2)}, u32[]{:S(2)}) %all-to-all-start.4) | async-done | bytes 2097184 | tf_op jit(solution)/shard_map/all_to_all | solution.py:345
  136.8 4.3 %all-to-all-start.3 = ((bf16[8,1,16,4096]{3,2,1,0:T(8,128)(2,1)}), bf16[8,1,16,4096]{3,2,1,0:T(8,128)(2,1)S(1)}, u32[]{:S(2)}, u32[]{:S(2)}) async-start(bf16[8,1,16,4096]{3,2,1,0:T(8,128)(2,1)} %build_4.1), calls=%async_computation.3 | async-start | bytes 2097152 | tf_op jit(solution)/shard_map/all_to_all | solution.py:345
  145.1 3.9 %grads_3.1 = (bf16[256,16]{1,0:T(8,128)(2,1)S(1)}, f32[16,768]{1,0:T(8,128)S(1)}, f32[16,4096]{1,0:T(8,128)S(1)}) custom-call(s32[4]{0:T(128)S(1)} %pad_add_fusion.me, bf16[8,2,16,4096]{3,2,1,0:T(8,128)(2,1)} %all-to-all-done.4.part.refs_8_, bf16[64,16,768]{2,1,0:T(8,128)(2,1)} %bitcast.25, bf16[16,768]{1,0:T(8,128)(2,1)} %bitcast.17, ...), custom_call_target="tpu_custom_call" | custom-call | flops 3000000000 | bytes 9000000 | tf_op jit(solution)/shard_map/grads_3/pallas_call | solution.py:195
  149.0 7.2 %all-to-all-done.3.part.refs_9_ = bf16[8,1,16,4096]{3,2,1,0:T(8,128)(2,1)S(1)} async-done(((bf16[8,1,16,4096]{3,2,1,0:T(8,128)(2,1)}), bf16[8,1,16,4096]{3,2,1,0:T(8,128)(2,1)S(1)}, u32[]{:S(2)}, u32[]{:S(2)}) %all-to-all-start.3) | async-done | bytes 1048608 | tf_op jit(solution)/shard_map/all_to_all | solution.py:345
  156.2 3.1 %grads_4.1 = (bf16[128,16]{1,0:T(8,128)(2,1)S(1)}, bf16[8,16,608]{2,1,0:T(8,128)(2,1)}) custom-call(s32[4]{0:T(128)S(1)} %pad_add_fusion.me, bf16[8,1,16,4096]{3,2,1,0:T(8,128)(2,1)S(1)} %all-to-all-done.3.part.refs_9_, bf16[64,16,768]{2,1,0:T(8,128)(2,1)} %bitcast.26, bf16[16,768]{1,0:T(8,128)(2,1)} %bitcast.18, bf16[16,4096]{1,0:T(8,128)(2,1)} %bitcast.36, ...), custom_call_target="tpu_custom_call" | custom-call | flops 3000000000 | bytes 9000000 | tf_op jit(solution)/shard_map/grads_4/pallas_call | solution.py:195
  159.4 10.0 %all-to-all-start.5 = ((bf16[8,16,608]{2,1,0:T(8,128)(2,1)}), bf16[8,16,608]{2,1,0:T(8,128)(2,1)S(1)}, u32[]{:S(2)}, u32[]{:S(2)}) async-start(bf16[8,16,608]{2,1,0:T(8,128)(2,1)} %get-tuple-element.72), calls=%async_computation.5 | async-start | bytes 327680 | tf_op jit(solution)/shard_map/all_to_all | solution.py:405
  170.8 8.4 %back_0.1.refs_11_ = bf16[64,16,768]{2,1,0:T(8,128)(2,1)} custom-call(s32[4]{0:T(128)S(1)} %pad_add_fusion.me, bf16[768,512]{1,0:T(8,128)(2,1)} %bitcast.29, bf16[768,512]{1,0:T(8,128)(2,1)} %collective-permute-done.2.refs_1_, bf16[768,512]{1,0:T(8,128)(2,1)} %collective-permute-done.9.refs_2_, bf16[768,512]{1,0:T(8,128)(2,1)} %collective-permute-done.12.refs_3_, ...), custom_call_target="tpu_custom_call" | custom-call | flops 10000000000 | bytes 30000000 | tf_op jit(solution)/shard_map/back_0/pallas_call | solution.py:247
  181.4 5.2 %all-to-all-start.6 = ((bf16[8,16,608]{2,1,0:T(8,128)(2,1)}), bf16[8,16,608]{2,1,0:T(8,128)(2,1)S(1)}, u32[]{:S(2)}, u32[]{:S(2)}) async-start(bf16[8,16,608]{2,1,0:T(8,128)(2,1)} %spread.1), calls=%async_computation.6 | async-start | bytes 327680 | tf_op jit(solution)/shard_map/all_to_all | solution.py:408
  186.6 6.6 %back_1.1.refs_13_ = bf16[64,16,768]{2,1,0:T(8,128)(2,1)} custom-call(s32[4]{0:T(128)S(1)} %pad_add_fusion.me, bf16[768,512]{1,0:T(8,128)(2,1)} %bitcast.30, bf16[768,512]{1,0:T(8,128)(2,1)} %collective-permute-done.2.refs_1_, bf16[768,512]{1,0:T(8,128)(2,1)} %collective-permute-done.9.refs_2_, ...), custom_call_target="tpu_custom_call", output_to_operand_aliasing={{}: (12, {})} | custom-call | flops 10000000000 | bytes 30000000 | tf_op jit(solution)/shard_map/back_1/pallas_call | solution.py:247
  195.5 6.3 %all-to-all-start.7 = ((bf16[8,16,608]{2,1,0:T(8,128)(2,1)}), bf16[8,16,608]{2,1,0:T(8,128)(2,1)S(1)}, u32[]{:S(2)}, u32[]{:S(2)}) async-start(bf16[8,16,608]{2,1,0:T(8,128)(2,1)} %turn.1), calls=%async_computation.7 | async-start | bytes 327680 | tf_op jit(solution)/shard_map/all_to_all | solution.py:411
  201.8 8.4 %back_2.1 = bf16[64,16,768]{2,1,0:T(8,128)(2,1)} custom-call(s32[4]{0:T(128)S(1)} %pad_add_fusion.me, bf16[768,512]{1,0:T(8,128)(2,1)} %bitcast.31, bf16[768,512]{1,0:T(8,128)(2,1)} %collective-permute-done.2.refs_1_, bf16[768,512]{1,0:T(8,128)(2,1)} %collective-permute-done.9.refs_2_, ...), custom_call_target="tpu_custom_call", output_to_operand_aliasing={{}: (14, {})} | custom-call | flops 10000000000 | bytes 30000000 | tf_op jit(solution)/shard_map/back_2/pallas_call | solution.py:247
  (53 shorter events, 30.5 us)
Async XLA Ops:
  1.9 28.6 %collective-permute-start = (bf16[128,4224]{1,0:T(8,128)(2,1)S(1)}, bf16[128,4224]{1,0:T(8,128)(2,1)S(1)}, u32[]{:S(2)}, u32[]{:S(2)}) collective-permute-start(bf16[128,4224]{1,0:T(8,128)(2,1)S(1)} %pack.1.refs_0_), channel_id=1, source_target_pairs={{0,2},{2,4},{4,6},{6,8},{8,10},{10,12},{12,14},{14,0},{1,3},{3,5},... | collective-permute-start | bytes 3244040 | tf_op jit(solution)/shard_map/ppermute | solution.py:373
  6.0 26.4 %collective-permute-start.4 = (bf16[128,4224]{1,0:T(8,128)(2,1)S(1)}, bf16[128,4224]{1,0:T(8,128)(2,1)S(1)}, u32[]{:S(2)}, u32[]{:S(2)}) collective-permute-start(bf16[128,4224]{1,0:T(8,128)(2,1)S(1)} %pack.1.refs_0_), channel_id=1, source_target_pairs={{0,14},{2,0},{4,2},{6,4},{8,6},{10,8},{12,10},{14,12},{1,15},{3,1}... | collective-permute-start | bytes 3244040 | tf_op jit(solution)/shard_map/ppermute | solution.py:373
  11.8 18.0 %copy-start.8 = (s32[64]{0:T(128)S(1)}, s32[64]{0:T(128)}, u32[]{:S(2)}) copy-start(s32[64]{0:T(128)} %param.17) | copy-start | bytes 772
  11.8 28.4 %all-to-all-start = ((bf16[8,1,16,4096]{3,2,1,0:T(8,128)(2,1)}), bf16[8,1,16,4096]{3,2,1,0:T(8,128)(2,1)}, u32[]{:S(2)}, u32[]{:S(2)}) async-start(bf16[8,1,16,4096]{3,2,1,0:T(8,128)(2,1)} %build_0.1), calls=%async_computation | async-start | bytes 2097152 | tf_op jit(solution)/shard_map/all_to_all | solution.py:345
  22.0 25.3 %collective-permute-start.2 = (bf16[768,512]{1,0:T(8,128)(2,1)}, bf16[768,512]{1,0:T(8,128)(2,1)}, u32[]{:S(2)}, u32[]{:S(2)}) collective-permute-start(bf16[768,512]{1,0:T(8,128)(2,1)} %bitcast.27), channel_id=1, source_target_pairs={{0,64},{64,128},{128,192},{192,256},{256,320},{320,384},{384,448},... | collective-permute-start | bytes 2359304 | tf_op jit(solution)/shard_map/ppermute | solution.py:388
  23.9 23.3 %collective-permute-start.3 = (bf16[768,512]{1,0:T(8,128)(2,1)}, bf16[768,512]{1,0:T(8,128)(2,1)}, u32[]{:S(2)}, u32[]{:S(2)}) collective-permute-start(bf16[768,512]{1,0:T(8,128)(2,1)} %bitcast.28), channel_id=1, source_target_pairs={{0,448},{64,0},{128,64},{192,128},{256,192},{320,256},{384,320},{4... | collective-permute-start | bytes 2359304 | tf_op jit(solution)/shard_map/ppermute | solution.py:389
  30.5 26.4 %collective-permute-start.1 = (bf16[128,4224]{1,0:T(8,128)(2,1)S(1)}, bf16[128,4224]{1,0:T(8,128)(2,1)}, u32[]{:S(2)}, u32[]{:S(2)}) collective-permute-start(bf16[128,4224]{1,0:T(8,128)(2,1)S(1)} %collective-permute-done.refs_0_), channel_id=1, source_target_pairs={{0,2},{2,4},{4,6},{6,8},{8,10},{10,12},{12,14},{14,0},{1,3},{3,5},... | collective-permute-start | bytes 3244040 | tf_op jit(solution)/shard_map/ppermute | solution.py:373
  32.4 26.4 %collective-permute-start.6 = (bf16[128,4224]{1,0:T(8,128)(2,1)S(1)}, bf16[128,4224]{1,0:T(8,128)(2,1)S(1)}, u32[]{:S(2)}, u32[]{:S(2)}) collective-permute-start(bf16[128,4224]{1,0:T(8,128)(2,1)S(1)} %collective-permute-done.4.refs_1_), channel_id=1, source_target_pairs={{0,14},{2,0},{4,2},{6,4},{8,6},{10,8},{12,10},{14,12},{1,15},{3,1}... | collective-permute-start | bytes 3244040 | tf_op jit(solution)/shard_map/ppermute | solution.py:373
  40.2 33.5 %all-to-all-start.1 = ((bf16[8,2,16,4096]{3,2,1,0:T(8,128)(2,1)}), bf16[8,2,16,4096]{3,2,1,0:T(8,128)(2,1)}, u32[]{:S(2)}, u32[]{:S(2)}) async-start(bf16[8,2,16,4096]{3,2,1,0:T(8,128)(2,1)} %build_1.1), calls=%async_computation.1 | async-start | bytes 4194304 | tf_op jit(solution)/shard_map/all_to_all | solution.py:345
  56.9 38.0 %collective-permute-start.5 = (bf16[128,4224]{1,0:T(8,128)(2,1)}, bf16[128,4224]{1,0:T(8,128)(2,1)S(1)}, u32[]{:S(2)}, u32[]{:S(2)}) collective-permute-start(bf16[128,4224]{1,0:T(8,128)(2,1)} %collective-permute-done.1.refs_0_), channel_id=1, source_target_pairs={{0,2},{2,4},{4,6},{6,8},{8,10},{10,12},{12,14},{14,0},{1,3},{3,5},... | collective-permute-start | bytes 3244040 | tf_op jit(solution)/shard_map/ppermute | solution.py:373
  58.8 36.0 %collective-permute-start.7 = (bf16[128,4224]{1,0:T(8,128)(2,1)S(1)}, bf16[128,4224]{1,0:T(8,128)(2,1)S(1)}, u32[]{:S(2)}, u32[]{:S(2)}) collective-permute-start(bf16[128,4224]{1,0:T(8,128)(2,1)S(1)} %collective-permute-done.6.refs_1_), channel_id=1, source_target_pairs={{0,14},{2,0},{4,2},{6,4},{8,6},{10,8},{12,10},{14,12},{1,15},{3,1}... | collective-permute-start | bytes 3244040 | tf_op jit(solution)/shard_map/ppermute | solution.py:373
  73.7 31.5 %all-to-all-start.2 = ((bf16[8,2,16,4096]{3,2,1,0:T(8,128)(2,1)}), bf16[8,2,16,4096]{3,2,1,0:T(8,128)(2,1)}, u32[]{:S(2)}, u32[]{:S(2)}) async-start(bf16[8,2,16,4096]{3,2,1,0:T(8,128)(2,1)} %build_2.1), calls=%async_computation.2 | async-start | bytes 4194304 | tf_op jit(solution)/shard_map/all_to_all | solution.py:345
  78.8 31.5 %collective-permute-start.9 = (bf16[768,512]{1,0:T(8,128)(2,1)}, bf16[768,512]{1,0:T(8,128)(2,1)}, u32[]{:S(2)}, u32[]{:S(2)}) collective-permute-start(bf16[768,512]{1,0:T(8,128)(2,1)} %collective-permute-done.2.refs_1_), channel_id=1, source_target_pairs={{0,64},{64,128},{128,192},{192,256},{256,320},{320,384},{384,448},... | collective-permute-start | bytes 2359304 | tf_op jit(solution)/shard_map/ppermute | solution.py:388
  82.8 27.6 %collective-permute-start.10 = (bf16[768,512]{1,0:T(8,128)(2,1)}, bf16[768,512]{1,0:T(8,128)(2,1)}, u32[]{:S(2)}, u32[]{:S(2)}) collective-permute-start(bf16[768,512]{1,0:T(8,128)(2,1)} %collective-permute-done.3.refs_7_), channel_id=1, source_target_pairs={{0,448},{64,0},{128,64},{192,128},{256,192},{320,256},{384,320},{4... | collective-permute-start | bytes 2359304 | tf_op jit(solution)/shard_map/ppermute | solution.py:389
  94.3 0.6 copy-start.2
  96.0 34.8 %collective-permute-start.8 = (bf16[128,4224]{1,0:T(8,128)(2,1)}, bf16[128,4224]{1,0:T(8,128)(2,1)S(1)}, u32[]{:S(2)}, u32[]{:S(2)}) collective-permute-start(bf16[128,4224]{1,0:T(8,128)(2,1)} %broadcast_select_fusion), channel_id=1, source_target_pairs={{0,2},{2,4},{4,6},{6,8},{8,10},{10,12},{12,14},{14,0},{1,15},{3,1}... | collective-permute-start | bytes 3244040 | tf_op jit(solution)/shard_map/ppermute | solution.py:375
  101.3 21.6 %copy-start.3 = (f32[16,768]{1,0:T(8,128)S(1)}, f32[16,768]{1,0:T(8,128)}, u32[]{:S(2)}) copy-start(f32[16,768]{1,0:T(8,128)} %copy-done.2) | copy-start | bytes 147460
  105.2 31.5 %all-to-all-start.4 = ((bf16[8,2,16,4096]{3,2,1,0:T(8,128)(2,1)}), bf16[8,2,16,4096]{3,2,1,0:T(8,128)(2,1)}, u32[]{:S(2)}, u32[]{:S(2)}) async-start(bf16[8,2,16,4096]{3,2,1,0:T(8,128)(2,1)} %build_3.1), calls=%async_computation.4 | async-start | bytes 4194304 | tf_op jit(solution)/shard_map/all_to_all | solution.py:345
  110.3 34.8 %collective-permute-start.11 = (bf16[768,512]{1,0:T(8,128)(2,1)}, bf16[768,512]{1,0:T(8,128)(2,1)}, u32[]{:S(2)}, u32[]{:S(2)}) collective-permute-start(bf16[768,512]{1,0:T(8,128)(2,1)} %collective-permute-done.10.refs_6_), channel_id=1, source_target_pairs={{0,448},{64,0},{128,64},{192,128},{256,192},{320,256},{384,320},{4... | collective-permute-start | bytes 2359304 | tf_op jit(solution)/shard_map/ppermute | solution.py:389
  121.0 22.1 %collective-permute-start.12 = (bf16[768,512]{1,0:T(8,128)(2,1)}, bf16[768,512]{1,0:T(8,128)(2,1)}, u32[]{:S(2)}, u32[]{:S(2)}) collective-permute-start(bf16[768,512]{1,0:T(8,128)(2,1)} %collective-permute-done.9.refs_2_), channel_id=1, source_target_pairs={{0,64},{64,128},{128,192},{192,256},{256,320},{320,384},{384,448},... | collective-permute-start | bytes 2359304 | tf_op jit(solution)/shard_map/ppermute | solution.py:388
  136.8 19.5 %all-to-all-start.3 = ((bf16[8,1,16,4096]{3,2,1,0:T(8,128)(2,1)}), bf16[8,1,16,4096]{3,2,1,0:T(8,128)(2,1)S(1)}, u32[]{:S(2)}, u32[]{:S(2)}) async-start(bf16[8,1,16,4096]{3,2,1,0:T(8,128)(2,1)} %build_4.1), calls=%async_computation.3 | async-start | bytes 2097152 | tf_op jit(solution)/shard_map/all_to_all | solution.py:345
  143.1 26.7 %collective-permute-start.13 = (bf16[768,512]{1,0:T(8,128)(2,1)}, bf16[768,512]{1,0:T(8,128)(2,1)S(1)}, u32[]{:S(2)}, u32[]{:S(2)}) collective-permute-start(bf16[768,512]{1,0:T(8,128)(2,1)} %collective-permute-done.12.refs_3_), channel_id=1, source_target_pairs={{0,64},{64,128},{128,192},{192,256},{256,320},{320,384},{384,448},... | collective-permute-start | bytes 2359304 | tf_op jit(solution)/shard_map/ppermute | solution.py:393
  156.2 3.1 %copy-start = (bf16[8,1,16,4096]{3,2,1,0:T(8,128)(2,1)}, bf16[8,1,16,4096]{3,2,1,0:T(8,128)(2,1)S(1)}, u32[]{:S(2)}) copy-start(bf16[8,1,16,4096]{3,2,1,0:T(8,128)(2,1)S(1)} %all-to-all-done.3.part.refs_9_) | copy-start | bytes 3145732
  156.2 14.5 %copy-start.1 = (bf16[1,16,768]{2,1,0:T(8,128)(2,1)S(1)}, bf16[1,16,768]{2,1,0:T(8,128)(2,1)}, u32[]{:S(2)}) copy-start(bf16[1,16,768]{2,1,0:T(8,128)(2,1)} %param.15) | copy-start | bytes 73732
  159.4 19.8 %all-to-all-start.5 = ((bf16[8,16,608]{2,1,0:T(8,128)(2,1)}), bf16[8,16,608]{2,1,0:T(8,128)(2,1)S(1)}, u32[]{:S(2)}, u32[]{:S(2)}) async-start(bf16[8,16,608]{2,1,0:T(8,128)(2,1)} %get-tuple-element.72), calls=%async_computation.5 | async-start | bytes 327680 | tf_op jit(solution)/shard_map/all_to_all | solution.py:405
  169.8 1.0 copy-start.7
  179.1 0.7 copy-start.5
  181.4 11.7 %all-to-all-start.6 = ((bf16[8,16,608]{2,1,0:T(8,128)(2,1)}), bf16[8,16,608]{2,1,0:T(8,128)(2,1)S(1)}, u32[]{:S(2)}, u32[]{:S(2)}) async-start(bf16[8,16,608]{2,1,0:T(8,128)(2,1)} %spread.1), calls=%async_computation.6 | async-start | bytes 327680 | tf_op jit(solution)/shard_map/all_to_all | solution.py:408
  193.2 0.7 copy-start.6
  195.5 15.6 %all-to-all-start.7 = ((bf16[8,16,608]{2,1,0:T(8,128)(2,1)}), bf16[8,16,608]{2,1,0:T(8,128)(2,1)S(1)}, u32[]{:S(2)}, u32[]{:S(2)}) async-start(bf16[8,16,608]{2,1,0:T(8,128)(2,1)} %turn.1), calls=%async_computation.7 | async-start | bytes 327680 | tf_op jit(solution)/shard_map/all_to_all | solution.py:411
  211.0 0.7 copy-start.4
